TPU v7x, 128 devices: a whole 4x4x4 slice. The times are simulated.
128 devices in a mesh: band: 64 (over z, y, x), feat: 2 (over core).
Axes of the slice: x: 4, y: 4, z: 4, core: 2. Of those that a mesh axis runs over, the one named last changes fastest.
Arguments:
- grid_latent: bfloat16 [65536, 512], P('band'), may hold values from -6 to 6
- mesh_latent: bfloat16 [16384, 512], P('band', 'feat'), may hold values from -6 to 6
- grid_in_w: bfloat16 [512, 512], P(None, 'feat'), may hold values from -0.25 to 0.25
- grid_bias: bfloat16 [512], P('feat'), may hold values from -3 to 3
- g2m_src: int32 [64, 64, 64], P('band'), may hold values from 0 to 1023
- g2m_dst: int32 [64, 64, 64], P('band'), may hold values from 0 to 255
- g2m_weight: bfloat16 [64, 64, 64], P('band'), may hold values from 0 to 2, as said below
- mesh_src: int32 [64, 12288], P('band'), may hold values from 0 to 383
- mesh_dst: int32 [64, 12288], P('band'), may hold values from 0 to 255
- halo_index: int32 [64, 2, 64], P('band'), may hold values from 0 to 255
- edge_send_w: bfloat16 [2, 512, 512], P(None, None, 'feat'), may hold values from -0.25 to 0.25
- edge_recv_w: bfloat16 [2, 512, 512], P(None, None, 'feat'), may hold values from -0.25 to 0.25
- edge_bias: bfloat16 [2, 512], P(None, 'feat'), may hold values from -3 to 3
- node_in_w: bfloat16 [3, 1024, 512], P(None, None, 'feat'), may hold values from -0.125 to 0.125
- node_bias: bfloat16 [3, 512], P(None, 'feat'), may hold values from -3 to 3
- node_out_w: bfloat16 [3, 512, 512], P(None, 'feat'), may hold values from -0.25 to 0.25
Outputs:
- mesh_out: bfloat16 [16384, 512], P('band', 'feat')
Inputs may be any that keep to these rules, and one draw needn't show every extreme that they name: `g2m_weight`: each pair of band s and partition d has a live count of 48 to 64: slots c below it have positive weights, the others weight 0. A partition's slots from its own band are all live.
All inputs are finite; a program needn't handle non-finite values.
Results may differ from a plain program's by a relative error of at most 0.029.
Values may be sent and summed in bfloat16 or wider, within the bound.
No kernel may reach another device: no remote copies, remote signals or barrier semaphores. Data moves between devices by JAX's collectives and lax.ppermute only.
A program may use at most 64 MiB of HBM per device.

v0:
```python
import jax
import jax.numpy as jnp
from jax import lax
from jax.sharding import PartitionSpec as P


def with_halo(value, sides, width):
    for axis, dim in sides:
        devices, length = (lax.axis_size(axis), value.shape[dim])
        up = [(i, (i + 1) % devices) for i in range(devices - 1)]
        down = [(j, i) for i, j in up]
        last = lax.slice_in_dim(value, length - width, length, axis=dim)
        leading = lax.slice_in_dim(value, 0, width, axis=dim)
        before = lax.ppermute(last, axis, up)
        after = lax.ppermute(leading, axis, down)
        value = jnp.concatenate([before, value, after], axis=dim)
    return value


def select_rows(lookup_table, indices):
    row_ids = lax.broadcasted_iota(jnp.int32, (indices.shape[0], lookup_table.shape[0]), 1)
    selector = (indices[:, None] == row_ids).astype(lookup_table.dtype)
    return jnp.dot(selector, lookup_table, preferred_element_type=jnp.float32).astype(
        lookup_table.dtype
    )


def widen_state(mesh_state):
    return lax.all_gather(mesh_state, "feat", axis=1, tiled=True)


def mesh_messages(
    state_full, edge_layer, edge_send_w, edge_recv_w, edge_bias, mesh_src, mesh_dst, halo_index
):
    sender_rows = (
        jnp.dot(state_full, edge_send_w[edge_layer], preferred_element_type=jnp.float32)
        + edge_bias[edge_layer].astype(jnp.float32)
    ).astype(jnp.bfloat16)
    receiver_rows = jnp.dot(
        state_full, edge_recv_w[edge_layer], preferred_element_type=jnp.float32
    ).astype(jnp.bfloat16)
    halo_width = halo_index.shape[2]
    outgoing_ids = jnp.concatenate([halo_index[0, 1], halo_index[0, 0]], 0)
    buffer = select_rows(sender_rows, outgoing_ids)
    padded = with_halo(buffer, (("band", 0),), halo_width)
    source_table = jnp.concatenate([sender_rows, padded[:halo_width], padded[3 * halo_width :]], 0)
    messages = jax.nn.silu(
        select_rows(source_table, mesh_src[0]).astype(jnp.float32)
        + select_rows(receiver_rows, mesh_dst[0]).astype(jnp.float32)
    ).astype(jnp.bfloat16)
    node_ids = lax.broadcasted_iota(jnp.int32, (sender_rows.shape[0], messages.shape[0]), 0)
    matrix = (node_ids == mesh_dst[0][None, :]).astype(jnp.bfloat16)
    return jnp.dot(matrix, messages, preferred_element_type=jnp.float32).astype(jnp.bfloat16)


def body(
    grid_latent,
    mesh_latent,
    grid_in_w,
    grid_bias,
    g2m_src,
    g2m_dst,
    g2m_weight,
    mesh_src,
    mesh_dst,
    halo_index,
    edge_send_w,
    edge_recv_w,
    edge_bias,
    node_in_w,
    node_bias,
    node_out_w,
):
    feature_width = grid_in_w.shape[1]
    embedding = jax.nn.silu(
        jnp.dot(grid_latent, grid_in_w, preferred_element_type=jnp.float32)
        + grid_bias.astype(jnp.float32)
    ).astype(jnp.bfloat16)
    band_count = g2m_src.shape[1]
    slot_count = g2m_src.shape[2]
    outgoing = select_rows(embedding, g2m_src[0].reshape(-1)).reshape(
        band_count, slot_count, feature_width
    )
    incoming = lax.all_to_all(outgoing, "band", split_axis=0, concat_axis=0, tiled=True)
    node_count = mesh_latent.shape[0]
    slot_rows = incoming.reshape(-1, feature_width)
    slot_nodes = g2m_dst[0].reshape(-1)
    slot_weights = g2m_weight[0].reshape(-1)
    node_ids = lax.broadcasted_iota(jnp.int32, (node_count, slot_nodes.shape[0]), 0)
    matrix = jnp.where(
        node_ids == slot_nodes[None, :], slot_weights[None, :], jnp.zeros((), jnp.bfloat16)
    )
    aggregate = jnp.dot(matrix, slot_rows, preferred_element_type=jnp.float32).astype(jnp.bfloat16)
    mesh_state = mesh_latent
    state_full = widen_state(mesh_state)
    layer_total = node_in_w.shape[0]
    for layer_index in range(layer_total):
        if layer_index > 0:
            aggregate = mesh_messages(
                state_full,
                layer_index - 1,
                edge_send_w,
                edge_recv_w,
                edge_bias,
                mesh_src,
                mesh_dst,
                halo_index,
            )
        aggregate_full = lax.all_gather(aggregate, "feat", axis=1, tiled=True)
        inputs = jnp.concatenate([state_full, aggregate_full], 1)
        hidden = jax.nn.silu(
            jnp.dot(inputs, node_in_w[layer_index], preferred_element_type=jnp.float32)
            + node_bias[layer_index].astype(jnp.float32)
        ).astype(jnp.bfloat16)
        update_terms = jnp.dot(hidden, node_out_w[layer_index], preferred_element_type=jnp.float32)
        update_total = lax.psum_scatter(
            update_terms.astype(jnp.bfloat16), "feat", scatter_dimension=1, tiled=True
        ).astype(jnp.float32)
        mesh_state = (mesh_state.astype(jnp.float32) + update_total).astype(jnp.bfloat16)
        if layer_index + 1 < layer_total:
            state_full = widen_state(mesh_state)
    return mesh_state


def solution(mesh):
    in_specs = (
        P("band", None),
        P("band", "feat"),
        P(None, "feat"),
        P("feat"),
        P("band", None, None),
        P("band", None, None),
        P("band", None, None),
        P("band", None),
        P("band", None),
        P("band", None, None),
        P(None, None, "feat"),
        P(None, None, "feat"),
        P(None, "feat"),
        P(None, None, "feat"),
        P(None, "feat"),
        P(None, "feat", None),
    )
    out_specs = P("band", "feat")
    return jax.shard_map(body, mesh=mesh, in_specs=in_specs, out_specs=out_specs, check_vma=False)
```

profile of v0, /device:TPU:1, one launch (start us, length us, event | category | flops | bytes accessed | tf_op | source)
XLA Modules:
  0.0 168.2 jit_solution(7317991304794518363)
XLA Ops:
  6.5 0.0 copy-start
  6.5 0.7 convert_element_type.131
  7.3 0.8 eq.35
  8.1 0.0 copy-done
  8.1 0.0 copy-start.3
  8.1 0.0 copy-start.6
  8.1 6.2 %fusion.20 = bf16[4096,256]{1,0:T(8,128)(2,1)} fusion(s32[4096]{0:T(1024)S(1)} %eq.35, bf16[1024,512]{1,0:T(8,128)(2,1)S(1)} %copy-done, bf16[512,256]{1,0:T(8,128)(2,1)} %param.18, f32[256]{0:T(256)S(1)} %convert_element_type.131), kind=kOutput, calls=%fused_computation.28 | convolution fusion | flops 2422734848 | bytes 3425280 | tf_op jit(solution)/shard_map/dot_general | solution.py:23
  14.4 12.0 %all-to-all-start = ((bf16[64,64,256]{2,1,0:T(8,128)(2,1)}), bf16[64,64,256]{2,1,0:T(8,128)(2,1)S(1)}, u32[]{:S(2)}, u32[]{:S(2)}) async-start(bf16[64,64,256]{2,1,0:T(8,128)(2,1)} %bitcast.83), calls=%async_computation | async-start | bytes 4194304 | tf_op jit(solution)/shard_map/all_to_all | solution.py:84
  26.3 0.0 copy-start.8
  26.3 0.0 copy-start.7
  26.4 0.0 reduce-scatter.4.cloned.1.call-start
  26.4 0.0 copy-done.5
  26.4 0.1 broadcast_in_dim.14
  26.5 0.0 copy-done.4
  26.5 0.1 eq.32
  26.6 0.0 copy-done.3
  26.6 2.7 %all_gather.18 = bf16[256,512]{1,0:T(8,128)(2,1)} all-gather(bf16[256,256]{1,0:T(8,128)(2,1)S(1)} %copy-done.3), channel_id=1, replica_groups=mesh['band'=64,'feat'=2] {'feat'}, dimensions={1}, use_global_device_ids=true | all-gather | bytes 393216 | tf_op jit(solution)/shard_map/all_gather | solution.py:29
  29.3 0.0 copy-done.6
  29.3 25.5 %all-to-all-done = bf16[64,64,256]{2,1,0:T(8,128)(2,1)S(1)} async-done(((bf16[64,64,256]{2,1,0:T(8,128)(2,1)}), bf16[64,64,256]{2,1,0:T(8,128)(2,1)S(1)}, u32[]{:S(2)}, u32[]{:S(2)}) %all-to-all-start) | async-done | bytes 2097184 | tf_op jit(solution)/shard_map/all_to_all | solution.py:84
  54.8 0.7 fusion.27
  55.5 4.1 %all_gather.19 = bf16[256,512]{1,0:T(8,128)(2,1)S(1)} all-gather(bf16[256,256]{1,0:T(8,128)(2,1)S(1)} %fusion.27), channel_id=1, replica_groups=mesh['band'=64,'feat'=2] {'feat'}, dimensions={1}, use_global_device_ids=true | all-gather | bytes 393216 | tf_op jit(solution)/shard_map/all_gather | solution.py:109
  59.6 2.4 %convolution_convert_fusion.4 = bf16[256,512]{1,0:T(8,128)(2,1)} fusion(bf16[3,256,512]{2,1,0:T(8,128)(2,1)} %param.31, bf16[3,1024,256]{2,1,0:T(8,128)(2,1)} %param.29, bf16[256,512]{1,0:T(8,128)(2,1)S(1)} %all_gather.19, bf16[256,512]{1,0:T(8,128)(2,1)} %all_gather.18, f32[256]{0:T(256)S(1)} %bitcast.91), kind=kOutput, calls=%fused_computation.36 | convolution fusion | flops 202899456 | bytes 1573888 | tf_op jit(solution)/shard_map/dot_general | solution.py:115
  62.0 0.0 reduce-scatter.4.cloned.1.call-update
  62.1 0.0 reduce-scatter.6.cloned.1.call-start
  62.1 0.0 copy-done.8
  62.1 0.1 pad_add_fusion
  62.2 0.0 copy-done.7
  62.2 7.3 %reduce-scatter.4.cloned.1.call-done = bf16[256,256]{1,0:T(8,128)(2,1)} async-done(((bf16[256,512]{1,0:T(8,128)(2,1)}), bf16[256,256]{1,0:T(8,128)(2,1)}) %reduce-scatter.4.cloned.1.call-update) | async-done | bytes 131088 | tf_op jit(solution)/shard_map/reduce_scatter | solution.py:116
  69.5 0.9 add_convert_fusion.2
  70.5 2.0 %all_gather.20 = bf16[256,512]{1,0:T(8,128)(2,1)S(1)} all-gather(bf16[256,256]{1,0:T(8,128)(2,1)S(1)} %add_convert_fusion.2), channel_id=1, replica_groups=mesh['band'=64,'feat'=2] {'feat'}, dimensions={1}, use_global_device_ids=true | all-gather | bytes 393216 | tf_op jit(solution)/shard_map/all_gather | solution.py:29
  72.5 1.2 fusion.25
  73.6 0.2 convolution_convert_fusion.8
  73.9 3.2 %collective-permute-start = (bf16[64,256]{1,0:T(8,128)(2,1)S(1)}, bf16[64,256]{1,0:T(8,128)(2,1)S(1)}, u32[]{:S(2)}, u32[]{:S(2)}) collective-permute-start(bf16[64,256]{1,0:T(8,128)(2,1)S(1)} %get-tuple-element.7), channel_id=1, source_target_pairs={{0,2},{2,4},{4,6},{6,8},{8,10},{10,12},{12,14},{14,16},{16,18},{18... | collective-permute-start | bytes 98312 | tf_op jit(solution)/shard_map/ppermute | solution.py:14
  77.1 1.5 collective-permute-start.1
  78.5 0.0 copy-done.1
  78.5 0.0 copy-start.10
  78.6 6.8 %fusion.8 = f32[12288,256]{1,0:T(8,128)} fusion(s32[12288]{0:T(1024)S(1)} %bitcast.84, bf16[256,512]{1,0:T(8,128)(2,1)S(1)} %all_gather.20, bf16[2,512,256]{2,1,0:T(8,128)(2,1)} %param.27), kind=kOutput, calls=%fused_computation.12 | convolution fusion | flops 1687224320 | bytes 13156352 | tf_op jit(solution)/shard_map/dot_general | solution.py:23
  85.3 0.0 collective-permute-done
  85.3 0.0 collective-permute-done.1
  85.3 0.0 copy-done.10
  85.3 0.0 copy-start.9
  85.4 0.0 copy-start.2
  85.4 12.1 %fusion.30 = bf16[256,256]{1,0:T(8,128)(2,1)S(1)} fusion(f32[12288,256]{1,0:T(8,128)} %fusion.8, s32[12288]{0:T(1024)S(1)} %bitcast.93, s32[12288]{0:T(1024)S(1)} %bitcast.85, bf16[64,256]{1,0:T(8,128)(2,1)S(1)} %collective-permute-done.1, bf16[64,256]{1,0:T(8,128)(2,1)S(1)} %collective-permute-done, bf16[256,256]{1,0:T(8,128)(2,1)S(1)} %fusion.25), kind=kOutput, calls=%fused_computation.47 | convolution fusion | flops 4060217344 | bytes 13008896 | tf_op jit(solution)/shard_map/dot_general | solution.py:53
  97.5 2.1 %all_gather.21 = bf16[256,512]{1,0:T(8,128)(2,1)S(1)} all-gather(bf16[256,256]{1,0:T(8,128)(2,1)S(1)} %fusion.30), channel_id=1, replica_groups=mesh['band'=64,'feat'=2] {'feat'}, dimensions={1}, use_global_device_ids=true | all-gather | bytes 393216 | tf_op jit(solution)/shard_map/all_gather | solution.py:109
  99.6 2.3 %convolution_convert_fusion.3 = bf16[256,512]{1,0:T(8,128)(2,1)} fusion(bf16[3,256,512]{2,1,0:T(8,128)(2,1)S(1)} %copy-done.9, bf16[3,1024,256]{2,1,0:T(8,128)(2,1)} %param.29, bf16[256,512]{1,0:T(8,128)(2,1)S(1)} %all_gather.21, bf16[256,512]{1,0:T(8,128)(2,1)S(1)} %all_gather.20, f32[256]{0:T(256)S(1)} %bitcast.89), kind=kOutput, calls=%fused_computation.35 | convolution fusion | flops 202899456 | bytes 1573888 | tf_op jit(solution)/shard_map/dot_general | solution.py:115
  101.9 0.0 reduce-scatter.6.cloned.1.call-update
  101.9 0.0 reduce-scatter.8.cloned.1.call-start
  102.0 13.0 %reduce-scatter.6.cloned.1.call-done = bf16[256,256]{1,0:T(8,128)(2,1)} async-done(((bf16[256,512]{1,0:T(8,128)(2,1)}), bf16[256,256]{1,0:T(8,128)(2,1)}) %reduce-scatter.6.cloned.1.call-update) | async-done | bytes 131088 | tf_op jit(solution)/shard_map/reduce_scatter | solution.py:116
  115.0 0.9 add_convert_fusion.1
  116.0 2.0 %all_gather.22 = bf16[256,512]{1,0:T(8,128)(2,1)S(1)} all-gather(bf16[256,256]{1,0:T(8,128)(2,1)S(1)} %add_convert_fusion.1), channel_id=1, replica_groups=mesh['band'=64,'feat'=2] {'feat'}, dimensions={1}, use_global_device_ids=true | all-gather | bytes 393216 | tf_op jit(solution)/shard_map/all_gather | solution.py:29
  117.9 1.2 fusion.26
  119.1 0.2 convolution_convert_fusion.7
  119.4 3.2 %collective-permute-start.2 = (bf16[64,256]{1,0:T(8,128)(2,1)S(1)}, bf16[64,256]{1,0:T(8,128)(2,1)S(1)}, u32[]{:S(2)}, u32[]{:S(2)}) collective-permute-start(bf16[64,256]{1,0:T(8,128)(2,1)S(1)} %get-tuple-element.5), channel_id=1, source_target_pairs={{0,2},{2,4},{4,6},{6,8},{8,10},{10,12},{12,14},{14,16},{16,18},{18... | collective-permute-start | bytes 98312 | tf_op jit(solution)/shard_map/ppermute | solution.py:14
  122.6 1.5 collective-permute-start.3
  124.1 0.0 copy-done.2
  124.1 5.8 %fusion.7 = f32[12288,256]{1,0:T(8,128)} fusion(s32[12288]{0:T(1024)S(1)} %bitcast.86, bf16[256,512]{1,0:T(8,128)(2,1)S(1)} %all_gather.22, bf16[2,512,256]{2,1,0:T(8,128)(2,1)S(1)} %copy-done.2), kind=kOutput, calls=%fused_computation.10 | convolution fusion | flops 1687224320 | bytes 13156352 | tf_op jit(solution)/shard_map/dot_general | solution.py:23
  129.9 0.0 collective-permute-done.2
  129.9 0.0 collective-permute-done.3
  129.9 12.0 %fusion.31 = bf16[256,256]{1,0:T(8,128)(2,1)S(1)} fusion(f32[12288,256]{1,0:T(8,128)} %fusion.7, s32[12288]{0:T(1024)S(1)} %bitcast.94, s32[12288]{0:T(1024)S(1)} %bitcast.87, bf16[64,256]{1,0:T(8,128)(2,1)S(1)} %collective-permute-done.3, bf16[64,256]{1,0:T(8,128)(2,1)S(1)} %collective-permute-done.2, bf16[256,256]{1,0:T(8,128)(2,1)S(1)} %fusion.26), kind=kOutput, calls=%fused_computation.48 | convolution fusion | flops 4060217344 | bytes 13008896 | tf_op jit(solution)/shard_map/dot_general | solution.py:53
  141.9 2.1 %all_gather.23 = bf16[256,512]{1,0:T(8,128)(2,1)S(1)} all-gather(bf16[256,256]{1,0:T(8,128)(2,1)S(1)} %fusion.31), channel_id=1, replica_groups=mesh['band'=64,'feat'=2] {'feat'}, dimensions={1}, use_global_device_ids=true | all-gather | bytes 393216 | tf_op jit(solution)/shard_map/all_gather | solution.py:109
  144.1 2.3 %convolution_convert_fusion.2 = bf16[256,512]{1,0:T(8,128)(2,1)} fusion(bf16[3,256,512]{2,1,0:T(8,128)(2,1)S(1)} %copy-done.9, bf16[3,1024,256]{2,1,0:T(8,128)(2,1)} %param.29, bf16[256,512]{1,0:T(8,128)(2,1)S(1)} %all_gather.23, bf16[256,512]{1,0:T(8,128)(2,1)S(1)} %all_gather.22, f32[256]{0:T(256)S(1)} %bitcast.88), kind=kOutput, calls=%fused_computation.34 | convolution fusion | flops 202899456 | bytes 1573888 | tf_op jit(solution)/shard_map/dot_general | solution.py:115
  146.4 0.0 reduce-scatter.8.cloned.1.call-update
  146.4 13.7 %reduce-scatter.8.cloned.1.call-done = bf16[256,256]{1,0:T(8,128)(2,1)} async-done(((bf16[256,512]{1,0:T(8,128)(2,1)}), bf16[256,256]{1,0:T(8,128)(2,1)}) %reduce-scatter.8.cloned.1.call-update) | async-done | bytes 131088 | tf_op jit(solution)/shard_map/reduce_scatter | solution.py:116
  160.1 1.6 add_convert_fusion
  (9 shorter events, 0.0 us)
Async XLA Ops:
  6.5 1.6 copy-start
  8.1 18.3 %copy-start.5 = (bf16[1,64,64]{2,1,0:T(8,128)(2,1)S(1)}, bf16[1,64,64]{2,1,0:T(8,128)(2,1)}, u32[]{:S(2)}) copy-start(bf16[1,64,64]{2,1,0:T(8,128)(2,1)} %param.22) | copy-start | bytes 24580
  8.1 18.4 %copy-start.4 = (s32[1,64,64]{2,1,0:T(8,128)S(1)}, s32[1,64,64]{2,1,0:T(8,128)}, u32[]{:S(2)}) copy-start(s32[1,64,64]{2,1,0:T(8,128)} %param.21) | copy-start | bytes 49156
  8.1 18.5 %copy-start.3 = (bf16[256,256]{1,0:T(8,128)(2,1)S(1)}, bf16[256,256]{1,0:T(8,128)(2,1)}, u32[]{:S(2)}) copy-start(bf16[256,256]{1,0:T(8,128)(2,1)} %param.17) | copy-start | bytes 393220
  8.1 21.2 %copy-start.6 = (bf16[3,256]{1,0:T(4,128)(2,1)S(1)}, bf16[3,256]{1,0:T(4,128)(2,1)}, u32[]{:S(2)}) copy-start(bf16[3,256]{1,0:T(4,128)(2,1)} %param.30) | copy-start | bytes 4612
  14.4 40.4 %all-to-all-start = ((bf16[64,64,256]{2,1,0:T(8,128)(2,1)}), bf16[64,64,256]{2,1,0:T(8,128)(2,1)S(1)}, u32[]{:S(2)}, u32[]{:S(2)}) async-start(bf16[64,64,256]{2,1,0:T(8,128)(2,1)} %bitcast.83), calls=%async_computation | async-start | bytes 4194304 | tf_op jit(solution)/shard_map/all_to_all | solution.py:84
  26.3 35.8 %copy-start.8 = (s32[1,2,64]{2,1,0:T(2,128)S(1)}, s32[1,2,64]{2,1,0:T(2,128)}, u32[]{:S(2)}) copy-start(s32[1,2,64]{2,1,0:T(2,128)} %param.25) | copy-start | bytes 1540
  26.3 35.9 %copy-start.7 = (bf16[2,256]{1,0:T(2,128)(2,1)S(1)}, bf16[2,256]{1,0:T(2,128)(2,1)}, u32[]{:S(2)}) copy-start(bf16[2,256]{1,0:T(2,128)(2,1)} %param.28) | copy-start | bytes 3076
  26.4 43.2 %reduce-scatter.4.cloned.1.call-start = ((), (), s32[]{:S(2)}) async-start(), calls=%async_computation.4 | async-start | bytes 393216 | tf_op jit(solution)/shard_map/reduce_scatter | solution.py:116
  29.3 49.2 %copy-start.1 = (s32[1,12288]{1,0:T(1,128)S(1)}, s32[1,12288]{1,0:T(1,128)}, u32[]{:S(2)}) copy-start(s32[1,12288]{1,0:T(1,128)} %param.24) | copy-start | bytes 147460
  62.1 53.0 %reduce-scatter.6.cloned.1.call-start = ((), (), s32[]{:S(2)}) async-start(), calls=%async_computation.5 | async-start | bytes 393216 | tf_op jit(solution)/shard_map/reduce_scatter | solution.py:116
  73.9 11.5 %collective-permute-start = (bf16[64,256]{1,0:T(8,128)(2,1)S(1)}, bf16[64,256]{1,0:T(8,128)(2,1)S(1)}, u32[]{:S(2)}, u32[]{:S(2)}) collective-permute-start(bf16[64,256]{1,0:T(8,128)(2,1)S(1)} %get-tuple-element.7), channel_id=1, source_target_pairs={{0,2},{2,4},{4,6},{6,8},{8,10},{10,12},{12,14},{14,16},{16,18},{18... | collective-permute-start | bytes 98312 | tf_op jit(solution)/shard_map/ppermute | solution.py:14
  77.1 8.3 %collective-permute-start.1 = (bf16[64,256]{1,0:T(8,128)(2,1)S(1)}, bf16[64,256]{1,0:T(8,128)(2,1)S(1)}, u32[]{:S(2)}, u32[]{:S(2)}) collective-permute-start(bf16[64,256]{1,0:T(8,128)(2,1)S(1)} %get-tuple-element.8), channel_id=1, source_target_pairs={{2,0},{4,2},{6,4},{8,6},{10,8},{12,10},{14,12},{16,14},{18,16},{20... | collective-permute-start | bytes 98312 | tf_op jit(solution)/shard_map/ppermute | solution.py:15
  78.5 6.8 %copy-start.10 = (s32[1,12288]{1,0:T(1,128)S(1)}, s32[1,12288]{1,0:T(1,128)}, u32[]{:S(2)}) copy-start(s32[1,12288]{1,0:T(1,128)} %param.23) | copy-start | bytes 147460
  85.3 14.3 %copy-start.9 = (bf16[3,256,512]{2,1,0:T(8,128)(2,1)S(1)}, bf16[3,256,512]{2,1,0:T(8,128)(2,1)}, u32[]{:S(2)}) copy-start(bf16[3,256,512]{2,1,0:T(8,128)(2,1)} %param.31) | copy-start | bytes 2359300
  85.4 38.7 %copy-start.2 = (bf16[2,512,256]{2,1,0:T(8,128)(2,1)S(1)}, bf16[2,512,256]{2,1,0:T(8,128)(2,1)}, u32[]{:S(2)}) copy-start(bf16[2,512,256]{2,1,0:T(8,128)(2,1)} %param.27) | copy-start | bytes 1572868
  101.9 58.2 %reduce-scatter.8.cloned.1.call-start = ((), (), s32[]{:S(2)}) async-start(), calls=%async_computation.6 | async-start | bytes 393216 | tf_op jit(solution)/shard_map/reduce_scatter | solution.py:116
  119.4 10.6 %collective-permute-start.2 = (bf16[64,256]{1,0:T(8,128)(2,1)S(1)}, bf16[64,256]{1,0:T(8,128)(2,1)S(1)}, u32[]{:S(2)}, u32[]{:S(2)}) collective-permute-start(bf16[64,256]{1,0:T(8,128)(2,1)S(1)} %get-tuple-element.5), channel_id=1, source_target_pairs={{0,2},{2,4},{4,6},{6,8},{8,10},{10,12},{12,14},{14,16},{16,18},{18... | collective-permute-start | bytes 98312 | tf_op jit(solution)/shard_map/ppermute | solution.py:14
  122.6 7.4 %collective-permute-start.3 = (bf16[64,256]{1,0:T(8,128)(2,1)S(1)}, bf16[64,256]{1,0:T(8,128)(2,1)S(1)}, u32[]{:S(2)}, u32[]{:S(2)}) collective-permute-start(bf16[64,256]{1,0:T(8,128)(2,1)S(1)} %get-tuple-element.6), channel_id=1, source_target_pairs={{2,0},{4,2},{6,4},{8,6},{10,8},{12,10},{14,12},{16,14},{18,16},{20... | collective-permute-start | bytes 98312 | tf_op jit(solution)/shard_map/ppermute | solution.py:15
Sparse Core Ops, SparseCore 0:
  62.2 7.3 reduce-scatter.3
  102.0 12.9 reduce-scatter.5
  146.5 13.5 reduce-scatter.7
where the time goes:
time: 169 us; the launch traced here: 168 us
  waiting for transfers between devices  59.6 us (35%)
  matrix products  53.5 us (32%)
  starting transfers between devices  21.5 us (13%)
  blocking collectives  15 us (9%)
  between operations  13.3 us (8%)
  other arithmetic  4.29 us (3%)
    reduce_scatter x3, waiting for transfers between devices, body(): lax.psum_scatter(update_terms.astype(jnp.bfloat16), 'feat', scatter_dimen...  34.1 us
    all_to_all x1, waiting for transfers between devices, body(): lax.all_to_all(outgoing, 'band', split_axis=0, concat_axis=0, tiled=True)  25.5 us
    dot_general x2, matrix products, mesh_messages(): jnp.dot(matrix, messages, preferred_element_type=jnp.float32)  24.1 us
    dot_general x5, matrix products, select_rows(): jnp.dot(selector, lookup_table, preferred_element_type=jnp.float32)  19.2 us
    all_to_all x1, starting transfers between devices, body(): lax.all_to_all(outgoing, 'band', split_axis=0, concat_axis=0, tiled=True)  12 us
    all_gather x3, blocking collectives, body(): aggregate_full = lax.all_gather(aggregate, 'feat', axis=1, tiled=True)  8.3 us
    dot_general x3, matrix products, body(): jnp.dot(hidden, node_out_w[layer_index], preferred_element_type=jnp.float32)  7.05 us
    all_gather x3, blocking collectives, widen_state(): return lax.all_gather(mesh_state, 'feat', axis=1, tiled=True)  6.7 us
  transfers between devices with their start and end apart: 8, of which 4 were waited for; matrix products, arithmetic and copies ran while one was open for 8% of the time, Pallas kernels for 0%

commit v1 on v0

v1 whole, which is shorter than its diff:
```python
import jax
import jax.numpy as jnp
from jax import lax
from jax.sharding import PartitionSpec as P


def select_rows(lookup_table, indices):
    row_ids = lax.broadcasted_iota(jnp.int32, (indices.shape[0], lookup_table.shape[0]), 1)
    selector = (indices[:, None] == row_ids).astype(lookup_table.dtype)
    return jnp.dot(selector, lookup_table, preferred_element_type=jnp.float32).astype(
        lookup_table.dtype
    )


def swap_cores(value):
    return lax.ppermute(value, "feat", [(0, 1), (1, 0)])


def dot32(a, b):
    return jnp.dot(a, b, preferred_element_type=jnp.float32)


def mesh_messages(state_full, send_w, recv_w, bias, source_ids, node_of_edge, halo_ids):
    sender_rows = (dot32(state_full, send_w) + bias.astype(jnp.float32)).astype(jnp.bfloat16)
    receiver_rows = dot32(state_full, recv_w).astype(jnp.bfloat16)
    partitions = lax.axis_size("band")
    up = [(i, (i + 1) % partitions) for i in range(partitions)]
    down = [(j, i) for i, j in up]
    outgoing = select_rows(sender_rows, halo_ids.reshape(-1))
    width = halo_ids.shape[1]
    from_lower = lax.ppermute(outgoing[:width], "band", up)
    from_upper = lax.ppermute(outgoing[width:], "band", down)
    source_table = jnp.concatenate([sender_rows, from_lower, from_upper], 0)
    messages = jax.nn.silu(
        select_rows(source_table, source_ids).astype(jnp.float32)
        + select_rows(receiver_rows, node_of_edge).astype(jnp.float32)
    ).astype(jnp.bfloat16)
    node_ids = lax.broadcasted_iota(jnp.int32, (sender_rows.shape[0], messages.shape[0]), 0)
    matrix = (node_ids == node_of_edge[None, :]).astype(jnp.bfloat16)
    return dot32(matrix, messages).astype(jnp.bfloat16)


def body(
    grid_latent,
    mesh_latent,
    grid_in_w,
    grid_bias,
    g2m_src,
    g2m_dst,
    g2m_weight,
    mesh_src,
    mesh_dst,
    halo_index,
    edge_send_w,
    edge_recv_w,
    edge_bias,
    node_in_w,
    node_bias,
    node_out_w,
):
    feature_width = grid_in_w.shape[1]
    core = lax.axis_index("feat")
    part = lax.axis_index("band")
    embedding = jax.nn.silu(
        dot32(grid_latent, grid_in_w) + grid_bias.astype(jnp.float32)
    ).astype(jnp.bfloat16)
    band_count = g2m_src.shape[1]
    slot_count = g2m_src.shape[2]
    outgoing = select_rows(embedding, g2m_src[0].reshape(-1)).reshape(
        band_count, slot_count, feature_width
    )
    incoming = lax.all_to_all(outgoing, "band", split_axis=0, concat_axis=0, tiled=True)

    state_full = lax.all_gather(mesh_latent, "feat", axis=1, tiled=True)
    in_w = jnp.concatenate([node_in_w, swap_cores(node_in_w)], 2)
    out_w = jnp.concatenate([node_out_w, swap_cores(node_out_w)], 1)
    bias = jnp.concatenate([node_bias, swap_cores(node_bias)], 1).astype(jnp.float32)
    wide = state_full.shape[1]
    mine_first = jnp.where(core == 0, 0, feature_width)
    in_w_state = in_w[:, :wide]
    in_w_mine = lax.dynamic_slice_in_dim(in_w, wide + mine_first, feature_width, 1)
    in_w_other = lax.dynamic_slice_in_dim(in_w, wide + feature_width - mine_first, feature_width, 1)
    last_out_w = lax.dynamic_slice_in_dim(out_w[-1], mine_first, feature_width, 1)

    source_ids = mesh_src[0]
    nodes = mesh_latent.shape[0]
    width = halo_index.shape[2]
    in_lower = (source_ids >= nodes) & (source_ids < nodes + width)
    in_upper = source_ids >= nodes + width
    outside = (in_lower & (part == 0)) | (in_upper & (part == lax.axis_size("band") - 1))
    source_ids = jnp.where(outside, -1, source_ids)

    node_count = mesh_latent.shape[0]
    slot_rows = incoming.reshape(-1, feature_width)
    slot_nodes = g2m_dst[0].reshape(-1)
    slot_weights = g2m_weight[0].reshape(-1)
    node_ids = lax.broadcasted_iota(jnp.int32, (node_count, slot_nodes.shape[0]), 0)
    matrix = jnp.where(
        node_ids == slot_nodes[None, :], slot_weights[None, :], jnp.zeros((), jnp.bfloat16)
    )
    aggregate = dot32(matrix, slot_rows).astype(jnp.bfloat16)
    layer_total = node_in_w.shape[0]
    for layer_index in range(layer_total):
        if layer_index > 0:
            k = layer_index - 1
            aggregate = mesh_messages(
                state_full,
                edge_send_w[k],
                edge_recv_w[k],
                edge_bias[k],
                source_ids,
                mesh_dst[0],
                halo_index[0],
            )
        other = swap_cores(aggregate)
        hidden = jax.nn.silu(
            dot32(state_full, in_w_state[layer_index])
            + dot32(aggregate, in_w_mine[layer_index])
            + dot32(other, in_w_other[layer_index])
            + bias[layer_index]
        ).astype(jnp.bfloat16)
        if layer_index + 1 < layer_total:
            update = dot32(hidden, out_w[layer_index])
            state_full = (state_full.astype(jnp.float32) + update).astype(jnp.bfloat16)
        else:
            before = lax.dynamic_slice_in_dim(state_full, mine_first, feature_width, 1)
            update = dot32(hidden, last_out_w)
            return (before.astype(jnp.float32) + update).astype(jnp.bfloat16)


def solution(mesh):
    in_specs = (
        P("band", None),
        P("band", "feat"),
        P(None, "feat"),
        P("feat"),
        P("band", None, None),
        P("band", None, None),
        P("band", None, None),
        P("band", None),
        P("band", None),
        P("band", None, None),
        P(None, None, "feat"),
        P(None, None, "feat"),
        P(None, "feat"),
        P(None, None, "feat"),
        P(None, "feat"),
        P(None, "feat", None),
    )
    out_specs = P("band", "feat")
    return jax.shard_map(body, mesh=mesh, in_specs=in_specs, out_specs=out_specs, check_vma=False)
```

time: 169 us -> 120 us (0.71)
  waiting for transfers between devices: 59.6 us -> 10.8 us
  between operations: 13.3 us -> 0.2 us
  blocking collectives: 15 us -> 2.3 us
  local copies, waits for them, and re-layouts: 1.06 us -> 13.3 us
  starting transfers between devices: 21.5 us -> 31.6 us
  matrix products: 53.5 us -> 59.1 us
  other arithmetic: 4.29 us -> 2.06 us
    reduce_scatter x3 -> x0, waiting for transfers between devices: 34.1 us -> none  [body(): lax.psum_scatter(update_terms.astype(jnp.bfloat16), 'feat', scatter_dimen...]
    all_to_all x1, waiting for transfers between devices: 25.5 us -> 10.8 us  [body(): lax.all_to_all(outgoing, 'band', split_axis=0, concat_axis=0, tiled=True)]
    all_gather x6 -> x1, blocking collectives: 15 us -> 2.3 us  [body(): state_full = lax.all_gather(mesh_latent, 'feat', axis=1, tiled=True)]
    ppermute x4 -> x10, starting transfers between devices: 9.37 us -> 19.5 us  [the longest x2 13.5 us: mesh_messages(): from_upper = lax.ppermute(outgoing[width:], 'band', down)]
    dot_general x8 -> x14, matrix products: 34.2 us -> 41 us  [dot32(): return jnp.dot(a, b, preferred_element_type=jnp.float32)]
    concatenate x0 -> x2, local copies, waits for them, and re-layouts: none -> 4.77 us  [the longest x1 2.71 us: body(): in_w = jnp.concatenate([node_in_w, swap_cores(node_in_w)], 2)]
    unnamed x22, local copies, waits for them, and re-layouts: 0.06 us -> 4.82 us
    convert_element_type x3 -> x1, other arithmetic: 3.46 us -> 0.81 us  [body(): jnp.concatenate([node_bias, swap_cores(node_bias)], 1).astype(jnp.float32)]
  transfers between devices with their start and end apart: 8 -> 11, of which waited for: 4 -> 1; matrix products, arithmetic and copies ran while one was open for 8% -> 24% of each run, Pallas kernels for 0% -> 0%
where the time goes in v1:
time: 120 us; the launch traced here: 119 us
  matrix products  59.1 us (49%)
  starting transfers between devices  31.6 us (26%)
  local copies, waits for them, and re-layouts  13.3 us (11%)
  waiting for transfers between devices  10.8 us (9%)
  blocking collectives  2.3 us (2%)
  other arithmetic  2.06 us (2%)
    dot_general x14, matrix products, dot32(): return jnp.dot(a, b, preferred_element_type=jnp.float32)  41 us
    dot_general x5, matrix products, select_rows(): jnp.dot(selector, lookup_table, preferred_element_type=jnp.float32)  18.2 us
    ppermute x2, starting transfers between devices, mesh_messages(): from_upper = lax.ppermute(outgoing[width:], 'band', down)  13.5 us
    all_to_all x1, starting transfers between devices, body(): lax.all_to_all(outgoing, 'band', split_axis=0, concat_axis=0, tiled=True)  12.1 us
    all_to_all x1, waiting for transfers between devices, body(): lax.all_to_all(outgoing, 'band', split_axis=0, concat_axis=0, tiled=True)  10.8 us
    ppermute x6, starting transfers between devices, swap_cores(): return lax.ppermute(value, 'feat', [(0, 1), (1, 0)])  5.53 us
    unnamed x22, local copies, waits for them, and re-layouts  4.82 us
    concatenate x1, local copies, waits for them, and re-layouts, body(): in_w = jnp.concatenate([node_in_w, swap_cores(node_in_w)], 2)  2.71 us
  transfers between devices with their start and end apart: 11, of which 1 were waited for; matrix products, arithmetic and copies ran while one was open for 24% of the time, Pallas kernels for 0%

profile of v1, /device:TPU:1, one launch (start us, length us, event | category | flops | bytes accessed | tf_op | source)
XLA Modules:
  0.0 119.5 jit_solution(14537825751686349057)
XLA Ops:
  0.0 0.0 copy-start
  0.0 0.9 eq.41
  0.9 0.7 convert_element_type.110
  1.6 0.0 copy-done
  1.6 6.2 %fusion.20 = bf16[4096,256]{1,0:T(8,128)(2,1)} fusion(s32[4096]{0:T(1024)S(1)} %eq.41, bf16[1024,512]{1,0:T(8,128)(2,1)S(1)} %copy-done, bf16[512,256]{1,0:T(8,128)(2,1)} %param.18, f32[256]{0:T(256)S(1)} %convert_element_type.110), kind=kOutput, calls=%fused_computation.28 | convolution fusion | flops 2422734848 | bytes 3425280 | tf_op jit(solution)/shard_map/dot_general | solution.py:10
  7.7 12.1 %all-to-all-start = ((bf16[64,64,256]{2,1,0:T(8,128)(2,1)}), bf16[64,64,256]{2,1,0:T(8,128)(2,1)S(1)}, u32[]{:S(2)}, u32[]{:S(2)}) async-start(bf16[64,64,256]{2,1,0:T(8,128)(2,1)} %bitcast.118), calls=%async_computation | async-start | bytes 4194304 | tf_op jit(solution)/shard_map/all_to_all | solution.py:72
  19.9 1.0 collective-permute-start
  20.9 0.1 collective-permute-start.3
  21.0 0.4 collective-permute-start.2
  21.4 0.0 copy-done.7
  21.4 0.6 slice_convert_fusion
  22.0 2.1 %constant_dynamic-update-slice_fusion.3 = bf16[3,512,512]{2,1,0:T(8,128)(2,1)} fusion(bf16[3,256,512]{2,1,0:T(8,128)(2,1)} %param.31), kind=kLoop, calls=%fused_computation.119 | loop fusion | bytes 1572864
  24.1 2.7 %constant_dynamic-update-slice_fusion.1 = bf16[3,1024,512]{2,1,0:T(8,128)(2,1)} fusion(bf16[3,1024,256]{2,1,0:T(8,128)(2,1)} %param.29), kind=kLoop, calls=%fused_computation.117 | loop fusion | bytes 3145728
  26.8 0.0 copy-done.4
  26.8 2.3 %all_gather.3 = bf16[256,512]{1,0:T(8,128)(2,1)S(1)} all-gather(bf16[256,256]{1,0:T(8,128)(2,1)} %param.17), channel_id=1, replica_groups=mesh['band'=64,'feat'=2] {'feat'}, dimensions={1}, use_global_device_ids=true | all-gather | bytes 393216 | tf_op jit(solution)/shard_map/all_gather | solution.py:74
  29.1 0.0 copy-done.5
  29.1 0.1 eq.38
  29.2 0.1 broadcast_in_dim.23
  29.3 0.8 eq.95
  30.0 0.0 collective-permute-done.2
  30.0 0.8 fusion.90
  30.8 0.0 collective-permute-done.3
  30.8 2.1 %constant_dynamic-update-slice_fusion.2 = bf16[3,512,512]{2,1,0:T(8,128)(2,1)} fusion(bf16[3,512,512]{2,1,0:T(8,128)(2,1)} %constant_dynamic-update-slice_fusion.3, bf16[3,256,512]{2,1,0:T(8,128)(2,1)} %collective-permute-done.3), kind=kLoop, calls=%fused_computation.118 | loop fusion | bytes 1572864 | tf_op jit(solution)/shard_map/concatenate | solution.py:76
  32.9 1.9 %slice.113 = bf16[1,512,512]{2,1,0:T(8,128)(2,1)} slice(bf16[3,512,512]{2,1,0:T(8,128)(2,1)} %constant_dynamic-update-slice_fusion.2), slice={[2:3], [0:512], [0:512]} | slice | bytes 1048576 | tf_op jit(solution)/shard_map/slice | solution.py:83
  34.8 0.0 collective-permute-done
  34.8 2.7 %constant_dynamic-update-slice_fusion = bf16[3,1024,512]{2,1,0:T(8,128)(2,1)} fusion(bf16[3,1024,512]{2,1,0:T(8,128)(2,1)} %constant_dynamic-update-slice_fusion.1, bf16[3,1024,256]{2,1,0:T(8,128)(2,1)} %collective-permute-done), kind=kLoop, calls=%fused_computation.116 | loop fusion | bytes 3145728 | tf_op jit(solution)/shard_map/concatenate | solution.py:75
  37.5 10.8 %all-to-all-done = bf16[64,64,256]{2,1,0:T(8,128)(2,1)S(1)} async-done(((bf16[64,64,256]{2,1,0:T(8,128)(2,1)}), bf16[64,64,256]{2,1,0:T(8,128)(2,1)S(1)}, u32[]{:S(2)}, u32[]{:S(2)}) %all-to-all-start) | async-done | bytes 2097184 | tf_op jit(solution)/shard_map/all_to_all | solution.py:72
  48.3 0.7 fusion.37
  49.0 0.0 copy-start.1
  49.0 0.0 copy-start.2
  49.1 2.5 %collective-permute-start.1 = (bf16[256,256]{1,0:T(8,128)(2,1)S(1)}, bf16[256,256]{1,0:T(8,128)(2,1)S(1)}, u32[]{:S(2)}, u32[]{:S(2)}) collective-permute-start(bf16[256,256]{1,0:T(8,128)(2,1)S(1)} %fusion.37), channel_id=1, source_target_pairs={{0,1},{1,0},{2,3},{3,2},{4,5},{5,4},{6,7},{7,6},{8,9},{9,8},{10,11... | collective-permute-start | bytes 393224 | tf_op jit(solution)/shard_map/ppermute | solution.py:16
  51.6 1.2 %fusion.51 = f32[256,512]{0,1:T(8,128)S(1)} fusion(bf16[256,256]{1,0:T(8,128)(2,1)S(1)} %fusion.37, bf16[3,1024,512]{2,1,0:T(8,128)(2,1)} %constant_dynamic-update-slice_fusion, s32[]{:T(128)S(6)} %select_n.26), kind=kOutput, calls=%fused_computation.85 | convolution fusion | flops 67108864 | bytes 917508 | tf_op jit(solution)/shard_map/dot_general | solution.py:20
  52.8 0.0 collective-permute-done.1
  52.8 1.2 %fusion.50 = f32[256,512]{0,1:T(8,128)S(1)} fusion(bf16[256,256]{1,0:T(8,128)(2,1)S(1)} %collective-permute-done.1, bf16[3,1024,512]{2,1,0:T(8,128)(2,1)} %constant_dynamic-update-slice_fusion, s32[]{:T(128)S(6)} %select_n.27), kind=kOutput, calls=%fused_computation.83 | convolution fusion | flops 67108864 | bytes 917508 | tf_op jit(solution)/shard_map/dot_general | solution.py:20
  54.1 2.0 %fusion.32 = bf16[256,512]{1,0:T(8,128)(2,1)S(1)} fusion(bf16[3,512,512]{2,1,0:T(8,128)(2,1)} %constant_dynamic-update-slice_fusion.2, f32[256,512]{0,1:T(8,128)S(1)} %fusion.50, f32[256,512]{0,1:T(8,128)S(1)} %fusion.51, bf16[256,512]{1,0:T(8,128)(2,1)S(1)} %all_gather.3, bf16[3,1024,512]{2,1,0:T(8,128)(2,1)} %constant_dynamic-update-slice_fusion, ...), kind=kOutput, calls=%fused_computation.46 | convolution fusion | flops 269877248 | bytes 2885632 | tf_op jit(solution)/shard_map/dot_general | solution.py:20
  56.1 0.0 copy-done.9
  56.1 1.2 fusion.34
  57.3 0.2 convolution_convert_fusion.5
  57.5 0.4 collective-permute-start.4
  57.9 6.6 %collective-permute-start.5 = (bf16[64,256]{1,0:T(8,128)(2,1)S(1)}, bf16[64,256]{1,0:T(8,128)(2,1)S(1)}, u32[]{:S(2)}, u32[]{:S(2)}) collective-permute-start(bf16[64,256]{1,0:T(8,128)(2,1)S(1)} %get-tuple-element.8), channel_id=1, source_target_pairs={{2,0},{4,2},{6,4},{8,6},{10,8},{12,10},{14,12},{16,14},{18,16},{20... | collective-permute-start | bytes 98312 | tf_op jit(solution)/shard_map/ppermute | solution.py:32
  64.5 0.0 copy-done.1
  64.5 5.8 %fusion.8 = f32[12288,256]{1,0:T(8,128)} fusion(s32[12288]{0:T(1024)S(1)} %bitcast.119, bf16[256,512]{1,0:T(8,128)(2,1)S(1)} %fusion.32, bf16[2,512,256]{2,1,0:T(8,128)(2,1)S(1)} %copy-done.2), kind=kOutput, calls=%fused_computation.12 | convolution fusion | flops 1687224320 | bytes 13156352 | tf_op jit(solution)/shard_map/dot_general | solution.py:10
  70.3 0.0 collective-permute-done.4
  70.3 0.0 collective-permute-done.5
  70.3 12.0 %fusion.40 = bf16[256,256]{1,0:T(8,128)(2,1)S(1)} fusion(f32[12288,256]{1,0:T(8,128)} %fusion.8, s32[12288]{0:T(1024)S(1)} %or_select_fusion, s32[12288]{0:T(1024)S(1)} %bitcast.120, bf16[64,256]{1,0:T(8,128)(2,1)S(1)} %collective-permute-done.5, bf16[64,256]{1,0:T(8,128)(2,1)S(1)} %collective-permute-done.4, bf16[256,256]{1,0:T(8,128)(2,1)S(1)} %fusion.34), kind=kOutput, calls=%fused_computation.57 | convolution fusion | flops 4060217344 | bytes 13008896 | tf_op jit(solution)/shard_map/dot_general | solution.py:20
  82.3 0.0 copy-start.8
  82.4 0.7 collective-permute-start.6
  83.1 1.2 %fusion.49 = f32[256,512]{0,1:T(8,128)S(1)} fusion(bf16[256,256]{1,0:T(8,128)(2,1)S(1)} %fusion.40, bf16[3,1024,512]{2,1,0:T(8,128)(2,1)} %constant_dynamic-update-slice_fusion, s32[]{:T(128)S(6)} %add.173, s32[]{:T(128)S(6)} %select_n.26), kind=kOutput, calls=%fused_computation.81 | convolution fusion | flops 67108864 | bytes 917512 | tf_op jit(solution)/shard_map/dot_general | solution.py:20
  84.3 0.0 collective-permute-done.6
  84.3 1.2 %fusion.48 = f32[256,512]{0,1:T(8,128)S(1)} fusion(bf16[256,256]{1,0:T(8,128)(2,1)S(1)} %collective-permute-done.6, bf16[3,1024,512]{2,1,0:T(8,128)(2,1)} %constant_dynamic-update-slice_fusion, s32[]{:T(128)S(6)} %add.173, s32[]{:T(128)S(6)} %select_n.27), kind=kOutput, calls=%fused_computation.79 | convolution fusion | flops 67108864 | bytes 917512 | tf_op jit(solution)/shard_map/dot_general | solution.py:20
  85.5 2.1 %fusion.33 = bf16[256,512]{1,0:T(8,128)(2,1)S(1)} fusion(bf16[3,512,512]{2,1,0:T(8,128)(2,1)} %constant_dynamic-update-slice_fusion.2, f32[256,512]{0,1:T(8,128)S(1)} %fusion.48, f32[256,512]{0,1:T(8,128)S(1)} %fusion.49, bf16[256,512]{1,0:T(8,128)(2,1)S(1)} %fusion.32, bf16[3,1024,512]{2,1,0:T(8,128)(2,1)} %constant_dynamic-update-slice_fusion, ...), kind=kOutput, calls=%fused_computation.47 | convolution fusion | flops 269877248 | bytes 2885632 | tf_op jit(solution)/shard_map/dot_general | solution.py:20
  87.6 1.2 fusion.35
  88.8 0.2 convolution_convert_fusion.4
  89.0 0.1 collective-permute-start.7
  89.1 6.9 %collective-permute-start.8 = (bf16[64,256]{1,0:T(8,128)(2,1)S(1)}, bf16[64,256]{1,0:T(8,128)(2,1)S(1)}, u32[]{:S(2)}, u32[]{:S(2)}) collective-permute-start(bf16[64,256]{1,0:T(8,128)(2,1)S(1)} %get-tuple-element.6), channel_id=1, source_target_pairs={{2,0},{4,2},{6,4},{8,6},{10,8},{12,10},{14,12},{16,14},{18,16},{20... | collective-permute-start | bytes 98312 | tf_op jit(solution)/shard_map/ppermute | solution.py:32
  96.0 5.8 %fusion.7 = f32[12288,256]{1,0:T(8,128)} fusion(s32[12288]{0:T(1024)S(1)} %bitcast.121, bf16[256,512]{1,0:T(8,128)(2,1)S(1)} %fusion.33, bf16[2,512,256]{2,1,0:T(8,128)(2,1)S(1)} %copy-done.2), kind=kOutput, calls=%fused_computation.10 | convolution fusion | flops 1687224320 | bytes 13156352 | tf_op jit(solution)/shard_map/dot_general | solution.py:10
  101.8 0.0 collective-permute-done.7
  101.8 0.0 collective-permute-done.8
  101.8 12.1 %fusion.41 = bf16[256,256]{1,0:T(8,128)(2,1)S(1)} fusion(f32[12288,256]{1,0:T(8,128)} %fusion.7, s32[12288]{0:T(1024)S(1)} %or_select_fusion, s32[12288]{0:T(1024)S(1)} %bitcast.122, bf16[64,256]{1,0:T(8,128)(2,1)S(1)} %collective-permute-done.8, bf16[64,256]{1,0:T(8,128)(2,1)S(1)} %collective-permute-done.7, bf16[256,256]{1,0:T(8,128)(2,1)S(1)} %fusion.35), kind=kOutput, calls=%fused_computation.58 | convolution fusion | flops 4060217344 | bytes 13008896 | tf_op jit(solution)/shard_map/dot_general | solution.py:20
  113.9 0.7 collective-permute-start.9
  114.6 1.2 %fusion.47 = f32[256,512]{0,1:T(8,128)S(1)} fusion(bf16[256,256]{1,0:T(8,128)(2,1)S(1)} %fusion.41, bf16[3,1024,512]{2,1,0:T(8,128)(2,1)} %constant_dynamic-update-slice_fusion, s32[]{:T(128)S(6)} %add.175, s32[]{:T(128)S(6)} %select_n.26), kind=kOutput, calls=%fused_computation.77 | convolution fusion | flops 67108864 | bytes 917512 | tf_op jit(solution)/shard_map/dot_general | solution.py:20
  115.8 0.0 collective-permute-done.9
  115.9 1.2 %fusion.46 = f32[256,512]{0,1:T(8,128)S(1)} fusion(bf16[256,256]{1,0:T(8,128)(2,1)S(1)} %collective-permute-done.9, bf16[3,1024,512]{2,1,0:T(8,128)(2,1)} %constant_dynamic-update-slice_fusion, s32[]{:T(128)S(6)} %add.175, s32[]{:T(128)S(6)} %select_n.27), kind=kOutput, calls=%fused_computation.75 | convolution fusion | flops 67108864 | bytes 917512 | tf_op jit(solution)/shard_map/dot_general | solution.py:20
  117.1 2.4 %fusion.36 = bf16[256,256]{1,0:T(8,128)(2,1)} fusion(f32[256,512]{0,1:T(8,128)S(1)} %fusion.46, f32[256,512]{0,1:T(8,128)S(1)} %fusion.47, bf16[256,512]{1,0:T(8,128)(2,1)S(1)} %fusion.33, bf16[3,1024,512]{2,1,0:T(8,128)(2,1)} %constant_dynamic-update-slice_fusion, bf16[1,512,512]{2,1,0:T(8,128)(2,1)S(1)} %copy-done.3, s32[]{:T(128)S(6)} %select_n.25, ...), kind=kOutput, calls=%fused_computation.53 | convolution fusion | flops 202571776 | bytes 2362368 | tf_op jit(solution)/shard_map/dot_general | solution.py:20
  (13 shorter events, 0.1 us)
Async XLA Ops:
  0.0 1.6 %copy-start = (bf16[1024,512]{1,0:T(8,128)(2,1)S(1)}, bf16[1024,512]{1,0:T(8,128)(2,1)}, u32[]{:S(2)}) copy-start(bf16[1024,512]{1,0:T(8,128)(2,1)} %param.16) | copy-start | bytes 3145732
  7.7 13.7 %copy-start.7 = (bf16[2,256]{1,0:T(2,128)(2,1)S(1)}, bf16[2,256]{1,0:T(2,128)(2,1)}, u32[]{:S(2)}) copy-start(bf16[2,256]{1,0:T(2,128)(2,1)} %param.28) | copy-start | bytes 3076
  7.7 19.0 %copy-start.4 = (s32[1,12288]{1,0:T(1,128)S(1)}, s32[1,12288]{1,0:T(1,128)}, u32[]{:S(2)}) copy-start(s32[1,12288]{1,0:T(1,128)} %param.23) | copy-start | bytes 147460
  7.7 21.4 %copy-start.5 = (s32[1,64,64]{2,1,0:T(8,128)S(1)}, s32[1,64,64]{2,1,0:T(8,128)}, u32[]{:S(2)}) copy-start(s32[1,64,64]{2,1,0:T(8,128)} %param.21) | copy-start | bytes 49156
  7.7 21.4 %copy-start.6 = (bf16[1,64,64]{2,1,0:T(8,128)(2,1)S(1)}, bf16[1,64,64]{2,1,0:T(8,128)(2,1)}, u32[]{:S(2)}) copy-start(bf16[1,64,64]{2,1,0:T(8,128)(2,1)} %param.22) | copy-start | bytes 24580
  7.7 40.6 %all-to-all-start = ((bf16[64,64,256]{2,1,0:T(8,128)(2,1)}), bf16[64,64,256]{2,1,0:T(8,128)(2,1)S(1)}, u32[]{:S(2)}, u32[]{:S(2)}) async-start(bf16[64,64,256]{2,1,0:T(8,128)(2,1)} %bitcast.118), calls=%async_computation | async-start | bytes 4194304 | tf_op jit(solution)/shard_map/all_to_all | solution.py:72
  19.9 14.9 %collective-permute-start = (bf16[3,1024,256]{2,1,0:T(8,128)(2,1)}, bf16[3,1024,256]{2,1,0:T(8,128)(2,1)}, u32[]{:S(2)}, u32[]{:S(2)}) collective-permute-start(bf16[3,1024,256]{2,1,0:T(8,128)(2,1)} %param.29), channel_id=1, source_target_pairs={{0,1},{1,0},{2,3},{3,2},{4,5},{5,4},{6,7},{7,6},{8,9},{9,8},{10,11... | collective-permute-start | bytes 4718600 | tf_op jit(solution)/shard_map/ppermute | solution.py:16
  20.9 9.9 %collective-permute-start.3 = (bf16[3,256,512]{2,1,0:T(8,128)(2,1)}, bf16[3,256,512]{2,1,0:T(8,128)(2,1)}, u32[]{:S(2)}, u32[]{:S(2)}) collective-permute-start(bf16[3,256,512]{2,1,0:T(8,128)(2,1)} %param.31), channel_id=1, source_target_pairs={{0,1},{1,0},{2,3},{3,2},{4,5},{5,4},{6,7},{7,6},{8,9},{9,8},{10,11... | collective-permute-start | bytes 2359304 | tf_op jit(solution)/shard_map/ppermute | solution.py:16
  21.0 9.0 %collective-permute-start.2 = (bf16[3,256]{1,0:T(4,128)(2,1)}, bf16[3,256]{1,0:T(4,128)(2,1)}, u32[]{:S(2)}, u32[]{:S(2)}) collective-permute-start(bf16[3,256]{1,0:T(4,128)(2,1)} %param.30), channel_id=1, source_target_pairs={{0,1},{1,0},{2,3},{3,2},{4,5},{5,4},{6,7},{7,6},{8,9},{9,8},{10,11... | collective-permute-start | bytes 4616 | tf_op jit(solution)/shard_map/ppermute | solution.py:16
  49.0 7.1 %copy-start.9 = (f32[1,256]{1,0:T(1,128)S(1)}, f32[1,256]{1,0:T(1,128)}, u32[]{:S(2)}) copy-start(f32[1,256]{1,0:T(1,128)} %get-tuple-element.13) | copy-start | bytes 3076
  49.0 15.5 %copy-start.1 = (s32[1,12288]{1,0:T(1,128)S(1)}, s32[1,12288]{1,0:T(1,128)}, u32[]{:S(2)}) copy-start(s32[1,12288]{1,0:T(1,128)} %param.24) | copy-start | bytes 147460
  49.0 15.5 %copy-start.2 = (bf16[2,512,256]{2,1,0:T(8,128)(2,1)S(1)}, bf16[2,512,256]{2,1,0:T(8,128)(2,1)}, u32[]{:S(2)}) copy-start(bf16[2,512,256]{2,1,0:T(8,128)(2,1)} %param.27) | copy-start | bytes 1572868
  49.1 3.8 %collective-permute-start.1 = (bf16[256,256]{1,0:T(8,128)(2,1)S(1)}, bf16[256,256]{1,0:T(8,128)(2,1)S(1)}, u32[]{:S(2)}, u32[]{:S(2)}) collective-permute-start(bf16[256,256]{1,0:T(8,128)(2,1)S(1)} %fusion.37), channel_id=1, source_target_pairs={{0,1},{1,0},{2,3},{3,2},{4,5},{5,4},{6,7},{7,6},{8,9},{9,8},{10,11... | collective-permute-start | bytes 393224 | tf_op jit(solution)/shard_map/ppermute | solution.py:16
  57.5 12.8 %collective-permute-start.4 = (bf16[64,256]{1,0:T(8,128)(2,1)S(1)}, bf16[64,256]{1,0:T(8,128)(2,1)S(1)}, u32[]{:S(2)}, u32[]{:S(2)}) collective-permute-start(bf16[64,256]{1,0:T(8,128)(2,1)S(1)} %get-tuple-element.7), channel_id=1, source_target_pairs={{0,2},{2,4},{4,6},{6,8},{8,10},{10,12},{12,14},{14,16},{16,18},{18... | collective-permute-start | bytes 98312 | tf_op jit(solution)/shard_map/ppermute | solution.py:31
  57.9 12.4 %collective-permute-start.5 = (bf16[64,256]{1,0:T(8,128)(2,1)S(1)}, bf16[64,256]{1,0:T(8,128)(2,1)S(1)}, u32[]{:S(2)}, u32[]{:S(2)}) collective-permute-start(bf16[64,256]{1,0:T(8,128)(2,1)S(1)} %get-tuple-element.8), channel_id=1, source_target_pairs={{2,0},{4,2},{6,4},{8,6},{10,8},{12,10},{14,12},{16,14},{18,16},{20... | collective-permute-start | bytes 98312 | tf_op jit(solution)/shard_map/ppermute | solution.py:32
  82.3 5.3 %copy-start.8 = (f32[1,256]{1,0:T(1,128)S(1)}, f32[1,256]{1,0:T(1,128)}, u32[]{:S(2)}) copy-start(f32[1,256]{1,0:T(1,128)} %get-tuple-element.12) | copy-start | bytes 3076
  82.4 1.9 %collective-permute-start.6 = (bf16[256,256]{1,0:T(8,128)(2,1)S(1)}, bf16[256,256]{1,0:T(8,128)(2,1)S(1)}, u32[]{:S(2)}, u32[]{:S(2)}) collective-permute-start(bf16[256,256]{1,0:T(8,128)(2,1)S(1)} %fusion.40), channel_id=1, source_target_pairs={{0,1},{1,0},{2,3},{3,2},{4,5},{5,4},{6,7},{7,6},{8,9},{9,8},{10,11... | collective-permute-start | bytes 393224 | tf_op jit(solution)/shard_map/ppermute | solution.py:16
  89.0 12.8 %collective-permute-start.7 = (bf16[64,256]{1,0:T(8,128)(2,1)S(1)}, bf16[64,256]{1,0:T(8,128)(2,1)S(1)}, u32[]{:S(2)}, u32[]{:S(2)}) collective-permute-start(bf16[64,256]{1,0:T(8,128)(2,1)S(1)} %get-tuple-element.5), channel_id=1, source_target_pairs={{0,2},{2,4},{4,6},{6,8},{8,10},{10,12},{12,14},{14,16},{16,18},{18... | collective-permute-start | bytes 98312 | tf_op jit(solution)/shard_map/ppermute | solution.py:31
  89.1 12.7 %collective-permute-start.8 = (bf16[64,256]{1,0:T(8,128)(2,1)S(1)}, bf16[64,256]{1,0:T(8,128)(2,1)S(1)}, u32[]{:S(2)}, u32[]{:S(2)}) collective-permute-start(bf16[64,256]{1,0:T(8,128)(2,1)S(1)} %get-tuple-element.6), channel_id=1, source_target_pairs={{2,0},{4,2},{6,4},{8,6},{10,8},{12,10},{14,12},{16,14},{18,16},{20... | collective-permute-start | bytes 98312 | tf_op jit(solution)/shard_map/ppermute | solution.py:32
  101.8 15.3 %copy-start.3 = (bf16[1,512,512]{2,1,0:T(8,128)(2,1)S(1)}, bf16[1,512,512]{2,1,0:T(8,128)(2,1)}, u32[]{:S(2)}) copy-start(bf16[1,512,512]{2,1,0:T(8,128)(2,1)} %slice.113) | copy-start | bytes 1572868
  113.9 1.9 %collective-permute-start.9 = (bf16[256,256]{1,0:T(8,128)(2,1)S(1)}, bf16[256,256]{1,0:T(8,128)(2,1)S(1)}, u32[]{:S(2)}, u32[]{:S(2)}) collective-permute-start(bf16[256,256]{1,0:T(8,128)(2,1)S(1)} %fusion.41), channel_id=1, source_target_pairs={{0,1},{1,0},{2,3},{3,2},{4,5},{5,4},{6,7},{7,6},{8,9},{9,8},{10,11... | collective-permute-start | bytes 393224 | tf_op jit(solution)/shard_map/ppermute | solution.py:16

commit v2 on v1

v2 whole, which is shorter than its diff:
```python
import functools

import jax
import jax.numpy as jnp
from jax import lax
from jax.experimental import pallas as pl
from jax.experimental.pallas import tpu as pltpu
from jax.sharding import PartitionSpec as P

VMEM = pl.BlockSpec(memory_space=pltpu.VMEM)
SMEM = pl.BlockSpec(memory_space=pltpu.SMEM)
F32 = jnp.float32
BF16 = jnp.bfloat16


def dot32(a, b):
    return jnp.dot(a, b, preferred_element_type=F32)


def dot32_nt(a, b):
    return lax.dot_general(a, b, (((1,), (1,)), ((), ())), preferred_element_type=F32)


def silu(v):
    half = 0.5 * v
    return half + half * jnp.tanh(half)


def one_hot_columns(row, count):
    ids = lax.broadcasted_iota(jnp.int32, (count, row.shape[1]), 0).astype(jnp.int16)
    return jnp.where(ids == row.astype(jnp.int16), jnp.ones((), BF16), jnp.zeros((), BF16))


def call(kernel, name, out_shape, in_specs, flops, limit=24):
    many = isinstance(out_shape, tuple)
    return pl.pallas_call(
        kernel,
        name=name,
        out_shape=out_shape,
        in_specs=in_specs,
        out_specs=(VMEM,) * len(out_shape) if many else VMEM,
        compiler_params=pltpu.CompilerParams(vmem_limit_bytes=limit * 2**20),
        cost_estimate=pl.CostEstimate(flops=flops, bytes_accessed=2**20, transcendentals=0),
    )


def node_hidden(core, state, mine, other, in_mine, in_other, bias_mine, bias_other):
    wide = state.shape[1]
    first = core == 0
    low = jnp.where(first, mine[...], other[...])
    high = jnp.where(first, other[...], mine[...])
    inputs = jnp.concatenate([state[...], low, high], 1)
    hidden_mine = silu(dot32(inputs, in_mine[...]) + bias_mine[...]).astype(BF16)
    hidden_other = silu(dot32(inputs, in_other[...]) + bias_other[...]).astype(BF16)
    return hidden_mine, hidden_other


def node_kernel(
    core, state, mine, other, in_mine, in_other, bias_mine, bias_other, out_mine, out_other,
    send_w, recv_w, edge_bias, halo_hot, state_out, sender_out, receiver_out, up_out, down_out,
):
    hidden_mine, hidden_other = node_hidden(
        core[0], state, mine, other, in_mine, in_other, bias_mine, bias_other
    )
    update = dot32(hidden_mine, out_mine[...]) + dot32(hidden_other, out_other[...])
    after = (state[...].astype(F32) + update).astype(BF16)
    state_out[...] = after
    sender = (dot32(after, send_w[...]) + edge_bias[...]).astype(BF16)
    sender_out[...] = sender
    receiver_out[...] = dot32(after, recv_w[...]).astype(BF16)
    leaving = dot32(halo_hot[...], sender).astype(BF16)
    width = up_out.shape[0]
    up_out[...] = leaving[:width]
    down_out[...] = leaving[width:]


def last_kernel(
    core, state, mine, other, in_mine, in_other, bias_mine, bias_other, out_mine, out_other, result
):
    hidden_mine, hidden_other = node_hidden(
        core[0], state, mine, other, in_mine, in_other, bias_mine, bias_other
    )
    first = core[0] == 0
    narrow = result.shape[1]

    def mine_of(ref):
        return jnp.where(first, ref[:, :narrow], ref[:, narrow:])

    update = dot32(hidden_mine, mine_of(out_mine)) + dot32(hidden_other, mine_of(out_other))
    result[...] = (mine_of(state).astype(F32) + update).astype(BF16)


def local_kernel(source, node, sender, receiver, pre):
    nodes = sender.shape[0]
    table = jnp.concatenate([sender[...].T, receiver[...].T], 1)
    chosen = jnp.concatenate(
        [one_hot_columns(source[...], nodes), one_hot_columns(node[...], nodes)], 0
    )
    pre[...] = dot32(table, chosen)


def halo_kernel(source, node, pre, lower, upper, aggregate):
    nodes = aggregate.shape[0]
    table = jnp.concatenate([lower[...], upper[...]], 0).T
    chosen = one_hot_columns(source[...] - nodes, table.shape[1])
    messages = silu(pre[...] + dot32(table, chosen)).astype(BF16)
    aggregate[...] = dot32_nt(one_hot_columns(node[...], nodes), messages).astype(BF16)


def select_rows(lookup_table, indices):
    row_ids = lax.broadcasted_iota(jnp.int32, (indices.shape[0], lookup_table.shape[0]), 1)
    selector = (indices[:, None] == row_ids).astype(lookup_table.dtype)
    return dot32(selector, lookup_table).astype(lookup_table.dtype)


def swap_cores(value):
    return lax.ppermute(value, "feat", [(0, 1), (1, 0)])


def body(
    grid_latent,
    mesh_latent,
    grid_in_w,
    grid_bias,
    g2m_src,
    g2m_dst,
    g2m_weight,
    mesh_src,
    mesh_dst,
    halo_index,
    edge_send_w,
    edge_recv_w,
    edge_bias,
    node_in_w,
    node_bias,
    node_out_w,
):
    feature_width = grid_in_w.shape[1]
    nodes = mesh_latent.shape[0]
    edges = mesh_src.shape[1]
    halo = halo_index.shape[2]
    partitions = lax.axis_size("band")
    core = lax.axis_index("feat").astype(jnp.int32).reshape(1)
    part = lax.axis_index("band")
    embedding = silu(dot32(grid_latent, grid_in_w) + grid_bias.astype(F32)).astype(BF16)
    band_count = g2m_src.shape[1]
    slot_count = g2m_src.shape[2]
    outgoing = select_rows(embedding, g2m_src[0].reshape(-1)).reshape(
        band_count, slot_count, feature_width
    )
    incoming = lax.all_to_all(outgoing, "band", split_axis=0, concat_axis=0, tiled=True)

    state = lax.all_gather(mesh_latent, "feat", axis=1, tiled=True)
    in_other = swap_cores(node_in_w)
    out_other = swap_cores(node_out_w)
    bias_other = swap_cores(node_bias)
    wide = state.shape[1]

    source = mesh_src
    in_lower = (source >= nodes) & (source < nodes + halo)
    in_upper = source >= nodes + halo
    outside = (in_lower & (part == 0)) | (in_upper & (part == partitions - 1))
    source = jnp.where(outside, -1, source)
    halo_ids = lax.broadcasted_iota(jnp.int32, (2 * halo, nodes), 1)
    halo_hot = (halo_index[0].reshape(-1)[:, None] == halo_ids).astype(BF16)

    slot_rows = incoming.reshape(-1, feature_width)
    slot_nodes = g2m_dst[0].reshape(-1)
    slot_weights = g2m_weight[0].reshape(-1)
    node_ids = lax.broadcasted_iota(jnp.int32, (nodes, slot_nodes.shape[0]), 0)
    matrix = jnp.where(node_ids == slot_nodes[None, :], slot_weights[None, :], jnp.zeros((), BF16))
    aggregate = dot32(matrix, slot_rows).astype(BF16)

    up = [(i, (i + 1) % partitions) for i in range(partitions)]
    down = [(j, i) for i, j in up]
    layer_total = node_in_w.shape[0]
    node_flops = 2 * nodes * wide * (2 * wide + wide)
    for layer in range(layer_total):
        operands = (
            core,
            state,
            aggregate,
            swap_cores(aggregate),
            node_in_w[layer],
            in_other[layer],
            node_bias[layer].astype(F32)[None],
            bias_other[layer].astype(F32)[None],
            node_out_w[layer],
            out_other[layer],
        )
        if layer + 1 == layer_total:
            return call(
                last_kernel,
                "node_last",
                jax.ShapeDtypeStruct((nodes, feature_width), BF16),
                [SMEM] + [VMEM] * 9,
                node_flops,
            )(*operands)
        half = jax.ShapeDtypeStruct((nodes, feature_width), BF16)
        edge_rows = jax.ShapeDtypeStruct((halo, feature_width), BF16)
        state, sender, receiver, to_upper, to_lower = call(
            node_kernel,
            "node",
            (jax.ShapeDtypeStruct((nodes, wide), BF16), half, half, edge_rows, edge_rows),
            [SMEM] + [VMEM] * 13,
            node_flops,
        )(
            *operands,
            edge_send_w[layer],
            edge_recv_w[layer],
            edge_bias[layer].astype(F32)[None],
            halo_hot,
        )
        from_lower = lax.ppermute(to_upper, "band", up)
        from_upper = lax.ppermute(to_lower, "band", down)
        pre = call(
            local_kernel,
            "edge_local",
            pltpu.VMEM((feature_width, edges), F32),
            [VMEM] * 4,
            4 * edges * nodes * feature_width,
        )(source, mesh_dst, sender, receiver)
        aggregate = call(
            halo_kernel,
            "edge_halo",
            half,
            [VMEM] * 5,
            3 * edges * nodes * feature_width,
        )(source, mesh_dst, pre, from_lower, from_upper)


def solution(mesh):
    in_specs = (
        P("band", None),
        P("band", "feat"),
        P(None, "feat"),
        P("feat"),
        P("band", None, None),
        P("band", None, None),
        P("band", None, None),
        P("band", None),
        P("band", None),
        P("band", None, None),
        P(None, None, "feat"),
        P(None, None, "feat"),
        P(None, "feat"),
        P(None, None, "feat"),
        P(None, "feat"),
        P(None, "feat", None),
    )
    out_specs = P("band", "feat")
    return jax.shard_map(body, mesh=mesh, in_specs=in_specs, out_specs=out_specs, check_vma=False)
```

time: 120 us -> 92.5 us (0.77)
  matrix products: 59.1 us -> 8.49 us
  Pallas kernels: 0 us -> 18.1 us
  waiting for transfers between devices: 10.8 us -> 21.3 us
  local copies, waits for them, and re-layouts: 13.3 us -> 9.27 us
    dot_general x19 -> x2, matrix products: 59.1 us -> 8.49 us  [dot32(): return jnp.dot(a, b, preferred_element_type=F32)]
    pallas_call x0 -> x7, Pallas kernels: none -> 18.1 us  [the longest x2 7.7 us: body(): call(halo_kernel, 'edge_halo', half, [VMEM] * 5, 3 * edges * nodes * feat...]
    all_to_all x1, waiting for transfers between devices: 10.8 us -> 19.3 us  [body(): lax.all_to_all(outgoing, 'band', split_axis=0, concat_axis=0, tiled=True)]
    squeeze x0 -> x5, local copies, waits for them, and re-layouts: none -> 6.92 us  [the longest x1 2.02 us: body(): out_other[layer]]
    concatenate x2 -> x0, local copies, waits for them, and re-layouts: 4.77 us -> none  [the longest x1 2.71 us: body(): in_w = jnp.concatenate([node_in_w, swap_cores(node_in_w)], 2)]
    unnamed x22 -> x40, local copies, waits for them, and re-layouts: 4.82 us -> 0.09 us
    ppermute x6, waiting for transfers between devices: 0.02 us -> 1.98 us  [swap_cores(): return lax.ppermute(value, 'feat', [(0, 1), (1, 0)])]
    slice x3 -> x0, local copies, waits for them, and re-layouts: 1.88 us -> none  [the longest x1 1.87 us: body(): out_w[-1]]
  transfers between devices with their start and end apart: 11 -> 11, of which waited for: 1 -> 3; matrix products, arithmetic and copies ran while one was open for 24% -> 21% of each run, Pallas kernels for 0% -> 8%
where the time goes in v2:
time: 92.5 us; the launch traced here: 92 us
  starting transfers between devices  30.9 us (33%)
  waiting for transfers between devices  21.3 us (23%)
  Pallas kernels  18.1 us (20%)
  local copies, waits for them, and re-layouts  9.27 us (10%)
  matrix products  8.49 us (9%)
  blocking collectives  1.99 us (2%)
  other arithmetic  1.69 us (2%)
    all_to_all x1, waiting for transfers between devices, body(): lax.all_to_all(outgoing, 'band', split_axis=0, concat_axis=0, tiled=True)  19.3 us
    ppermute x2, starting transfers between devices, body(): from_upper = lax.ppermute(to_lower, 'band', down)  13.5 us
    all_to_all x1, starting transfers between devices, body(): lax.all_to_all(outgoing, 'band', split_axis=0, concat_axis=0, tiled=True)  11.6 us
    dot_general x2, matrix products, dot32(): return jnp.dot(a, b, preferred_element_type=F32)  8.49 us
    pallas_call x2, Pallas kernels, body(): call(halo_kernel, 'edge_halo', half, [VMEM] * 5, 3 * edges * nodes * feat...  7.7 us
    pallas_call x2, Pallas kernels, body(): call(local_kernel, 'edge_local', pltpu.VMEM((feature_width, edges), F32),...  6.9 us
    ppermute x6, starting transfers between devices, swap_cores(): return lax.ppermute(value, 'feat', [(0, 1), (1, 0)])  5.29 us
    pallas_call x2, Pallas kernels, body(): call(node_kernel, 'node', (jax.ShapeDtypeStruct((nodes, wide), BF16), hal...  2.11 us
  transfers between devices with their start and end apart: 11, of which 3 were waited for; matrix products, arithmetic and copies ran while one was open for 21% of the time, Pallas kernels for 8%

profile of v2, /device:TPU:1, one launch (start us, length us, event | category | flops | bytes accessed | tf_op | source)
XLA Modules:
  0.0 92.0 jit_solution(11309566242427053065)
XLA Ops:
  0.0 0.0 copy-start
  0.0 1.4 %collective-permute-start.2 = (bf16[3,256]{1,0:T(4,128)(2,1)}, bf16[3,256]{1,0:T(4,128)(2,1)}, u32[]{:S(2)}, u32[]{:S(2)}) collective-permute-start(bf16[3,256]{1,0:T(4,128)(2,1)} %param.30), channel_id=1, source_target_pairs={{0,1},{1,0},{2,3},{3,2},{4,5},{5,4},{6,7},{7,6},{8,9},{9,8},{10,11... | collective-permute-start | bytes 4616 | tf_op jit(solution)/shard_map/ppermute | solution.py:117
  1.4 0.0 collective-permute-start.3
  1.4 0.5 collective-permute-start.1
  1.9 0.7 convert_element_type.48
  2.6 0.8 eq.39
  3.4 0.0 copy-done
  3.4 6.2 %fusion.2 = bf16[4096,256]{1,0:T(8,128)(2,1)} fusion(s32[4096]{0:T(1024)S(1)} %eq.39, bf16[1024,512]{1,0:T(8,128)(2,1)S(1)} %copy-done, bf16[512,256]{1,0:T(8,128)(2,1)} %param.18, f32[256]{0:T(256)S(1)} %convert_element_type.48), kind=kOutput, calls=%fused_computation.3 | convolution fusion | flops 2422472704 | bytes 3425280 | tf_op jit(solution)/shard_map/dot_general | solution.py:17
  9.6 0.0 copy-start.12
  9.6 11.6 %all-to-all-start = ((bf16[64,64,256]{2,1,0:T(8,128)(2,1)}), bf16[64,64,256]{2,1,0:T(8,128)(2,1)}, u32[]{:S(2)}, u32[]{:S(2)}) async-start(bf16[64,64,256]{2,1,0:T(8,128)(2,1)} %bitcast.1), calls=%async_computation | async-start | bytes 4194304 | tf_op jit(solution)/shard_map/all_to_all | solution.py:151
  21.3 0.0 copy-start.17
  21.3 0.0 copy-start.18
  21.3 0.0 copy-done.14
  21.3 0.1 or_select_fusion.source
  21.5 0.0 copy-done.19
  21.5 0.1 eq.42
  21.5 0.1 fusion.16.halo_hot
  21.6 0.0 copy-done.10
  21.7 0.9 slice_bitcast_fusion.9
  22.5 0.0 copy-done.11
  22.5 0.0 copy-done.12
  22.5 1.1 %slice_bitcast_fusion.10 = (bf16[512,256]{1,0:T(8,128)(2,1)}, bf16[512,256]{1,0:T(8,128)(2,1)}, bf16[512,256]{1,0:T(8,128)(2,1)}, bf16[512,256]{1,0:T(8,128)(2,1)}) fusion(bf16[2,512,256]{2,1,0:T(8,128)(2,1)S(1)} %copy-done.11, bf16[2,512,256]{2,1,0:T(8,128)(2,1)S(1)} %copy-done.12), kind=kLoop, calls=%fused_computation.27 | loop fusion | bytes 2097152 | tf_op jit(solution)/shard_map/squeeze | solution.py:210
  23.6 0.0 copy-done.17
  23.6 0.0 copy-done.18
  23.6 1.5 %slice_bitcast_fusion.3 = (bf16[1024,256]{1,0:T(8,128)(2,1)S(1)}, bf16[1024,256]{1,0:T(8,128)(2,1)S(1)}, bf16[1024,256]{1,0:T(8,128)(2,1)S(1)}) fusion(bf16[3,1024,256]{2,1,0:T(8,128)(2,1)} %param.29), kind=kLoop, calls=%fused_computation.18 | loop fusion | bytes 3145728 | tf_op jit(solution)/shard_map/squeeze | solution.py:184
  25.2 2.0 %all_gather.3.state = bf16[256,512]{1,0:T(8,128)(2,1)S(1)} all-gather(bf16[256,256]{1,0:T(8,128)(2,1)S(1)} %copy-done.13), channel_id=1, replica_groups=mesh['band'=64,'feat'=2] {'feat'}, dimensions={1}, use_global_device_ids=true | all-gather | bytes 393216 | tf_op jit(solution)/shard_map/all_gather | solution.py:153
  27.2 0.7 broadcast_in_dim.18
  27.8 0.7 eq.36
  28.5 0.0 collective-permute-done.2
  28.5 0.8 slice_convert_fusion
  29.3 0.0 collective-permute-done.3
  29.3 2.0 %slice_bitcast_fusion.6 = (bf16[256,512]{1,0:T(8,128)(2,1)}, bf16[256,512]{1,0:T(8,128)(2,1)S(1)}, bf16[256,512]{1,0:T(8,128)(2,1)}) fusion(bf16[3,256,512]{2,1,0:T(8,128)(2,1)} %collective-permute-done.3), kind=kLoop, calls=%fused_computation.23 | loop fusion | bytes 1572864 | tf_op jit(solution)/shard_map/squeeze | solution.py:189
  31.3 19.3 %all-to-all-done = bf16[64,64,256]{2,1,0:T(8,128)(2,1)} async-done(((bf16[64,64,256]{2,1,0:T(8,128)(2,1)}), bf16[64,64,256]{2,1,0:T(8,128)(2,1)}, u32[]{:S(2)}, u32[]{:S(2)}) %all-to-all-start) | async-done | bytes 2097184 | tf_op jit(solution)/shard_map/all_to_all | solution.py:151
  50.6 2.3 %fusion.9.mine = bf16[256,256]{1,0:T(8,128)(2,1)S(1)} fusion(bf16[4096,256]{1,0:T(8,128)(2,1)} %bitcast.2, s32[4096]{0:T(1024)} %eq.36, bf16[4096]{0:T(1024)(128)(2,1)} %broadcast_in_dim.18), kind=kOutput, calls=%fused_computation.12 | convolution fusion | flops 539033600 | bytes 2252800 | tf_op jit(solution)/shard_map/dot_general | solution.py:17
  52.9 0.0 copy-start.1
  53.0 0.0 copy-start.2
  53.0 0.0 copy-start.5
  53.0 0.0 copy-start.6
  53.0 1.6 %collective-permute-start = (bf16[256,256]{1,0:T(8,128)(2,1)S(1)}, bf16[256,256]{1,0:T(8,128)(2,1)S(1)}, u32[]{:S(2)}, u32[]{:S(2)}) collective-permute-start(bf16[256,256]{1,0:T(8,128)(2,1)S(1)} %fusion.9.mine), channel_id=1, source_target_pairs={{0,1},{1,0},{2,3},{3,2},{4,5},{5,4},{6,7},{7,6},{8,9},{9,8},{10,11... | collective-permute-start | bytes 393224 | tf_op jit(solution)/shard_map/ppermute | solution.py:117
  54.6 0.0 collective-permute-done.1
  54.6 1.5 %slice_bitcast_fusion = (bf16[1024,256]{1,0:T(8,128)(2,1)S(1)}, bf16[1024,256]{1,0:T(8,128)(2,1)S(1)}, bf16[1024,256]{1,0:T(8,128)(2,1)S(1)}) fusion(bf16[3,1024,256]{2,1,0:T(8,128)(2,1)} %collective-permute-done.1), kind=kLoop, calls=%fused_computation.15 | loop fusion | bytes 3145728 | tf_op jit(solution)/shard_map/squeeze | solution.py:185
  56.1 0.0 copy-start.9
  56.1 0.0 collective-permute-done.other
  56.2 1.1 %node.6 = (bf16[256,512]{1,0:T(8,128)(2,1)S(1)}, bf16[256,256]{1,0:T(8,128)(2,1)S(1)}, bf16[256,256]{1,0:T(8,128)(2,1)S(1)}, bf16[64,256]{1,0:T(8,128)(2,1)S(1)}, bf16[64,256]{1,0:T(8,128)(2,1)S(1)}) custom-call(s32[1]{0:T(128)} %bitcast.core, bf16[256,512]{1,0:T(8,128)(2,1)S(1)} %all_gather.3.state, bf16[256,256]{1,0:T(8,128)(2,1)S(1)} %fusion.9.mine, ...), custom_call_target="tpu_custom_call" | custom-call | flops 402653184 | bytes 1048576 | tf_op jit(solution)/shard_map/node/pallas_call | solution.py:201
  57.2 0.3 collective-permute-start.4
  57.6 6.6 %collective-permute-start.5 = (bf16[64,256]{1,0:T(8,128)(2,1)S(1)}, bf16[64,256]{1,0:T(8,128)(2,1)S(1)}, u32[]{:S(2)}, u32[]{:S(2)}) collective-permute-start(bf16[64,256]{1,0:T(8,128)(2,1)S(1)} %get-tuple-element.19), channel_id=1, source_target_pairs={{2,0},{4,2},{6,4},{8,6},{10,8},{12,10},{14,12},{16,14},{18,16},{20... | collective-permute-start | bytes 98312 | tf_op jit(solution)/shard_map/ppermute | solution.py:215
  64.2 3.5 %edge_local.2.pre = f32[256,12288]{1,0:T(8,128)S(1)} custom-call(s32[1,12288]{1,0:T(1,128)S(1)} %or_select_fusion.source, s32[1,12288]{1,0:T(1,128)S(1)} %copy-done.9, bf16[256,256]{1,0:T(8,128)(2,1)S(1)} %get-tuple-element.16.sender, bf16[256,256]{1,0:T(8,128)(2,1)S(1)} %get-tuple-element.17.receiver), custom_call_target="tpu_custom_call" | custom-call | flops 3221225472 | bytes 1048576 | tf_op jit(solution)/shard_map/edge_local/pallas_call | solution.py:216
  67.7 0.0 collective-permute-done.4.lower
  67.7 0.0 collective-permute-done.5.upper
  67.7 3.8 %edge_halo.2.mine = bf16[256,256]{1,0:T(8,128)(2,1)S(1)} custom-call(s32[1,12288]{1,0:T(1,128)S(1)} %or_select_fusion.source, s32[1,12288]{1,0:T(1,128)S(1)} %copy-done.9, f32[256,12288]{1,0:T(8,128)S(1)} %edge_local.2.pre, bf16[64,256]{1,0:T(8,128)(2,1)S(1)} %collective-permute-done.4.lower, bf16[64,256]{1,0:T(8,128)(2,1)S(1)} %collective-permute-done.5.upper), custom_call_target="tpu_custom_call" | custom-call | flops 2415919104 | bytes 1048576 | tf_op jit(solution)/shard_map/edge_halo/pallas_call | solution.py:223
  71.6 0.7 collective-permute-start.6
  72.3 1.0 %collective-permute-done.6.other = bf16[256,256]{1,0:T(8,128)(2,1)S(1)} collective-permute-done((bf16[256,256]{1,0:T(8,128)(2,1)S(1)}, bf16[256,256]{1,0:T(8,128)(2,1)S(1)}, u32[]{:S(2)}, u32[]{:S(2)}) %collective-permute-start.6) | collective-permute-done | bytes 131104 | tf_op jit(solution)/shard_map/ppermute | solution.py:117
  73.3 0.0 copy-done.3
  73.3 1.1 %node.9 = (bf16[256,512]{1,0:T(8,128)(2,1)S(1)}, bf16[256,256]{1,0:T(8,128)(2,1)S(1)}, bf16[256,256]{1,0:T(8,128)(2,1)S(1)}, bf16[64,256]{1,0:T(8,128)(2,1)S(1)}, bf16[64,256]{1,0:T(8,128)(2,1)S(1)}) custom-call(s32[1]{0:T(128)} %bitcast.core, bf16[256,512]{1,0:T(8,128)(2,1)S(1)} %get-tuple-element.15.state, bf16[256,256]{1,0:T(8,128)(2,1)S(1)} %edge_halo.2.mine, ...), custom_call_target="tpu_custom_call" | custom-call | flops 402653184 | bytes 1048576 | tf_op jit(solution)/shard_map/node/pallas_call | solution.py:201
  74.3 0.1 collective-permute-start.7
  74.4 6.9 %collective-permute-start.8 = (bf16[64,256]{1,0:T(8,128)(2,1)S(1)}, bf16[64,256]{1,0:T(8,128)(2,1)S(1)}, u32[]{:S(2)}, u32[]{:S(2)}) collective-permute-start(bf16[64,256]{1,0:T(8,128)(2,1)S(1)} %get-tuple-element.24), channel_id=1, source_target_pairs={{2,0},{4,2},{6,4},{8,6},{10,8},{12,10},{14,12},{16,14},{18,16},{20... | collective-permute-start | bytes 98312 | tf_op jit(solution)/shard_map/ppermute | solution.py:215
  81.3 3.5 %edge_local.3.pre = f32[256,12288]{1,0:T(8,128)S(1)} custom-call(s32[1,12288]{1,0:T(1,128)S(1)} %or_select_fusion.source, s32[1,12288]{1,0:T(1,128)S(1)} %copy-done.9, bf16[256,256]{1,0:T(8,128)(2,1)S(1)} %get-tuple-element.21.sender, bf16[256,256]{1,0:T(8,128)(2,1)S(1)} %get-tuple-element.22.receiver), custom_call_target="tpu_custom_call" | custom-call | flops 3221225472 | bytes 1048576 | tf_op jit(solution)/shard_map/edge_local/pallas_call | solution.py:216
  84.8 0.0 collective-permute-done.7.lower
  84.8 0.0 collective-permute-done.8.upper
  84.8 3.9 %edge_halo.3.mine = bf16[256,256]{1,0:T(8,128)(2,1)S(1)} custom-call(s32[1,12288]{1,0:T(1,128)S(1)} %or_select_fusion.source, s32[1,12288]{1,0:T(1,128)S(1)} %copy-done.9, f32[256,12288]{1,0:T(8,128)S(1)} %edge_local.3.pre, bf16[64,256]{1,0:T(8,128)(2,1)S(1)} %collective-permute-done.7.lower, bf16[64,256]{1,0:T(8,128)(2,1)S(1)} %collective-permute-done.8.upper), custom_call_target="tpu_custom_call" | custom-call | flops 2415919104 | bytes 1048576 | tf_op jit(solution)/shard_map/edge_halo/pallas_call | solution.py:223
  88.7 1.0 %collective-permute-start.9 = (bf16[256,256]{1,0:T(8,128)(2,1)S(1)}, bf16[256,256]{1,0:T(8,128)(2,1)S(1)}, u32[]{:S(2)}, u32[]{:S(2)}) collective-permute-start(bf16[256,256]{1,0:T(8,128)(2,1)S(1)} %edge_halo.3.mine), channel_id=1, source_target_pairs={{0,1},{1,0},{2,3},{3,2},{4,5},{5,4},{6,7},{7,6},{8,9},{9,8},{10,11... | collective-permute-start | bytes 393224 | tf_op jit(solution)/shard_map/ppermute | solution.py:117
  89.6 1.0 %collective-permute-done.9.other = bf16[256,256]{1,0:T(8,128)(2,1)S(1)} collective-permute-done((bf16[256,256]{1,0:T(8,128)(2,1)S(1)}, bf16[256,256]{1,0:T(8,128)(2,1)S(1)}, u32[]{:S(2)}, u32[]{:S(2)}) %collective-permute-start.9) | collective-permute-done | bytes 131104 | tf_op jit(solution)/shard_map/ppermute | solution.py:117
  90.6 0.0 copy-done.8
  90.6 1.4 %node_last.1 = bf16[256,256]{1,0:T(8,128)(2,1)} custom-call(s32[1]{0:T(128)} %bitcast.core, bf16[256,512]{1,0:T(8,128)(2,1)S(1)} %get-tuple-element.20.state, bf16[256,256]{1,0:T(8,128)(2,1)S(1)} %edge_halo.3.mine, bf16[256,256]{1,0:T(8,128)(2,1)S(1)} %collective-permute-done.9.other, bf16[1024,256]{1,0:T(8,128)(2,1)S(1)} %get-tuple-element.28.in_mine, ...), custom_call_target="tpu_custom_call" | custom-call | flops 402653184 | bytes 1048576 | tf_op jit(solution)/shard_map/node_last/pallas_call | solution.py:192
  (23 shorter events, 0.1 us)
Async XLA Ops:
  0.0 3.4 %copy-start = (bf16[1024,512]{1,0:T(8,128)(2,1)S(1)}, bf16[1024,512]{1,0:T(8,128)(2,1)}, u32[]{:S(2)}) copy-start(bf16[1024,512]{1,0:T(8,128)(2,1)} %param.16) | copy-start | bytes 3145732
  0.0 28.5 %collective-permute-start.2 = (bf16[3,256]{1,0:T(4,128)(2,1)}, bf16[3,256]{1,0:T(4,128)(2,1)}, u32[]{:S(2)}, u32[]{:S(2)}) collective-permute-start(bf16[3,256]{1,0:T(4,128)(2,1)} %param.30), channel_id=1, source_target_pairs={{0,1},{1,0},{2,3},{3,2},{4,5},{5,4},{6,7},{7,6},{8,9},{9,8},{10,11... | collective-permute-start | bytes 4616 | tf_op jit(solution)/shard_map/ppermute | solution.py:117
  1.4 27.9 %collective-permute-start.3 = (bf16[3,256,512]{2,1,0:T(8,128)(2,1)}, bf16[3,256,512]{2,1,0:T(8,128)(2,1)}, u32[]{:S(2)}, u32[]{:S(2)}) collective-permute-start(bf16[3,256,512]{2,1,0:T(8,128)(2,1)} %param.31), channel_id=1, source_target_pairs={{0,1},{1,0},{2,3},{3,2},{4,5},{5,4},{6,7},{7,6},{8,9},{9,8},{10,11... | collective-permute-start | bytes 2359304 | tf_op jit(solution)/shard_map/ppermute | solution.py:117
  1.4 53.2 %collective-permute-start.1 = (bf16[3,1024,256]{2,1,0:T(8,128)(2,1)}, bf16[3,1024,256]{2,1,0:T(8,128)(2,1)}, u32[]{:S(2)}, u32[]{:S(2)}) collective-permute-start(bf16[3,1024,256]{2,1,0:T(8,128)(2,1)} %param.29), channel_id=1, source_target_pairs={{0,1},{1,0},{2,3},{3,2},{4,5},{5,4},{6,7},{7,6},{8,9},{9,8},{10,11... | collective-permute-start | bytes 4718600 | tf_op jit(solution)/shard_map/ppermute | solution.py:117
  9.6 11.7 %copy-start.14 = (s32[1,12288]{1,0:T(1,128)S(1)}, s32[1,12288]{1,0:T(1,128)}, u32[]{:S(2)}) copy-start(s32[1,12288]{1,0:T(1,128)} %param.23) | copy-start | bytes 147460
  9.6 11.9 %copy-start.19 = (s32[1,2,64]{2,1,0:T(2,128)S(1)}, s32[1,2,64]{2,1,0:T(2,128)}, u32[]{:S(2)}) copy-start(s32[1,2,64]{2,1,0:T(2,128)} %param.25) | copy-start | bytes 1540
  9.6 12.0 %copy-start.10 = (bf16[3,256,512]{2,1,0:T(8,128)(2,1)S(1)}, bf16[3,256,512]{2,1,0:T(8,128)(2,1)}, u32[]{:S(2)}) copy-start(bf16[3,256,512]{2,1,0:T(8,128)(2,1)} %param.31) | copy-start | bytes 2359300
  9.6 12.9 %copy-start.11 = (bf16[2,512,256]{2,1,0:T(8,128)(2,1)S(1)}, bf16[2,512,256]{2,1,0:T(8,128)(2,1)}, u32[]{:S(2)}) copy-start(bf16[2,512,256]{2,1,0:T(8,128)(2,1)} %param.27) | copy-start | bytes 1572868
  9.6 12.9 %copy-start.12 = (bf16[2,512,256]{2,1,0:T(8,128)(2,1)S(1)}, bf16[2,512,256]{2,1,0:T(8,128)(2,1)}, u32[]{:S(2)}) copy-start(bf16[2,512,256]{2,1,0:T(8,128)(2,1)} %param.26) | copy-start | bytes 1572868
  9.6 41.0 %all-to-all-start = ((bf16[64,64,256]{2,1,0:T(8,128)(2,1)}), bf16[64,64,256]{2,1,0:T(8,128)(2,1)}, u32[]{:S(2)}, u32[]{:S(2)}) async-start(bf16[64,64,256]{2,1,0:T(8,128)(2,1)} %bitcast.1), calls=%async_computation | async-start | bytes 4194304 | tf_op jit(solution)/shard_map/all_to_all | solution.py:151
  21.3 2.3 %copy-start.17 = (bf16[3,256]{1,0:T(4,128)(2,1)S(1)}, bf16[3,256]{1,0:T(4,128)(2,1)}, u32[]{:S(2)}) copy-start(bf16[3,256]{1,0:T(4,128)(2,1)} %param.30) | copy-start | bytes 4612
  21.3 2.3 %copy-start.18 = (bf16[2,256]{1,0:T(2,128)(2,1)S(1)}, bf16[2,256]{1,0:T(2,128)(2,1)}, u32[]{:S(2)}) copy-start(bf16[2,256]{1,0:T(2,128)(2,1)} %param.28) | copy-start | bytes 3076
  23.6 1.6 %copy-start.13 = (bf16[256,256]{1,0:T(8,128)(2,1)S(1)}, bf16[256,256]{1,0:T(8,128)(2,1)}, u32[]{:S(2)}) copy-start(bf16[256,256]{1,0:T(8,128)(2,1)} %param.17) | copy-start | bytes 393220
  23.6 3.6 %copy-start.16 = (bf16[1,64,64]{2,1,0:T(8,128)(2,1)S(1)}, bf16[1,64,64]{2,1,0:T(8,128)(2,1)}, u32[]{:S(2)}) copy-start(bf16[1,64,64]{2,1,0:T(8,128)(2,1)} %param.22) | copy-start | bytes 24580
  23.6 4.2 %copy-start.15 = (s32[1,64,64]{2,1,0:T(8,128)S(1)}, s32[1,64,64]{2,1,0:T(8,128)}, u32[]{:S(2)}) copy-start(s32[1,64,64]{2,1,0:T(8,128)} %param.21) | copy-start | bytes 49156
  52.9 3.2 %copy-start.1 = (bf16[256,512]{1,0:T(8,128)(2,1)S(1)}, bf16[256,512]{1,0:T(8,128)(2,1)}, u32[]{:S(2)}) copy-start(bf16[256,512]{1,0:T(8,128)(2,1)} %get-tuple-element.35.out_mine) | copy-start | bytes 786436
  53.0 3.2 %copy-start.2 = (bf16[256,512]{1,0:T(8,128)(2,1)S(1)}, bf16[256,512]{1,0:T(8,128)(2,1)}, u32[]{:S(2)}) copy-start(bf16[256,512]{1,0:T(8,128)(2,1)} %get-tuple-element.33.out_other) | copy-start | bytes 786436
  53.0 3.2 %copy-start.5 = (bf16[512,256]{1,0:T(8,128)(2,1)S(1)}, bf16[512,256]{1,0:T(8,128)(2,1)}, u32[]{:S(2)}) copy-start(bf16[512,256]{1,0:T(8,128)(2,1)} %get-tuple-element.38.recv_w) | copy-start | bytes 786436
  53.0 3.2 %copy-start.6 = (bf16[512,256]{1,0:T(8,128)(2,1)S(1)}, bf16[512,256]{1,0:T(8,128)(2,1)}, u32[]{:S(2)}) copy-start(bf16[512,256]{1,0:T(8,128)(2,1)} %get-tuple-element.49.send_w) | copy-start | bytes 786436
  53.0 3.1 %collective-permute-start = (bf16[256,256]{1,0:T(8,128)(2,1)S(1)}, bf16[256,256]{1,0:T(8,128)(2,1)S(1)}, u32[]{:S(2)}, u32[]{:S(2)}) collective-permute-start(bf16[256,256]{1,0:T(8,128)(2,1)S(1)} %fusion.9.mine), channel_id=1, source_target_pairs={{0,1},{1,0},{2,3},{3,2},{4,5},{5,4},{6,7},{7,6},{8,9},{9,8},{10,11... | collective-permute-start | bytes 393224 | tf_op jit(solution)/shard_map/ppermute | solution.py:117
  56.1 8.1 %copy-start.9 = (s32[1,12288]{1,0:T(1,128)S(1)}, s32[1,12288]{1,0:T(1,128)}, u32[]{:S(2)}) copy-start(s32[1,12288]{1,0:T(1,128)} %node.11) | copy-start | bytes 147460
  57.2 10.5 %collective-permute-start.4 = (bf16[64,256]{1,0:T(8,128)(2,1)S(1)}, bf16[64,256]{1,0:T(8,128)(2,1)S(1)}, u32[]{:S(2)}, u32[]{:S(2)}) collective-permute-start(bf16[64,256]{1,0:T(8,128)(2,1)S(1)} %get-tuple-element.18), channel_id=1, source_target_pairs={{0,2},{2,4},{4,6},{6,8},{8,10},{10,12},{12,14},{14,16},{16,18},{18... | collective-permute-start | bytes 98312 | tf_op jit(solution)/shard_map/ppermute | solution.py:214
  57.6 10.1 %collective-permute-start.5 = (bf16[64,256]{1,0:T(8,128)(2,1)S(1)}, bf16[64,256]{1,0:T(8,128)(2,1)S(1)}, u32[]{:S(2)}, u32[]{:S(2)}) collective-permute-start(bf16[64,256]{1,0:T(8,128)(2,1)S(1)} %get-tuple-element.19), channel_id=1, source_target_pairs={{2,0},{4,2},{6,4},{8,6},{10,8},{12,10},{14,12},{16,14},{18,16},{20... | collective-permute-start | bytes 98312 | tf_op jit(solution)/shard_map/ppermute | solution.py:215
  67.7 5.6 %copy-start.3 = (bf16[512,256]{1,0:T(8,128)(2,1)S(1)}, bf16[512,256]{1,0:T(8,128)(2,1)}, u32[]{:S(2)}) copy-start(bf16[512,256]{1,0:T(8,128)(2,1)} %get-tuple-element.37.recv_w) | copy-start | bytes 786436
  67.7 5.6 %copy-start.4 = (bf16[512,256]{1,0:T(8,128)(2,1)S(1)}, bf16[512,256]{1,0:T(8,128)(2,1)}, u32[]{:S(2)}) copy-start(bf16[512,256]{1,0:T(8,128)(2,1)} %get-tuple-element.50.send_w) | copy-start | bytes 786436
  71.6 1.7 %collective-permute-start.6 = (bf16[256,256]{1,0:T(8,128)(2,1)S(1)}, bf16[256,256]{1,0:T(8,128)(2,1)S(1)}, u32[]{:S(2)}, u32[]{:S(2)}) collective-permute-start(bf16[256,256]{1,0:T(8,128)(2,1)S(1)} %edge_halo.2.mine), channel_id=1, source_target_pairs={{0,1},{1,0},{2,3},{3,2},{4,5},{5,4},{6,7},{7,6},{8,9},{9,8},{10,11... | collective-permute-start | bytes 393224 | tf_op jit(solution)/shard_map/ppermute | solution.py:117
  74.3 10.4 %collective-permute-start.7 = (bf16[64,256]{1,0:T(8,128)(2,1)S(1)}, bf16[64,256]{1,0:T(8,128)(2,1)S(1)}, u32[]{:S(2)}, u32[]{:S(2)}) collective-permute-start(bf16[64,256]{1,0:T(8,128)(2,1)S(1)} %get-tuple-element.23), channel_id=1, source_target_pairs={{0,2},{2,4},{4,6},{6,8},{8,10},{10,12},{12,14},{14,16},{16,18},{18... | collective-permute-start | bytes 98312 | tf_op jit(solution)/shard_map/ppermute | solution.py:214
  74.4 10.4 %collective-permute-start.8 = (bf16[64,256]{1,0:T(8,128)(2,1)S(1)}, bf16[64,256]{1,0:T(8,128)(2,1)S(1)}, u32[]{:S(2)}, u32[]{:S(2)}) collective-permute-start(bf16[64,256]{1,0:T(8,128)(2,1)S(1)} %get-tuple-element.24), channel_id=1, source_target_pairs={{2,0},{4,2},{6,4},{8,6},{10,8},{12,10},{14,12},{16,14},{18,16},{20... | collective-permute-start | bytes 98312 | tf_op jit(solution)/shard_map/ppermute | solution.py:215
  84.8 5.9 %copy-start.7 = (bf16[256,512]{1,0:T(8,128)(2,1)S(1)}, bf16[256,512]{1,0:T(8,128)(2,1)}, u32[]{:S(2)}) copy-start(bf16[256,512]{1,0:T(8,128)(2,1)} %get-tuple-element.34.out_mine) | copy-start | bytes 786436
  84.8 5.9 %copy-start.8 = (bf16[256,512]{1,0:T(8,128)(2,1)S(1)}, bf16[256,512]{1,0:T(8,128)(2,1)}, u32[]{:S(2)}) copy-start(bf16[256,512]{1,0:T(8,128)(2,1)} %get-tuple-element.31.out_other) | copy-start | bytes 786436
  88.7 2.0 %collective-permute-start.9 = (bf16[256,256]{1,0:T(8,128)(2,1)S(1)}, bf16[256,256]{1,0:T(8,128)(2,1)S(1)}, u32[]{:S(2)}, u32[]{:S(2)}) collective-permute-start(bf16[256,256]{1,0:T(8,128)(2,1)S(1)} %edge_halo.3.mine), channel_id=1, source_target_pairs={{0,1},{1,0},{2,3},{3,2},{4,5},{5,4},{6,7},{7,6},{8,9},{9,8},{10,11... | collective-permute-start | bytes 393224 | tf_op jit(solution)/shard_map/ppermute | solution.py:117

commit v3 on v2

v3 whole, which is shorter than its diff:
```python
import functools

import jax
import jax.numpy as jnp
from jax import lax
from jax.experimental import pallas as pl
from jax.experimental.pallas import tpu as pltpu
from jax.sharding import PartitionSpec as P

VMEM = pl.BlockSpec(memory_space=pltpu.VMEM)
SMEM = pl.BlockSpec(memory_space=pltpu.SMEM)
HBM = pl.BlockSpec(memory_space=pltpu.HBM)
F32 = jnp.float32
BF16 = jnp.bfloat16


def dot32(a, b):
    return jnp.dot(a, b, preferred_element_type=F32)


def dot32_nt(a, b):
    return lax.dot_general(a, b, (((1,), (1,)), ((), ())), preferred_element_type=F32)


def silu(v):
    half = 0.5 * v
    return half + half * jnp.tanh(half)


def one_hot_columns(row, count):
    ids = lax.broadcasted_iota(jnp.int32, (count, row.shape[1]), 0).astype(jnp.int16)
    return jnp.where(ids == row.astype(jnp.int16), jnp.ones((), BF16), jnp.zeros((), BF16))


def call(kernel, name, out_shape, in_specs, flops, out_specs=None, limit=24, scratch=()):
    many = isinstance(out_shape, tuple)
    return pl.pallas_call(
        kernel,
        name=name,
        out_shape=out_shape,
        in_specs=in_specs,
        out_specs=out_specs or ((VMEM,) * len(out_shape) if many else VMEM),
        scratch_shapes=scratch,
        compiler_params=pltpu.CompilerParams(vmem_limit_bytes=limit * 2**20),
        cost_estimate=pl.CostEstimate(flops=flops, bytes_accessed=2**20, transcendentals=0),
    )


def embed_kernel(grid, weights, bias, source, rows_out, grid_in, weights_in, source_in, rows, sems):
    fetch = [
        pltpu.make_async_copy(grid, grid_in, sems.at[0]),
        pltpu.make_async_copy(weights, weights_in, sems.at[1]),
        pltpu.make_async_copy(source, source_in, sems.at[2]),
    ]
    for copy in fetch:
        copy.start()
    for copy in fetch:
        copy.wait()
    bands, slots, _ = rows_out.shape
    count = grid.shape[0]
    add = bias[...].astype(F32).reshape(1, bias.shape[0])
    embedding = silu(dot32(grid_in[...], weights_in[...]) + add).astype(BF16)
    columns = source_in[0].T
    ids = lax.broadcasted_iota(jnp.int32, (slots, count), 1)
    group = 8 if bands % 8 == 0 else 1
    leave = []
    for first in range(0, bands, group):
        chosen = [
            jnp.where(ids == columns[:, band : band + 1], jnp.ones((), BF16), jnp.zeros((), BF16))
            for band in range(first, first + group)
        ]
        part = dot32(jnp.concatenate(chosen, 0), embedding).astype(BF16)
        rows[first : first + group] = part.reshape(group, slots, part.shape[1])
        copy = pltpu.make_async_copy(
            rows.at[pl.ds(first, group)],
            rows_out.at[pl.ds(first, group)],
            sems.at[3 + first // group],
        )
        copy.start()
        leave.append(copy)
    for copy in leave:
        copy.wait()


def slots_kernel(node, weight, rows, aggregate):
    ids = lax.broadcasted_iota(jnp.int32, (aggregate.shape[0], node.shape[1]), 0)
    chosen = ids.astype(jnp.int16) == node[...].astype(jnp.int16)
    matrix = jnp.where(chosen, weight[...], jnp.zeros((), BF16))
    aggregate[...] = dot32(matrix, rows[...]).astype(BF16)


def node_hidden(core, state, mine, other, in_mine, in_other, bias_mine, bias_other):
    wide = state.shape[1]
    first = core == 0
    low = jnp.where(first, mine[...], other[...])
    high = jnp.where(first, other[...], mine[...])
    inputs = jnp.concatenate([state[...], low, high], 1)
    hidden_mine = silu(dot32(inputs, in_mine[...]) + bias_mine[...]).astype(BF16)
    hidden_other = silu(dot32(inputs, in_other[...]) + bias_other[...]).astype(BF16)
    return hidden_mine, hidden_other


def node_kernel(
    core, state, mine, other, in_mine, in_other, bias_mine, bias_other, out_mine, out_other,
    send_w, recv_w, edge_bias, halo_hot, state_out, sender_out, receiver_out, one_out, two_out,
):
    hidden_mine, hidden_other = node_hidden(
        core[0], state, mine, other, in_mine, in_other, bias_mine, bias_other
    )
    update = dot32(hidden_mine, out_mine[...]) + dot32(hidden_other, out_other[...])
    after = (state[...].astype(F32) + update).astype(BF16)
    state_out[...] = after
    sender = (dot32(after, send_w[...]) + edge_bias[...]).astype(BF16)
    sender_out[...] = sender
    receiver_out[...] = dot32(after, recv_w[...]).astype(BF16)
    leaving = dot32(halo_hot[...], sender).astype(BF16)
    width = one_out.shape[0]
    one_out[...] = leaving[:width]
    two_out[...] = leaving[width:]


def last_kernel(
    core, state, mine, other, in_mine, in_other, bias_mine, bias_other, out_mine, out_other, result
):
    hidden_mine, hidden_other = node_hidden(
        core[0], state, mine, other, in_mine, in_other, bias_mine, bias_other
    )
    first = core[0] == 0
    narrow = result.shape[1]

    def mine_of(ref):
        return jnp.where(first, ref[:, :narrow], ref[:, narrow:])

    update = dot32(hidden_mine, mine_of(out_mine)) + dot32(hidden_other, mine_of(out_other))
    result[...] = (mine_of(state).astype(F32) + update).astype(BF16)


def local_kernel(source, node, sender, receiver, pre):
    nodes = sender.shape[0]
    table = jnp.concatenate([sender[...].T, receiver[...].T], 1)
    chosen = jnp.concatenate(
        [one_hot_columns(source[...], nodes), one_hot_columns(node[...], nodes)], 0
    )
    pre[...] = dot32(table, chosen)


def halo_kernel(source, node, pre, one, two, aggregate):
    nodes = aggregate.shape[0]
    table = jnp.concatenate([one[...], two[...]], 0).T
    chosen = one_hot_columns(source[...] - nodes, table.shape[1])
    messages = silu(pre[...] + dot32(table, chosen)).astype(BF16)
    aggregate[...] = dot32_nt(one_hot_columns(node[...], nodes), messages).astype(BF16)


def swap_cores(value):
    return lax.ppermute(value, "feat", [(0, 1), (1, 0)])


def body(
    grid_latent,
    mesh_latent,
    grid_in_w,
    grid_bias,
    g2m_src,
    g2m_dst,
    g2m_weight,
    mesh_src,
    mesh_dst,
    halo_index,
    edge_send_w,
    edge_recv_w,
    edge_bias,
    node_in_w,
    node_bias,
    node_out_w,
):
    feature_width = grid_in_w.shape[1]
    nodes = mesh_latent.shape[0]
    edges = mesh_src.shape[1]
    halo = halo_index.shape[2]
    partitions = lax.axis_size("band")
    core = lax.axis_index("feat").astype(jnp.int32).reshape(1)
    part = lax.axis_index("band")
    band_count = g2m_src.shape[1]
    slot_count = g2m_src.shape[2]
    slots = band_count * slot_count
    outgoing_shape = (band_count, slot_count, feature_width)
    outgoing = call(
        embed_kernel,
        "embed",
        jax.ShapeDtypeStruct(outgoing_shape, BF16),
        [HBM, HBM, VMEM, HBM],
        2 * slots * grid_latent.shape[0] * feature_width,
        HBM,
        60,
        [
            pltpu.VMEM(grid_latent.shape, BF16),
            pltpu.VMEM(grid_in_w.shape, BF16),
            pltpu.VMEM(g2m_src.shape, jnp.int32),
            pltpu.VMEM(outgoing_shape, BF16),
            pltpu.SemaphoreType.DMA((3 + band_count,)),
        ],
    )(grid_latent, grid_in_w, grid_bias, g2m_src)
    incoming = lax.all_to_all(outgoing, "band", split_axis=0, concat_axis=0, tiled=True)

    _, latent, in_mine, bias_mine, out_mine = lax.optimization_barrier(
        (outgoing, mesh_latent, node_in_w, node_bias, node_out_w)
    )
    layers, deep, _ = node_in_w.shape
    wide = node_out_w.shape[2]
    state = lax.all_gather(latent, "feat", axis=1, tiled=True)
    in_other, bias_other, out_other = swap_cores(in_mine), swap_cores(bias_mine), swap_cores(out_mine)
    node_w = [
        (
            in_mine[layer],
            in_other[layer],
            bias_mine[layer].astype(F32)[None],
            bias_other[layer].astype(F32)[None],
            out_mine[layer],
            out_other[layer],
        )
        for layer in range(layers)
    ]
    edge_w = [
        (edge_send_w[step], edge_recv_w[step], edge_bias[step].astype(F32)[None])
        for step in range(layers - 1)
    ]
    even = part % 2 == 0
    to_next, to_previous = halo_index[0, 0], halo_index[0, 1]
    leaving = jnp.concatenate(
        [jnp.where(even, to_next, to_previous), jnp.where(even, to_previous, to_next)]
    )
    halo_ids = lax.broadcasted_iota(jnp.int32, (2 * halo, nodes), 1)
    halo_hot = (leaving[:, None] == halo_ids).astype(BF16)
    from_previous = (mesh_src >= nodes) & (mesh_src < nodes + halo)
    from_next = mesh_src >= nodes + halo
    source = mesh_src + jnp.where(
        even & from_previous, halo, jnp.where(even & from_next, -halo, 0)
    )
    outside = (from_previous & (part == 0)) | (from_next & (part == partitions - 1))
    source = jnp.where(outside, -1, source)
    slot_node, slot_weight = g2m_dst.reshape(1, slots), g2m_weight.reshape(1, slots)
    incoming, core, state, node_w, edge_w, halo_hot, source, slot_node, slot_weight = (
        lax.optimization_barrier(
            (incoming, core, state, node_w, edge_w, halo_hot, source, slot_node, slot_weight)
        )
    )
    half = jax.ShapeDtypeStruct((nodes, feature_width), BF16)
    aggregate = call(
        slots_kernel,
        "slots",
        half,
        [VMEM] * 3,
        2 * slots * nodes * feature_width,
    )(slot_node, slot_weight, incoming.reshape(slots, -1))

    pairs_one = [(i, i ^ 1) if i ^ 1 < partitions else (i, i) for i in range(partitions)]
    pairs_two = [
        (i, ((i - 1) ^ 1) + 1) if 0 < i and ((i - 1) ^ 1) + 1 < partitions else (i, i)
        for i in range(partitions)
    ]
    halo_rows = jax.ShapeDtypeStruct((halo, feature_width), BF16)
    node_flops = 2 * nodes * wide * (deep + wide)
    for layer in range(layers):
        operands = (core, state, aggregate, swap_cores(aggregate), *node_w[layer])
        if layer + 1 == layers:
            return call(last_kernel, "node_last", half, [SMEM] + [VMEM] * 9, node_flops)(*operands)
        state, sender, receiver, leaving_one, leaving_two = call(
            node_kernel,
            "node",
            (jax.ShapeDtypeStruct((nodes, wide), BF16), half, half, halo_rows, halo_rows),
            [SMEM] + [VMEM] * 13,
            node_flops,
        )(*operands, *edge_w[layer], halo_hot)
        arrived_one = lax.ppermute(leaving_one, "band", pairs_one)
        arrived_two = lax.ppermute(leaving_two, "band", pairs_two)
        pre = call(
            local_kernel,
            "edge_local",
            pltpu.VMEM((feature_width, edges), F32),
            [VMEM] * 4,
            4 * edges * nodes * feature_width,
        )(source, mesh_dst, sender, receiver)
        aggregate = call(
            halo_kernel,
            "edge_halo",
            half,
            [VMEM] * 5,
            3 * edges * nodes * feature_width,
        )(source, mesh_dst, pre, arrived_one, arrived_two)


def solution(mesh):
    in_specs = (
        P("band", None),
        P("band", "feat"),
        P(None, "feat"),
        P("feat"),
        P("band", None, None),
        P("band", None, None),
        P("band", None, None),
        P("band", None),
        P("band", None),
        P("band", None, None),
        P(None, None, "feat"),
        P(None, None, "feat"),
        P(None, "feat"),
        P(None, None, "feat"),
        P(None, "feat"),
        P(None, "feat", None),
    )
    out_specs = P("band", "feat")
    return jax.shard_map(body, mesh=mesh, in_specs=in_specs, out_specs=out_specs, check_vma=False)
```

time: 92.5 us -> 84 us (0.908)
  the two profiles are of different devices: /device:TPU:1 before, /device:TPU:33 now
where the time goes in v3:
time: 84 us; the launch traced here: 83.6 us
  starting transfers between devices  28.7 us (34%)
  Pallas kernels  24.9 us (30%)
  waiting for transfers between devices  15.3 us (18%)
  local copies, waits for them, and re-layouts  9.02 us (11%)
  other arithmetic  3.18 us (4%)
  blocking collectives  1.98 us (2%)
    all_to_all x1, waiting for transfers between devices, body(): lax.all_to_all(outgoing, 'band', split_axis=0, concat_axis=0, tiled=True)  11.2 us
    all_to_all x1, starting transfers between devices, body(): lax.all_to_all(outgoing, 'band', split_axis=0, concat_axis=0, tiled=True)  10.7 us
    ppermute x2, starting transfers between devices, body(): arrived_two = lax.ppermute(leaving_two, 'band', pairs_two)  9.49 us
    ppermute x6, starting transfers between devices, swap_cores(): return lax.ppermute(value, 'feat', [(0, 1), (1, 0)])  8.11 us
    pallas_call x2, Pallas kernels, body(): call(halo_kernel, 'edge_halo', half, [VMEM] * 5, 3 * edges * nodes * feat...  7.66 us
    pallas_call x2, Pallas kernels, body(): call(local_kernel, 'edge_local', pltpu.VMEM((feature_width, edges), F32),...  6.91 us
    pallas_call x1, Pallas kernels, body(): call(embed_kernel, 'embed', jax.ShapeDtypeStruct(outgoing_shape, BF16), [...  6.11 us
    ppermute x6, waiting for transfers between devices, swap_cores(): return lax.ppermute(value, 'feat', [(0, 1), (1, 0)])  2.97 us
  transfers between devices with their start and end apart: 11, of which 6 were waited for; matrix products, arithmetic and copies ran while one was open for 14% of the time, Pallas kernels for 8%

profile of v3, /device:TPU:33, one launch (start us, length us, event | category | flops | bytes accessed | tf_op | source)
XLA Modules:
  0.0 83.6 jit_solution(2899644326166006238)
XLA Ops:
  0.0 6.1 %embed.1 = bf16[64,64,256]{2,1,0:T(8,128)(2,1)} custom-call(bf16[1024,512]{1,0:T(8,128)(2,1)} %grid.1, bf16[512,256]{1,0:T(8,128)(2,1)} %weights.1, bf16[256]{0:T(256)(128)(2,1)} %bias.1, s32[1,64,64]{2,1,0:T(8,128)} %source.1), custom_call_target="tpu_custom_call" | custom-call | flops 2147483648 | bytes 1048576 | tf_op jit(solution)/shard_map/embed/pallas_call | solution.py:188
  6.1 0.0 copy-start.31
  6.1 0.0 copy-start.27
  6.1 0.0 copy-start.24
  6.2 0.0 copy-start.25
  6.2 10.7 %all-to-all-start = ((bf16[64,64,256]{2,1,0:T(8,128)(2,1)}), bf16[64,64,256]{2,1,0:T(8,128)(2,1)S(1)}, u32[]{:S(2)}, u32[]{:S(2)}) async-start(bf16[64,64,256]{2,1,0:T(8,128)(2,1)} %embed.1), calls=%async_computation | async-start | bytes 4194304 | tf_op jit(solution)/shard_map/all_to_all | solution.py:204
  16.8 0.0 copy-start.30
  16.8 1.3 %collective-permute-start.1 = (bf16[3,256]{1,0:T(4,128)(2,1)}, bf16[3,256]{1,0:T(4,128)(2,1)}, u32[]{:S(2)}, u32[]{:S(2)}) collective-permute-start(bf16[3,256]{1,0:T(4,128)(2,1)} %param.30), channel_id=1, source_target_pairs={{0,1},{1,0},{2,3},{3,2},{4,5},{5,4},{6,7},{7,6},{8,9},{9,8},{10,11... | collective-permute-start | bytes 4616 | tf_op jit(solution)/shard_map/ppermute | solution.py:156
  18.2 0.1 collective-permute-start.2
  18.3 0.4 collective-permute-start
  18.7 0.0 copy-done.31
  18.7 0.0 copy-done.27
  18.7 0.2 or_select_fusion.source
  18.9 0.1 pad_add_fusion
  19.0 0.1 fusion.halo_hot
  19.1 2.1 %slice_bitcast_fusion.13 = (bf16[256,512]{1,0:T(8,128)(2,1)}, bf16[256,512]{1,0:T(8,128)(2,1)}, bf16[256,512]{1,0:T(8,128)(2,1)}) fusion(bf16[3,256,512]{2,1,0:T(8,128)(2,1)} %param.31), kind=kLoop, calls=%fused_computation.13 | loop fusion | bytes 1572864 | tf_op jit(solution)/shard_map/squeeze | solution.py:219
  21.2 0.0 copy-done.24
  21.2 0.0 copy-done.25
  21.2 1.0 %slice_bitcast_fusion.9 = (bf16[512,256]{1,0:T(8,128)(2,1)}, bf16[512,256]{1,0:T(8,128)(2,1)}, bf16[512,256]{1,0:T(8,128)(2,1)}, bf16[512,256]{1,0:T(8,128)(2,1)}) fusion(bf16[2,512,256]{2,1,0:T(8,128)(2,1)S(1)} %copy-done.24, bf16[2,512,256]{2,1,0:T(8,128)(2,1)S(1)} %copy-done.25), kind=kLoop, calls=%fused_computation.9 | loop fusion | bytes 2097152 | tf_op jit(solution)/shard_map/squeeze | solution.py:225
  22.2 0.0 copy-done.30
  22.2 1.4 %slice_convert_fusion.3 = (f32[1,256]{1,0:T(1,128)}, f32[1,256]{1,0:T(1,128)}, f32[1,256]{1,0:T(1,128)}, f32[1,256]{1,0:T(1,128)}, f32[1,256]{1,0:T(1,128)}) fusion(bf16[2,256]{1,0:T(2,128)(2,1)S(1)} %copy-done.30, bf16[3,256]{1,0:T(4,128)(2,1)} %param.30), kind=kLoop, calls=%fused_computation.26 | loop fusion | flops 1280 | bytes 7680 | tf_op jit(solution)/shard_map/convert_element_type | solution.py:225
  23.6 0.0 copy-done.23
  23.6 1.1 %slice_bitcast_fusion.3 = (bf16[1024,256]{1,0:T(8,128)(2,1)S(1)}, bf16[1024,256]{1,0:T(8,128)(2,1)}, bf16[1024,256]{1,0:T(8,128)(2,1)}) fusion(bf16[3,1024,256]{2,1,0:T(8,128)(2,1)S(1)} %copy-done.23), kind=kLoop, calls=%fused_computation.3 | loop fusion | bytes 3145728 | tf_op jit(solution)/shard_map/squeeze | solution.py:215
  24.7 0.0 copy-done.26
  24.7 2.0 %all_gather.3.state = bf16[256,512]{1,0:T(8,128)(2,1)S(1)} all-gather(bf16[256,256]{1,0:T(8,128)(2,1)S(1)} %copy-done.26), channel_id=1, replica_groups=mesh['band'=64,'feat'=2] {'feat'}, dimensions={1}, use_global_device_ids=true | all-gather | bytes 393216 | tf_op jit(solution)/shard_map/all_gather | solution.py:211
  26.7 0.0 copy-done.28
  26.7 0.1 reshape.18.node
  26.8 0.1 reshape.19.weight
  26.9 0.0 collective-permute-done.1
  26.9 1.4 %slice_convert_fusion = (f32[1,256]{1,0:T(1,128)}, f32[1,256]{1,0:T(1,128)}, f32[1,256]{1,0:T(1,128)}) fusion(bf16[3,256]{1,0:T(4,128)(2,1)} %collective-permute-done.1), kind=kLoop, calls=%fused_computation.23 | loop fusion | flops 768 | bytes 4608 | tf_op jit(solution)/shard_map/convert_element_type | solution.py:218
  28.3 0.0 collective-permute-done.2
  28.3 2.1 %slice_bitcast_fusion.6 = (bf16[256,512]{1,0:T(8,128)(2,1)}, bf16[256,512]{1,0:T(8,128)(2,1)}, bf16[256,512]{1,0:T(8,128)(2,1)}) fusion(bf16[3,256,512]{2,1,0:T(8,128)(2,1)} %collective-permute-done.2), kind=kLoop, calls=%fused_computation.6 | loop fusion | bytes 1572864 | tf_op jit(solution)/shard_map/squeeze | solution.py:220
  30.4 0.0 collective-permute-done
  30.4 2.4 %slice_bitcast_fusion = (bf16[1024,256]{1,0:T(8,128)(2,1)S(1)}, bf16[1024,256]{1,0:T(8,128)(2,1)}, bf16[1024,256]{1,0:T(8,128)(2,1)}) fusion(bf16[3,1024,256]{2,1,0:T(8,128)(2,1)} %collective-permute-done), kind=kLoop, calls=%fused_computation | loop fusion | bytes 3145728 | tf_op jit(solution)/shard_map/squeeze | solution.py:216
  32.8 11.2 %all-to-all-done = bf16[64,64,256]{2,1,0:T(8,128)(2,1)S(1)} async-done(((bf16[64,64,256]{2,1,0:T(8,128)(2,1)}), bf16[64,64,256]{2,1,0:T(8,128)(2,1)S(1)}, u32[]{:S(2)}, u32[]{:S(2)}) %all-to-all-start) | async-done | bytes 2097184 | tf_op jit(solution)/shard_map/all_to_all | solution.py:204
  44.1 0.0 copy-start.14
  44.1 0.7 slots.1.mine
  44.8 2.8 %collective-permute-start.3 = (bf16[256,256]{1,0:T(8,128)(2,1)S(1)}, bf16[256,256]{1,0:T(8,128)(2,1)S(1)}, u32[]{:S(2)}, u32[]{:S(2)}) collective-permute-start(bf16[256,256]{1,0:T(8,128)(2,1)S(1)} %slots.1.mine), channel_id=1, source_target_pairs={{0,1},{1,0},{2,3},{3,2},{4,5},{5,4},{6,7},{7,6},{8,9},{9,8},{10,11... | collective-permute-start | bytes 393224 | tf_op jit(solution)/shard_map/ppermute | solution.py:156
  47.6 1.0 %collective-permute-done.3.other = bf16[256,256]{1,0:T(8,128)(2,1)S(1)} collective-permute-done((bf16[256,256]{1,0:T(8,128)(2,1)S(1)}, bf16[256,256]{1,0:T(8,128)(2,1)S(1)}, u32[]{:S(2)}, u32[]{:S(2)}) %collective-permute-start.3) | collective-permute-done | bytes 131104 | tf_op jit(solution)/shard_map/ppermute | solution.py:156
  48.6 0.0 copy-done.3
  48.7 1.0 %node.6 = (bf16[256,512]{1,0:T(8,128)(2,1)S(1)}, bf16[256,256]{1,0:T(8,128)(2,1)S(1)}, bf16[256,256]{1,0:T(8,128)(2,1)S(1)}, bf16[64,256]{1,0:T(8,128)(2,1)S(1)}, bf16[64,256]{1,0:T(8,128)(2,1)S(1)}) custom-call(s32[1]{0:T(128)} %bitcast.core, bf16[256,512]{1,0:T(8,128)(2,1)S(1)} %all_gather.3.state, bf16[256,256]{1,0:T(8,128)(2,1)S(1)} %slots.1.mine, ...), custom_call_target="tpu_custom_call" | custom-call | flops 402653184 | bytes 1048576 | tf_op jit(solution)/shard_map/node/pallas_call | solution.py:268
  49.7 0.4 collective-permute-start.4
  50.1 4.7 %collective-permute-start.5 = (bf16[64,256]{1,0:T(8,128)(2,1)S(1)}, bf16[64,256]{1,0:T(8,128)(2,1)S(1)}, u32[]{:S(2)}, u32[]{:S(2)}) collective-permute-start(bf16[64,256]{1,0:T(8,128)(2,1)S(1)} %get-tuple-element.74), channel_id=1, source_target_pairs={{0,0},{2,4},{4,2},{6,8},{8,6},{10,12},{12,10},{14,16},{16,14},{18,... | collective-permute-start | bytes 98312 | tf_op jit(solution)/shard_map/ppermute | solution.py:276
  54.8 3.5 %edge_local.2.pre = f32[256,12288]{1,0:T(8,128)S(1)} custom-call(s32[1,12288]{1,0:T(1,128)S(1)} %or_select_fusion.source, s32[1,12288]{1,0:T(1,128)S(1)} %copy-done.14, bf16[256,256]{1,0:T(8,128)(2,1)S(1)} %get-tuple-element.71.sender, bf16[256,256]{1,0:T(8,128)(2,1)S(1)} %get-tuple-element.72.receiver), custom_call_target="tpu_custom_call" | custom-call | flops 3221225472 | bytes 1048576 | tf_op jit(solution)/shard_map/edge_local/pallas_call | solution.py:277
  58.4 0.0 copy-start.16
  58.4 0.0 copy-start.17
  58.4 0.0 copy-start.21
  58.4 0.0 collective-permute-done.4.one
  58.4 0.6 collective-permute-done.5.two
  59.0 3.8 %edge_halo.2.mine = bf16[256,256]{1,0:T(8,128)(2,1)S(1)} custom-call(s32[1,12288]{1,0:T(1,128)S(1)} %or_select_fusion.source, s32[1,12288]{1,0:T(1,128)S(1)} %copy-done.14, f32[256,12288]{1,0:T(8,128)S(1)} %edge_local.2.pre, bf16[64,256]{1,0:T(8,128)(2,1)S(1)} %collective-permute-done.4.one, bf16[64,256]{1,0:T(8,128)(2,1)S(1)} %collective-permute-done.5.two), custom_call_target="tpu_custom_call" | custom-call | flops 2415919104 | bytes 1048576 | tf_op jit(solution)/shard_map/edge_halo/pallas_call | solution.py:284
  62.8 1.9 %collective-permute-start.6 = (bf16[256,256]{1,0:T(8,128)(2,1)S(1)}, bf16[256,256]{1,0:T(8,128)(2,1)S(1)}, u32[]{:S(2)}, u32[]{:S(2)}) collective-permute-start(bf16[256,256]{1,0:T(8,128)(2,1)S(1)} %edge_halo.2.mine), channel_id=1, source_target_pairs={{0,1},{1,0},{2,3},{3,2},{4,5},{5,4},{6,7},{7,6},{8,9},{9,8},{10,11... | collective-permute-start | bytes 393224 | tf_op jit(solution)/shard_map/ppermute | solution.py:156
  64.7 1.0 %collective-permute-done.6.other = bf16[256,256]{1,0:T(8,128)(2,1)S(1)} collective-permute-done((bf16[256,256]{1,0:T(8,128)(2,1)S(1)}, bf16[256,256]{1,0:T(8,128)(2,1)S(1)}, u32[]{:S(2)}, u32[]{:S(2)}) %collective-permute-start.6) | collective-permute-done | bytes 131104 | tf_op jit(solution)/shard_map/ppermute | solution.py:156
  65.7 0.0 copy-done.1
  65.7 1.0 %node.9 = (bf16[256,512]{1,0:T(8,128)(2,1)S(1)}, bf16[256,256]{1,0:T(8,128)(2,1)S(1)}, bf16[256,256]{1,0:T(8,128)(2,1)S(1)}, bf16[64,256]{1,0:T(8,128)(2,1)S(1)}, bf16[64,256]{1,0:T(8,128)(2,1)S(1)}) custom-call(s32[1]{0:T(128)} %bitcast.core, bf16[256,512]{1,0:T(8,128)(2,1)S(1)} %get-tuple-element.69.state, bf16[256,256]{1,0:T(8,128)(2,1)S(1)} %edge_halo.2.mine, ...), custom_call_target="tpu_custom_call" | custom-call | flops 402653184 | bytes 1048576 | tf_op jit(solution)/shard_map/node/pallas_call | solution.py:268
  66.8 0.1 collective-permute-start.7
  66.9 4.8 %collective-permute-start.8 = (bf16[64,256]{1,0:T(8,128)(2,1)S(1)}, bf16[64,256]{1,0:T(8,128)(2,1)S(1)}, u32[]{:S(2)}, u32[]{:S(2)}) collective-permute-start(bf16[64,256]{1,0:T(8,128)(2,1)S(1)} %get-tuple-element.88), channel_id=1, source_target_pairs={{0,0},{2,4},{4,2},{6,8},{8,6},{10,12},{12,10},{14,16},{16,14},{18,... | collective-permute-start | bytes 98312 | tf_op jit(solution)/shard_map/ppermute | solution.py:276
  71.7 3.5 %edge_local.3.pre = f32[256,12288]{1,0:T(8,128)S(1)} custom-call(s32[1,12288]{1,0:T(1,128)S(1)} %or_select_fusion.source, s32[1,12288]{1,0:T(1,128)S(1)} %copy-done.14, bf16[256,256]{1,0:T(8,128)(2,1)S(1)} %get-tuple-element.85.sender, bf16[256,256]{1,0:T(8,128)(2,1)S(1)} %get-tuple-element.86.receiver), custom_call_target="tpu_custom_call" | custom-call | flops 3221225472 | bytes 1048576 | tf_op jit(solution)/shard_map/edge_local/pallas_call | solution.py:277
  75.2 0.0 collective-permute-done.7.one
  75.2 0.6 collective-permute-done.8.two
  75.8 3.8 %edge_halo.3.mine = bf16[256,256]{1,0:T(8,128)(2,1)S(1)} custom-call(s32[1,12288]{1,0:T(1,128)S(1)} %or_select_fusion.source, s32[1,12288]{1,0:T(1,128)S(1)} %copy-done.14, f32[256,12288]{1,0:T(8,128)S(1)} %edge_local.3.pre, bf16[64,256]{1,0:T(8,128)(2,1)S(1)} %collective-permute-done.7.one, bf16[64,256]{1,0:T(8,128)(2,1)S(1)} %collective-permute-done.8.two), custom_call_target="tpu_custom_call" | custom-call | flops 2415919104 | bytes 1048576 | tf_op jit(solution)/shard_map/edge_halo/pallas_call | solution.py:284
  79.6 1.6 %collective-permute-start.9 = (bf16[256,256]{1,0:T(8,128)(2,1)S(1)}, bf16[256,256]{1,0:T(8,128)(2,1)S(1)}, u32[]{:S(2)}, u32[]{:S(2)}) collective-permute-start(bf16[256,256]{1,0:T(8,128)(2,1)S(1)} %edge_halo.3.mine), channel_id=1, source_target_pairs={{0,1},{1,0},{2,3},{3,2},{4,5},{5,4},{6,7},{7,6},{8,9},{9,8},{10,11... | collective-permute-start | bytes 393224 | tf_op jit(solution)/shard_map/ppermute | solution.py:156
  81.2 1.0 %collective-permute-done.9.other = bf16[256,256]{1,0:T(8,128)(2,1)S(1)} collective-permute-done((bf16[256,256]{1,0:T(8,128)(2,1)S(1)}, bf16[256,256]{1,0:T(8,128)(2,1)S(1)}, u32[]{:S(2)}, u32[]{:S(2)}) %collective-permute-start.9) | collective-permute-done | bytes 131104 | tf_op jit(solution)/shard_map/ppermute | solution.py:156
  82.2 0.0 copy-done.13
  82.2 1.4 %node_last.1 = bf16[256,256]{1,0:T(8,128)(2,1)} custom-call(s32[1]{0:T(128)} %bitcast.core, bf16[256,512]{1,0:T(8,128)(2,1)S(1)} %get-tuple-element.84.state, bf16[256,256]{1,0:T(8,128)(2,1)S(1)} %edge_halo.3.mine, bf16[256,256]{1,0:T(8,128)(2,1)S(1)} %collective-permute-done.9.other, bf16[1024,256]{1,0:T(8,128)(2,1)S(1)} %get-tuple-element.89.in_mine, ...), custom_call_target="tpu_custom_call" | custom-call | flops 402653184 | bytes 1048576 | tf_op jit(solution)/shard_map/node_last/pallas_call | solution.py:267
  (45 shorter events, 0.1 us)
Async XLA Ops:
  6.1 12.6 %copy-start.31 = (s32[1,2,64]{2,1,0:T(2,128)S(1)}, s32[1,2,64]{2,1,0:T(2,128)}, u32[]{:S(2)}) copy-start(s32[1,2,64]{2,1,0:T(2,128)} %param.25) | copy-start | bytes 1540
  6.1 12.6 %copy-start.27 = (s32[1,12288]{1,0:T(1,128)S(1)}, s32[1,12288]{1,0:T(1,128)}, u32[]{:S(2)}) copy-start(s32[1,12288]{1,0:T(1,128)} %param.23) | copy-start | bytes 147460
  6.1 15.0 %copy-start.24 = (bf16[2,512,256]{2,1,0:T(8,128)(2,1)S(1)}, bf16[2,512,256]{2,1,0:T(8,128)(2,1)}, u32[]{:S(2)}) copy-start(bf16[2,512,256]{2,1,0:T(8,128)(2,1)} %param.27) | copy-start | bytes 1572868
  6.2 15.0 %copy-start.25 = (bf16[2,512,256]{2,1,0:T(8,128)(2,1)S(1)}, bf16[2,512,256]{2,1,0:T(8,128)(2,1)}, u32[]{:S(2)}) copy-start(bf16[2,512,256]{2,1,0:T(8,128)(2,1)} %param.26) | copy-start | bytes 1572868
  6.2 37.8 %all-to-all-start = ((bf16[64,64,256]{2,1,0:T(8,128)(2,1)}), bf16[64,64,256]{2,1,0:T(8,128)(2,1)S(1)}, u32[]{:S(2)}, u32[]{:S(2)}) async-start(bf16[64,64,256]{2,1,0:T(8,128)(2,1)} %embed.1), calls=%async_computation | async-start | bytes 4194304 | tf_op jit(solution)/shard_map/all_to_all | solution.py:204
  16.8 5.4 %copy-start.30 = (bf16[2,256]{1,0:T(2,128)(2,1)S(1)}, bf16[2,256]{1,0:T(2,128)(2,1)}, u32[]{:S(2)}) copy-start(bf16[2,256]{1,0:T(2,128)(2,1)} %param.28) | copy-start | bytes 3076
  16.8 10.1 %collective-permute-start.1 = (bf16[3,256]{1,0:T(4,128)(2,1)}, bf16[3,256]{1,0:T(4,128)(2,1)}, u32[]{:S(2)}, u32[]{:S(2)}) collective-permute-start(bf16[3,256]{1,0:T(4,128)(2,1)} %param.30), channel_id=1, source_target_pairs={{0,1},{1,0},{2,3},{3,2},{4,5},{5,4},{6,7},{7,6},{8,9},{9,8},{10,11... | collective-permute-start | bytes 4616 | tf_op jit(solution)/shard_map/ppermute | solution.py:156
  18.2 10.1 %collective-permute-start.2 = (bf16[3,256,512]{2,1,0:T(8,128)(2,1)}, bf16[3,256,512]{2,1,0:T(8,128)(2,1)}, u32[]{:S(2)}, u32[]{:S(2)}) collective-permute-start(bf16[3,256,512]{2,1,0:T(8,128)(2,1)} %param.31), channel_id=1, source_target_pairs={{0,1},{1,0},{2,3},{3,2},{4,5},{5,4},{6,7},{7,6},{8,9},{9,8},{10,11... | collective-permute-start | bytes 2359304 | tf_op jit(solution)/shard_map/ppermute | solution.py:156
  18.3 12.1 %collective-permute-start = (bf16[3,1024,256]{2,1,0:T(8,128)(2,1)}, bf16[3,1024,256]{2,1,0:T(8,128)(2,1)}, u32[]{:S(2)}, u32[]{:S(2)}) collective-permute-start(bf16[3,1024,256]{2,1,0:T(8,128)(2,1)} %param.29), channel_id=1, source_target_pairs={{0,1},{1,0},{2,3},{3,2},{4,5},{5,4},{6,7},{7,6},{8,9},{9,8},{10,11... | collective-permute-start | bytes 4718600 | tf_op jit(solution)/shard_map/ppermute | solution.py:156
  18.7 4.9 %copy-start.23 = (bf16[3,1024,256]{2,1,0:T(8,128)(2,1)S(1)}, bf16[3,1024,256]{2,1,0:T(8,128)(2,1)}, u32[]{:S(2)}) copy-start(bf16[3,1024,256]{2,1,0:T(8,128)(2,1)} %param.29) | copy-start | bytes 4718596
  22.2 2.5 %copy-start.26 = (bf16[256,256]{1,0:T(8,128)(2,1)S(1)}, bf16[256,256]{1,0:T(8,128)(2,1)}, u32[]{:S(2)}) copy-start(bf16[256,256]{1,0:T(8,128)(2,1)} %param.17) | copy-start | bytes 393220
  22.2 4.5 %copy-start.28 = (s32[1,64,64]{2,1,0:T(8,128)S(1)}, s32[1,64,64]{2,1,0:T(8,128)}, u32[]{:S(2)}) copy-start(s32[1,64,64]{2,1,0:T(8,128)} %param.21) | copy-start | bytes 49156
  22.2 4.6 %copy-start.29 = (bf16[1,64,64]{2,1,0:T(8,128)(2,1)S(1)}, bf16[1,64,64]{2,1,0:T(8,128)(2,1)}, u32[]{:S(2)}) copy-start(bf16[1,64,64]{2,1,0:T(8,128)(2,1)} %param.22) | copy-start | bytes 24580
  44.0 4.6 %copy-start.2 = (bf16[1024,256]{1,0:T(8,128)(2,1)S(1)}, bf16[1024,256]{1,0:T(8,128)(2,1)}, u32[]{:S(2)}) copy-start(bf16[1024,256]{1,0:T(8,128)(2,1)} %get-tuple-element.59.in_mine) | copy-start | bytes 1572868
  44.0 4.6 %copy-start.3 = (bf16[1024,256]{1,0:T(8,128)(2,1)S(1)}, bf16[1024,256]{1,0:T(8,128)(2,1)}, u32[]{:S(2)}) copy-start(bf16[1024,256]{1,0:T(8,128)(2,1)} %get-tuple-element.60.in_other) | copy-start | bytes 1572868
  44.0 4.6 %copy-start.6 = (bf16[256,512]{1,0:T(8,128)(2,1)S(1)}, bf16[256,512]{1,0:T(8,128)(2,1)}, u32[]{:S(2)}) copy-start(bf16[256,512]{1,0:T(8,128)(2,1)} %get-tuple-element.63.out_mine) | copy-start | bytes 786436
  44.0 4.6 %copy-start.7 = (bf16[256,512]{1,0:T(8,128)(2,1)S(1)}, bf16[256,512]{1,0:T(8,128)(2,1)}, u32[]{:S(2)}) copy-start(bf16[256,512]{1,0:T(8,128)(2,1)} %get-tuple-element.64.out_other) | copy-start | bytes 786436
  44.0 4.6 %copy-start.10 = (bf16[512,256]{1,0:T(8,128)(2,1)S(1)}, bf16[512,256]{1,0:T(8,128)(2,1)}, u32[]{:S(2)}) copy-start(bf16[512,256]{1,0:T(8,128)(2,1)} %get-tuple-element.66.recv_w) | copy-start | bytes 786436
  44.0 4.6 %copy-start.11 = (bf16[512,256]{1,0:T(8,128)(2,1)S(1)}, bf16[512,256]{1,0:T(8,128)(2,1)}, u32[]{:S(2)}) copy-start(bf16[512,256]{1,0:T(8,128)(2,1)} %get-tuple-element.65.send_w) | copy-start | bytes 786436
  44.0 4.6 %copy-start.18 = (f32[1,256]{1,0:T(1,128)S(1)}, f32[1,256]{1,0:T(1,128)}, u32[]{:S(2)}) copy-start(f32[1,256]{1,0:T(1,128)} %get-tuple-element.67.edge_bias) | copy-start | bytes 3076
  44.1 4.6 %copy-start.19 = (f32[1,256]{1,0:T(1,128)S(1)}, f32[1,256]{1,0:T(1,128)}, u32[]{:S(2)}) copy-start(f32[1,256]{1,0:T(1,128)} %get-tuple-element.61.bias_mine) | copy-start | bytes 3076
  44.1 4.6 %copy-start.22 = (f32[1,256]{1,0:T(1,128)S(1)}, f32[1,256]{1,0:T(1,128)}, u32[]{:S(2)}) copy-start(f32[1,256]{1,0:T(1,128)} %get-tuple-element.62.bias_other) | copy-start | bytes 3076
  44.1 10.8 %copy-start.14 = (s32[1,12288]{1,0:T(1,128)S(1)}, s32[1,12288]{1,0:T(1,128)}, u32[]{:S(2)}) copy-start(s32[1,12288]{1,0:T(1,128)} %node.11) | copy-start | bytes 147460
  44.8 3.8 %collective-permute-start.3 = (bf16[256,256]{1,0:T(8,128)(2,1)S(1)}, bf16[256,256]{1,0:T(8,128)(2,1)S(1)}, u32[]{:S(2)}, u32[]{:S(2)}) collective-permute-start(bf16[256,256]{1,0:T(8,128)(2,1)S(1)} %slots.1.mine), channel_id=1, source_target_pairs={{0,1},{1,0},{2,3},{3,2},{4,5},{5,4},{6,7},{7,6},{8,9},{9,8},{10,11... | collective-permute-start | bytes 393224 | tf_op jit(solution)/shard_map/ppermute | solution.py:156
  49.7 8.7 %collective-permute-start.4 = (bf16[64,256]{1,0:T(8,128)(2,1)S(1)}, bf16[64,256]{1,0:T(8,128)(2,1)S(1)}, u32[]{:S(2)}, u32[]{:S(2)}) collective-permute-start(bf16[64,256]{1,0:T(8,128)(2,1)S(1)} %get-tuple-element.73), channel_id=1, source_target_pairs={{0,2},{2,0},{4,6},{6,4},{8,10},{10,8},{12,14},{14,12},{16,18},{18,... | collective-permute-start | bytes 98312 | tf_op jit(solution)/shard_map/ppermute | solution.py:275
  50.1 8.9 %collective-permute-start.5 = (bf16[64,256]{1,0:T(8,128)(2,1)S(1)}, bf16[64,256]{1,0:T(8,128)(2,1)S(1)}, u32[]{:S(2)}, u32[]{:S(2)}) collective-permute-start(bf16[64,256]{1,0:T(8,128)(2,1)S(1)} %get-tuple-element.74), channel_id=1, source_target_pairs={{0,0},{2,4},{4,2},{6,8},{8,6},{10,12},{12,10},{14,16},{16,14},{18,... | collective-permute-start | bytes 98312 | tf_op jit(solution)/shard_map/ppermute | solution.py:276
  58.3 7.4 %copy-start = (bf16[1024,256]{1,0:T(8,128)(2,1)S(1)}, bf16[1024,256]{1,0:T(8,128)(2,1)}, u32[]{:S(2)}) copy-start(bf16[1024,256]{1,0:T(8,128)(2,1)} %get-tuple-element.75.in_mine) | copy-start | bytes 1572868
  58.3 7.4 %copy-start.1 = (bf16[1024,256]{1,0:T(8,128)(2,1)S(1)}, bf16[1024,256]{1,0:T(8,128)(2,1)}, u32[]{:S(2)}) copy-start(bf16[1024,256]{1,0:T(8,128)(2,1)} %get-tuple-element.76.in_other) | copy-start | bytes 1572868
  58.3 7.4 %copy-start.4 = (bf16[256,512]{1,0:T(8,128)(2,1)S(1)}, bf16[256,512]{1,0:T(8,128)(2,1)}, u32[]{:S(2)}) copy-start(bf16[256,512]{1,0:T(8,128)(2,1)} %get-tuple-element.79.out_mine) | copy-start | bytes 786436
  58.3 7.3 %copy-start.5 = (bf16[256,512]{1,0:T(8,128)(2,1)S(1)}, bf16[256,512]{1,0:T(8,128)(2,1)}, u32[]{:S(2)}) copy-start(bf16[256,512]{1,0:T(8,128)(2,1)} %get-tuple-element.80.out_other) | copy-start | bytes 786436
  58.3 7.3 %copy-start.8 = (bf16[512,256]{1,0:T(8,128)(2,1)S(1)}, bf16[512,256]{1,0:T(8,128)(2,1)}, u32[]{:S(2)}) copy-start(bf16[512,256]{1,0:T(8,128)(2,1)} %get-tuple-element.82.recv_w) | copy-start | bytes 786436
  58.4 7.3 %copy-start.9 = (bf16[512,256]{1,0:T(8,128)(2,1)S(1)}, bf16[512,256]{1,0:T(8,128)(2,1)}, u32[]{:S(2)}) copy-start(bf16[512,256]{1,0:T(8,128)(2,1)} %get-tuple-element.81.send_w) | copy-start | bytes 786436
  58.4 7.3 %copy-start.16 = (f32[1,256]{1,0:T(1,128)S(1)}, f32[1,256]{1,0:T(1,128)}, u32[]{:S(2)}) copy-start(f32[1,256]{1,0:T(1,128)} %get-tuple-element.83.edge_bias) | copy-start | bytes 3076
  58.4 7.3 %copy-start.17 = (f32[1,256]{1,0:T(1,128)S(1)}, f32[1,256]{1,0:T(1,128)}, u32[]{:S(2)}) copy-start(f32[1,256]{1,0:T(1,128)} %get-tuple-element.77.bias_mine) | copy-start | bytes 3076
  58.4 7.3 %copy-start.21 = (f32[1,256]{1,0:T(1,128)S(1)}, f32[1,256]{1,0:T(1,128)}, u32[]{:S(2)}) copy-start(f32[1,256]{1,0:T(1,128)} %get-tuple-element.78.bias_other) | copy-start | bytes 3076
  62.8 2.9 %collective-permute-start.6 = (bf16[256,256]{1,0:T(8,128)(2,1)S(1)}, bf16[256,256]{1,0:T(8,128)(2,1)S(1)}, u32[]{:S(2)}, u32[]{:S(2)}) collective-permute-start(bf16[256,256]{1,0:T(8,128)(2,1)S(1)} %edge_halo.2.mine), channel_id=1, source_target_pairs={{0,1},{1,0},{2,3},{3,2},{4,5},{5,4},{6,7},{7,6},{8,9},{9,8},{10,11... | collective-permute-start | bytes 393224 | tf_op jit(solution)/shard_map/ppermute | solution.py:156
  66.8 8.4 %collective-permute-start.7 = (bf16[64,256]{1,0:T(8,128)(2,1)S(1)}, bf16[64,256]{1,0:T(8,128)(2,1)S(1)}, u32[]{:S(2)}, u32[]{:S(2)}) collective-permute-start(bf16[64,256]{1,0:T(8,128)(2,1)S(1)} %get-tuple-element.87), channel_id=1, source_target_pairs={{0,2},{2,0},{4,6},{6,4},{8,10},{10,8},{12,14},{14,12},{16,18},{18,... | collective-permute-start | bytes 98312 | tf_op jit(solution)/shard_map/ppermute | solution.py:275
  66.9 8.9 %collective-permute-start.8 = (bf16[64,256]{1,0:T(8,128)(2,1)S(1)}, bf16[64,256]{1,0:T(8,128)(2,1)S(1)}, u32[]{:S(2)}, u32[]{:S(2)}) collective-permute-start(bf16[64,256]{1,0:T(8,128)(2,1)S(1)} %get-tuple-element.88), channel_id=1, source_target_pairs={{0,0},{2,4},{4,2},{6,8},{8,6},{10,12},{12,10},{14,16},{16,14},{18,... | collective-permute-start | bytes 98312 | tf_op jit(solution)/shard_map/ppermute | solution.py:276
  75.1 7.1 %copy-start.12 = (bf16[256,512]{1,0:T(8,128)(2,1)S(1)}, bf16[256,512]{1,0:T(8,128)(2,1)}, u32[]{:S(2)}) copy-start(bf16[256,512]{1,0:T(8,128)(2,1)} %get-tuple-element.93.out_mine) | copy-start | bytes 786436
  75.1 7.1 %copy-start.13 = (bf16[256,512]{1,0:T(8,128)(2,1)S(1)}, bf16[256,512]{1,0:T(8,128)(2,1)}, u32[]{:S(2)}) copy-start(bf16[256,512]{1,0:T(8,128)(2,1)} %get-tuple-element.94.out_other) | copy-start | bytes 786436
  75.1 7.0 %copy-start.15 = (f32[1,256]{1,0:T(1,128)S(1)}, f32[1,256]{1,0:T(1,128)}, u32[]{:S(2)}) copy-start(f32[1,256]{1,0:T(1,128)} %get-tuple-element.91.bias_mine) | copy-start | bytes 3076
  75.2 7.0 %copy-start.20 = (f32[1,256]{1,0:T(1,128)S(1)}, f32[1,256]{1,0:T(1,128)}, u32[]{:S(2)}) copy-start(f32[1,256]{1,0:T(1,128)} %get-tuple-element.92.bias_other) | copy-start | bytes 3076
  79.6 2.6 %collective-permute-start.9 = (bf16[256,256]{1,0:T(8,128)(2,1)S(1)}, bf16[256,256]{1,0:T(8,128)(2,1)S(1)}, u32[]{:S(2)}, u32[]{:S(2)}) collective-permute-start(bf16[256,256]{1,0:T(8,128)(2,1)S(1)} %edge_halo.3.mine), channel_id=1, source_target_pairs={{0,1},{1,0},{2,3},{3,2},{4,5},{5,4},{6,7},{7,6},{8,9},{9,8},{10,11... | collective-permute-start | bytes 393224 | tf_op jit(solution)/shard_map/ppermute | solution.py:156

commit v4 on v3

--- a/solution.py
+++ b/solution.py
@@ -9,7 +9,6 @@
 
 VMEM = pl.BlockSpec(memory_space=pltpu.VMEM)
 SMEM = pl.BlockSpec(memory_space=pltpu.SMEM)
-HBM = pl.BlockSpec(memory_space=pltpu.HBM)
 F32 = jnp.float32
 BF16 = jnp.bfloat16
 
@@ -32,54 +31,34 @@
     return jnp.where(ids == row.astype(jnp.int16), jnp.ones((), BF16), jnp.zeros((), BF16))
 
 
-def call(kernel, name, out_shape, in_specs, flops, out_specs=None, limit=24, scratch=()):
+def call(kernel, name, out_shape, in_specs, flops, limit=24):
     many = isinstance(out_shape, tuple)
     return pl.pallas_call(
         kernel,
         name=name,
         out_shape=out_shape,
         in_specs=in_specs,
-        out_specs=out_specs or ((VMEM,) * len(out_shape) if many else VMEM),
-        scratch_shapes=scratch,
+        out_specs=(VMEM,) * len(out_shape) if many else VMEM,
         compiler_params=pltpu.CompilerParams(vmem_limit_bytes=limit * 2**20),
         cost_estimate=pl.CostEstimate(flops=flops, bytes_accessed=2**20, transcendentals=0),
     )
 
 
-def embed_kernel(grid, weights, bias, source, rows_out, grid_in, weights_in, source_in, rows, sems):
-    fetch = [
-        pltpu.make_async_copy(grid, grid_in, sems.at[0]),
-        pltpu.make_async_copy(weights, weights_in, sems.at[1]),
-        pltpu.make_async_copy(source, source_in, sems.at[2]),
-    ]
-    for copy in fetch:
-        copy.start()
-    for copy in fetch:
-        copy.wait()
+def embed_kernel(grid, weights, bias, source, rows_out):
     bands, slots, _ = rows_out.shape
     count = grid.shape[0]
     add = bias[...].astype(F32).reshape(1, bias.shape[0])
-    embedding = silu(dot32(grid_in[...], weights_in[...]) + add).astype(BF16)
-    columns = source_in[0].T
+    embedding = silu(dot32(grid[...], weights[...]) + add).astype(BF16)
+    columns = source[0].T
     ids = lax.broadcasted_iota(jnp.int32, (slots, count), 1)
     group = 8 if bands % 8 == 0 else 1
-    leave = []
     for first in range(0, bands, group):
         chosen = [
             jnp.where(ids == columns[:, band : band + 1], jnp.ones((), BF16), jnp.zeros((), BF16))
             for band in range(first, first + group)
         ]
         part = dot32(jnp.concatenate(chosen, 0), embedding).astype(BF16)
-        rows[first : first + group] = part.reshape(group, slots, part.shape[1])
-        copy = pltpu.make_async_copy(
-            rows.at[pl.ds(first, group)],
-            rows_out.at[pl.ds(first, group)],
-            sems.at[3 + first // group],
-        )
-        copy.start()
-        leave.append(copy)
-    for copy in leave:
-        copy.wait()
+        rows_out[first : first + group] = part.reshape(group, slots, part.shape[1])
 
 
 def slots_kernel(node, weight, rows, aggregate):
@@ -184,22 +163,13 @@
     band_count = g2m_src.shape[1]
     slot_count = g2m_src.shape[2]
     slots = band_count * slot_count
-    outgoing_shape = (band_count, slot_count, feature_width)
     outgoing = call(
         embed_kernel,
         "embed",
-        jax.ShapeDtypeStruct(outgoing_shape, BF16),
-        [HBM, HBM, VMEM, HBM],
+        jax.ShapeDtypeStruct((band_count, slot_count, feature_width), BF16),
+        [VMEM] * 4,
         2 * slots * grid_latent.shape[0] * feature_width,
-        HBM,
-        60,
-        [
-            pltpu.VMEM(grid_latent.shape, BF16),
-            pltpu.VMEM(grid_in_w.shape, BF16),
-            pltpu.VMEM(g2m_src.shape, jnp.int32),
-            pltpu.VMEM(outgoing_shape, BF16),
-            pltpu.SemaphoreType.DMA((3 + band_count,)),
-        ],
+        limit=60,
     )(grid_latent, grid_in_w, grid_bias, g2m_src)
     incoming = lax.all_to_all(outgoing, "band", split_axis=0, concat_axis=0, tiled=True)
 
@@ -225,17 +195,17 @@
         (edge_send_w[step], edge_recv_w[step], edge_bias[step].astype(F32)[None])
         for step in range(layers - 1)
     ]
-    even = part % 2 == 0
+    odd = part % 2 == 1
     to_next, to_previous = halo_index[0, 0], halo_index[0, 1]
     leaving = jnp.concatenate(
-        [jnp.where(even, to_next, to_previous), jnp.where(even, to_previous, to_next)]
+        [jnp.where(odd, to_next, to_previous), jnp.where(odd, to_previous, to_next)]
     )
     halo_ids = lax.broadcasted_iota(jnp.int32, (2 * halo, nodes), 1)
     halo_hot = (leaving[:, None] == halo_ids).astype(BF16)
     from_previous = (mesh_src >= nodes) & (mesh_src < nodes + halo)
     from_next = mesh_src >= nodes + halo
     source = mesh_src + jnp.where(
-        even & from_previous, halo, jnp.where(even & from_next, -halo, 0)
+        odd & from_previous, halo, jnp.where(odd & from_next, -halo, 0)
     )
     outside = (from_previous & (part == 0)) | (from_next & (part == partitions - 1))
     source = jnp.where(outside, -1, source)
@@ -254,11 +224,15 @@
         2 * slots * nodes * feature_width,
     )(slot_node, slot_weight, incoming.reshape(slots, -1))
 
-    pairs_one = [(i, i ^ 1) if i ^ 1 < partitions else (i, i) for i in range(partitions)]
-    pairs_two = [
-        (i, ((i - 1) ^ 1) + 1) if 0 < i and ((i - 1) ^ 1) + 1 < partitions else (i, i)
-        for i in range(partitions)
-    ]
+    cores = lax.axis_size("feat")
+    pairs_two = [(i, i ^ 1) for i in range(partitions)]
+    pairs_one = []
+    for i in range(partitions):
+        other = ((i - 1) ^ 1) + 1
+        for c in range(cores):
+            end = i == 0 or other >= partitions
+            partner = i * cores + (c ^ 1) if end else other * cores + c
+            pairs_one.append((i * cores + c, partner))
     halo_rows = jax.ShapeDtypeStruct((halo, feature_width), BF16)
     node_flops = 2 * nodes * wide * (deep + wide)
     for layer in range(layers):
@@ -272,7 +246,7 @@
             [SMEM] + [VMEM] * 13,
             node_flops,
         )(*operands, *edge_w[layer], halo_hot)
-        arrived_one = lax.ppermute(leaving_one, "band", pairs_one)
+        arrived_one = lax.ppermute(leaving_one, ("band", "feat"), pairs_one)
         arrived_two = lax.ppermute(leaving_two, "band", pairs_two)
         pre = call(
             local_kernel,

time: 84 us -> 78.8 us (0.938)
  starting transfers between devices: 28.7 us -> 22.1 us
  waiting for transfers between devices: 15.3 us -> 17.7 us
    ppermute x2, starting transfers between devices: 9.49 us -> 0.01 us  [body(): arrived_two = lax.ppermute(leaving_two, 'band', pairs_two)]
    ppermute x2, waiting for transfers between devices: 0.01 us -> 3.47 us  [body(): arrived_one = lax.ppermute(leaving_one, ('band', 'feat'), pairs_one)]
    ppermute x2, starting transfers between devices: 0.48 us -> 3.59 us  [body(): arrived_one = lax.ppermute(leaving_one, ('band', 'feat'), pairs_one)]
    ppermute x2, waiting for transfers between devices: 1.15 us -> 0.01 us  [body(): arrived_two = lax.ppermute(leaving_two, 'band', pairs_two)]
  transfers between devices with their start and end apart: 11 -> 11, of which waited for: 6 -> 6; matrix products, arithmetic and copies ran while one was open for 14% -> 15% of each run, Pallas kernels for 8% -> 9%
where the time goes in v4:
time: 78.8 us; the launch traced here: 78.4 us
  Pallas kernels  24.1 us (31%)
  starting transfers between devices  22.1 us (28%)
  waiting for transfers between devices  17.7 us (22%)
  local copies, waits for them, and re-layouts  9.01 us (11%)
  other arithmetic  3.18 us (4%)
  blocking collectives  1.98 us (3%)
    all_to_all x1, waiting for transfers between devices, body(): lax.all_to_all(outgoing, 'band', split_axis=0, concat_axis=0, tiled=True)  11.2 us
    all_to_all x1, starting transfers between devices, body(): lax.all_to_all(outgoing, 'band', split_axis=0, concat_axis=0, tiled=True)  10.7 us
    ppermute x6, starting transfers between devices, swap_cores(): return lax.ppermute(value, 'feat', [(0, 1), (1, 0)])  7.83 us
    pallas_call x2, Pallas kernels, body(): call(halo_kernel, 'edge_halo', half, [VMEM] * 5, 3 * edges * nodes * feat...  7.66 us
    pallas_call x2, Pallas kernels, body(): call(local_kernel, 'edge_local', pltpu.VMEM((feature_width, edges), F32),...  6.9 us
    pallas_call x1, Pallas kernels, body(): call(embed_kernel, 'embed', jax.ShapeDtypeStruct((band_count, slot_count,...  5.35 us
    ppermute x2, starting transfers between devices, body(): arrived_one = lax.ppermute(leaving_one, ('band', 'feat'), pairs_one)  3.59 us
    ppermute x2, waiting for transfers between devices, body(): arrived_one = lax.ppermute(leaving_one, ('band', 'feat'), pairs_one)  3.47 us
  transfers between devices with their start and end apart: 11, of which 6 were waited for; matrix products, arithmetic and copies ran while one was open for 15% of the time, Pallas kernels for 9%

profile of v4, /device:TPU:33, one launch (start us, length us, event | category | flops | bytes accessed | tf_op | source)
XLA Modules:
  0.0 78.4 jit_solution(1435913308857351602)
XLA Ops:
  0.0 5.3 %embed.1 = bf16[64,64,256]{2,1,0:T(8,128)(2,1)} custom-call(bf16[1024,512]{1,0:T(8,128)(2,1)} %grid.1, bf16[512,256]{1,0:T(8,128)(2,1)} %weights.1, bf16[256]{0:T(256)(128)(2,1)} %bias.1, s32[1,64,64]{2,1,0:T(8,128)} %source.1), custom_call_target="tpu_custom_call" | custom-call | flops 2147483648 | bytes 1048576 | tf_op jit(solution)/shard_map/embed/pallas_call | solution.py:166
  5.4 10.7 %all-to-all-start = ((bf16[64,64,256]{2,1,0:T(8,128)(2,1)}), bf16[64,64,256]{2,1,0:T(8,128)(2,1)S(1)}, u32[]{:S(2)}, u32[]{:S(2)}) async-start(bf16[64,64,256]{2,1,0:T(8,128)(2,1)} %embed.1), calls=%async_computation | async-start | bytes 4194304 | tf_op jit(solution)/shard_map/all_to_all | solution.py:174
  16.0 0.0 copy-start.30
  16.0 1.3 %collective-permute-start.1 = (bf16[3,256]{1,0:T(4,128)(2,1)}, bf16[3,256]{1,0:T(4,128)(2,1)}, u32[]{:S(2)}, u32[]{:S(2)}) collective-permute-start(bf16[3,256]{1,0:T(4,128)(2,1)} %param.30), channel_id=1, source_target_pairs={{0,1},{1,0},{2,3},{3,2},{4,5},{5,4},{6,7},{7,6},{8,9},{9,8},{10,11... | collective-permute-start | bytes 4616 | tf_op jit(solution)/shard_map/ppermute | solution.py:135
  17.4 0.1 collective-permute-start.2
  17.5 0.4 collective-permute-start
  17.9 0.2 or_select_fusion.source
  18.1 0.1 pad_add_fusion
  18.2 0.1 fusion.halo_hot
  18.3 2.1 %slice_bitcast_fusion.13 = (bf16[256,512]{1,0:T(8,128)(2,1)}, bf16[256,512]{1,0:T(8,128)(2,1)}, bf16[256,512]{1,0:T(8,128)(2,1)}) fusion(bf16[3,256,512]{2,1,0:T(8,128)(2,1)} %param.31), kind=kLoop, calls=%fused_computation.13 | loop fusion | bytes 1572864 | tf_op jit(solution)/shard_map/squeeze | solution.py:189
  20.4 0.0 copy-done.25
  20.4 1.0 %slice_bitcast_fusion.9 = (bf16[512,256]{1,0:T(8,128)(2,1)}, bf16[512,256]{1,0:T(8,128)(2,1)}, bf16[512,256]{1,0:T(8,128)(2,1)}, bf16[512,256]{1,0:T(8,128)(2,1)}) fusion(bf16[2,512,256]{2,1,0:T(8,128)(2,1)S(1)} %copy-done.24, bf16[2,512,256]{2,1,0:T(8,128)(2,1)S(1)} %copy-done.25), kind=kLoop, calls=%fused_computation.9 | loop fusion | bytes 2097152 | tf_op jit(solution)/shard_map/squeeze | solution.py:195
  21.4 1.4 %slice_convert_fusion.3 = (f32[1,256]{1,0:T(1,128)}, f32[1,256]{1,0:T(1,128)}, f32[1,256]{1,0:T(1,128)}, f32[1,256]{1,0:T(1,128)}, f32[1,256]{1,0:T(1,128)}) fusion(bf16[2,256]{1,0:T(2,128)(2,1)S(1)} %copy-done.30, bf16[3,256]{1,0:T(4,128)(2,1)} %param.30), kind=kLoop, calls=%fused_computation.26 | loop fusion | flops 1280 | bytes 7680 | tf_op jit(solution)/shard_map/convert_element_type | solution.py:195
  22.8 1.1 %slice_bitcast_fusion.3 = (bf16[1024,256]{1,0:T(8,128)(2,1)S(1)}, bf16[1024,256]{1,0:T(8,128)(2,1)}, bf16[1024,256]{1,0:T(8,128)(2,1)}) fusion(bf16[3,1024,256]{2,1,0:T(8,128)(2,1)S(1)} %copy-done.23), kind=kLoop, calls=%fused_computation.3 | loop fusion | bytes 3145728 | tf_op jit(solution)/shard_map/squeeze | solution.py:185
  23.9 2.0 %all_gather.3.state = bf16[256,512]{1,0:T(8,128)(2,1)S(1)} all-gather(bf16[256,256]{1,0:T(8,128)(2,1)S(1)} %copy-done.26), channel_id=1, replica_groups=mesh['band'=64,'feat'=2] {'feat'}, dimensions={1}, use_global_device_ids=true | all-gather | bytes 393216 | tf_op jit(solution)/shard_map/all_gather | solution.py:181
  25.9 0.0 copy-done.28
  25.9 0.1 reshape.18.node
  26.0 0.1 reshape.19.weight
  26.1 0.0 collective-permute-done.1
  26.1 1.4 %slice_convert_fusion = (f32[1,256]{1,0:T(1,128)}, f32[1,256]{1,0:T(1,128)}, f32[1,256]{1,0:T(1,128)}) fusion(bf16[3,256]{1,0:T(4,128)(2,1)} %collective-permute-done.1), kind=kLoop, calls=%fused_computation.23 | loop fusion | flops 768 | bytes 4608 | tf_op jit(solution)/shard_map/convert_element_type | solution.py:188
  27.5 0.0 collective-permute-done.2
  27.5 2.1 %slice_bitcast_fusion.6 = (bf16[256,512]{1,0:T(8,128)(2,1)}, bf16[256,512]{1,0:T(8,128)(2,1)}, bf16[256,512]{1,0:T(8,128)(2,1)}) fusion(bf16[3,256,512]{2,1,0:T(8,128)(2,1)} %collective-permute-done.2), kind=kLoop, calls=%fused_computation.6 | loop fusion | bytes 1572864 | tf_op jit(solution)/shard_map/squeeze | solution.py:190
  29.6 0.0 collective-permute-done
  29.6 2.4 %slice_bitcast_fusion = (bf16[1024,256]{1,0:T(8,128)(2,1)S(1)}, bf16[1024,256]{1,0:T(8,128)(2,1)}, bf16[1024,256]{1,0:T(8,128)(2,1)}) fusion(bf16[3,1024,256]{2,1,0:T(8,128)(2,1)} %collective-permute-done), kind=kLoop, calls=%fused_computation | loop fusion | bytes 3145728 | tf_op jit(solution)/shard_map/squeeze | solution.py:186
  32.0 11.2 %all-to-all-done = bf16[64,64,256]{2,1,0:T(8,128)(2,1)S(1)} async-done(((bf16[64,64,256]{2,1,0:T(8,128)(2,1)}), bf16[64,64,256]{2,1,0:T(8,128)(2,1)S(1)}, u32[]{:S(2)}, u32[]{:S(2)}) %all-to-all-start) | async-done | bytes 2097184 | tf_op jit(solution)/shard_map/all_to_all | solution.py:174
  43.2 0.0 copy-start.10
  43.2 0.0 copy-start.11
  43.2 0.0 copy-start.18
  43.3 0.0 copy-start.19
  43.3 0.0 copy-start.22
  43.3 0.0 copy-start.14
  43.3 0.7 slots.1.mine
  44.0 2.8 %collective-permute-start.3 = (bf16[256,256]{1,0:T(8,128)(2,1)S(1)}, bf16[256,256]{1,0:T(8,128)(2,1)S(1)}, u32[]{:S(2)}, u32[]{:S(2)}) collective-permute-start(bf16[256,256]{1,0:T(8,128)(2,1)S(1)} %slots.1.mine), channel_id=1, source_target_pairs={{0,1},{1,0},{2,3},{3,2},{4,5},{5,4},{6,7},{7,6},{8,9},{9,8},{10,11... | collective-permute-start | bytes 393224 | tf_op jit(solution)/shard_map/ppermute | solution.py:135
  46.8 1.0 %collective-permute-done.3.other = bf16[256,256]{1,0:T(8,128)(2,1)S(1)} collective-permute-done((bf16[256,256]{1,0:T(8,128)(2,1)S(1)}, bf16[256,256]{1,0:T(8,128)(2,1)S(1)}, u32[]{:S(2)}, u32[]{:S(2)}) %collective-permute-start.3) | collective-permute-done | bytes 131104 | tf_op jit(solution)/shard_map/ppermute | solution.py:135
  47.8 0.0 copy-done.2
  47.8 0.0 copy-done.6
  47.9 1.0 %node.6 = (bf16[256,512]{1,0:T(8,128)(2,1)S(1)}, bf16[256,256]{1,0:T(8,128)(2,1)S(1)}, bf16[256,256]{1,0:T(8,128)(2,1)S(1)}, bf16[64,256]{1,0:T(8,128)(2,1)S(1)}, bf16[64,256]{1,0:T(8,128)(2,1)S(1)}) custom-call(s32[1]{0:T(128)} %bitcast.core, bf16[256,512]{1,0:T(8,128)(2,1)S(1)} %all_gather.3.state, bf16[256,256]{1,0:T(8,128)(2,1)S(1)} %slots.1.mine, ...), custom_call_target="tpu_custom_call" | custom-call | flops 402653184 | bytes 1048576 | tf_op jit(solution)/shard_map/node/pallas_call | solution.py:242
  48.9 1.8 %collective-permute-start.4 = (bf16[64,256]{1,0:T(8,128)(2,1)S(1)}, bf16[64,256]{1,0:T(8,128)(2,1)S(1)}, u32[]{:S(2)}, u32[]{:S(2)}) collective-permute-start(bf16[64,256]{1,0:T(8,128)(2,1)S(1)} %get-tuple-element.73), channel_id=1, source_target_pairs={{0,1},{1,0},{2,4},{3,5},{4,2},{5,3},{6,8},{7,9},{8,6},{9,7},{10,12... | collective-permute-start | bytes 98312 | tf_op jit(solution)/shard_map/ppermute | solution.py:249
  50.7 0.0 collective-permute-start.5
  50.7 3.5 %edge_local.2.pre = f32[256,12288]{1,0:T(8,128)S(1)} custom-call(s32[1,12288]{1,0:T(1,128)S(1)} %or_select_fusion.source, s32[1,12288]{1,0:T(1,128)S(1)} %copy-done.14, bf16[256,256]{1,0:T(8,128)(2,1)S(1)} %get-tuple-element.71.sender, bf16[256,256]{1,0:T(8,128)(2,1)S(1)} %get-tuple-element.72.receiver), custom_call_target="tpu_custom_call" | custom-call | flops 3221225472 | bytes 1048576 | tf_op jit(solution)/shard_map/edge_local/pallas_call | solution.py:251
  54.1 0.0 copy-start
  54.2 0.0 copy-start.1
  54.2 0.0 copy-start.4
  54.2 0.0 copy-start.5
  54.2 0.0 copy-start.8
  54.2 0.0 copy-start.9
  54.2 0.0 copy-start.16
  54.2 1.7 %collective-permute-done.4.one = bf16[64,256]{1,0:T(8,128)(2,1)S(1)} collective-permute-done((bf16[64,256]{1,0:T(8,128)(2,1)S(1)}, bf16[64,256]{1,0:T(8,128)(2,1)S(1)}, u32[]{:S(2)}, u32[]{:S(2)}) %collective-permute-start.4) | collective-permute-done | bytes 32800 | tf_op jit(solution)/shard_map/ppermute | solution.py:249
  56.0 0.0 collective-permute-done.5.two
  56.0 3.8 %edge_halo.2.mine = bf16[256,256]{1,0:T(8,128)(2,1)S(1)} custom-call(s32[1,12288]{1,0:T(1,128)S(1)} %or_select_fusion.source, s32[1,12288]{1,0:T(1,128)S(1)} %copy-done.14, f32[256,12288]{1,0:T(8,128)S(1)} %edge_local.2.pre, bf16[64,256]{1,0:T(8,128)(2,1)S(1)} %collective-permute-done.4.one, bf16[64,256]{1,0:T(8,128)(2,1)S(1)} %collective-permute-done.5.two), custom_call_target="tpu_custom_call" | custom-call | flops 2415919104 | bytes 1048576 | tf_op jit(solution)/shard_map/edge_halo/pallas_call | solution.py:258
  59.8 1.6 %collective-permute-start.6 = (bf16[256,256]{1,0:T(8,128)(2,1)S(1)}, bf16[256,256]{1,0:T(8,128)(2,1)S(1)}, u32[]{:S(2)}, u32[]{:S(2)}) collective-permute-start(bf16[256,256]{1,0:T(8,128)(2,1)S(1)} %edge_halo.2.mine), channel_id=1, source_target_pairs={{0,1},{1,0},{2,3},{3,2},{4,5},{5,4},{6,7},{7,6},{8,9},{9,8},{10,11... | collective-permute-start | bytes 393224 | tf_op jit(solution)/shard_map/ppermute | solution.py:135
  61.4 1.0 %collective-permute-done.6.other = bf16[256,256]{1,0:T(8,128)(2,1)S(1)} collective-permute-done((bf16[256,256]{1,0:T(8,128)(2,1)S(1)}, bf16[256,256]{1,0:T(8,128)(2,1)S(1)}, u32[]{:S(2)}, u32[]{:S(2)}) %collective-permute-start.6) | collective-permute-done | bytes 131104 | tf_op jit(solution)/shard_map/ppermute | solution.py:135
  62.4 0.0 copy-done
  62.4 0.0 copy-done.8
  62.5 1.0 %node.9 = (bf16[256,512]{1,0:T(8,128)(2,1)S(1)}, bf16[256,256]{1,0:T(8,128)(2,1)S(1)}, bf16[256,256]{1,0:T(8,128)(2,1)S(1)}, bf16[64,256]{1,0:T(8,128)(2,1)S(1)}, bf16[64,256]{1,0:T(8,128)(2,1)S(1)}) custom-call(s32[1]{0:T(128)} %bitcast.core, bf16[256,512]{1,0:T(8,128)(2,1)S(1)} %get-tuple-element.69.state, bf16[256,256]{1,0:T(8,128)(2,1)S(1)} %edge_halo.2.mine, ...), custom_call_target="tpu_custom_call" | custom-call | flops 402653184 | bytes 1048576 | tf_op jit(solution)/shard_map/node/pallas_call | solution.py:242
  63.5 1.8 %collective-permute-start.7 = (bf16[64,256]{1,0:T(8,128)(2,1)S(1)}, bf16[64,256]{1,0:T(8,128)(2,1)S(1)}, u32[]{:S(2)}, u32[]{:S(2)}) collective-permute-start(bf16[64,256]{1,0:T(8,128)(2,1)S(1)} %get-tuple-element.87), channel_id=1, source_target_pairs={{0,1},{1,0},{2,4},{3,5},{4,2},{5,3},{6,8},{7,9},{8,6},{9,7},{10,12... | collective-permute-start | bytes 98312 | tf_op jit(solution)/shard_map/ppermute | solution.py:249
  65.3 0.0 collective-permute-start.8
  65.3 3.5 %edge_local.3.pre = f32[256,12288]{1,0:T(8,128)S(1)} custom-call(s32[1,12288]{1,0:T(1,128)S(1)} %or_select_fusion.source, s32[1,12288]{1,0:T(1,128)S(1)} %copy-done.14, bf16[256,256]{1,0:T(8,128)(2,1)S(1)} %get-tuple-element.85.sender, bf16[256,256]{1,0:T(8,128)(2,1)S(1)} %get-tuple-element.86.receiver), custom_call_target="tpu_custom_call" | custom-call | flops 3221225472 | bytes 1048576 | tf_op jit(solution)/shard_map/edge_local/pallas_call | solution.py:251
  68.8 1.7 %collective-permute-done.7.one = bf16[64,256]{1,0:T(8,128)(2,1)S(1)} collective-permute-done((bf16[64,256]{1,0:T(8,128)(2,1)S(1)}, bf16[64,256]{1,0:T(8,128)(2,1)S(1)}, u32[]{:S(2)}, u32[]{:S(2)}) %collective-permute-start.7) | collective-permute-done | bytes 32800 | tf_op jit(solution)/shard_map/ppermute | solution.py:249
  70.6 0.0 collective-permute-done.8.two
  70.6 3.8 %edge_halo.3.mine = bf16[256,256]{1,0:T(8,128)(2,1)S(1)} custom-call(s32[1,12288]{1,0:T(1,128)S(1)} %or_select_fusion.source, s32[1,12288]{1,0:T(1,128)S(1)} %copy-done.14, f32[256,12288]{1,0:T(8,128)S(1)} %edge_local.3.pre, bf16[64,256]{1,0:T(8,128)(2,1)S(1)} %collective-permute-done.7.one, bf16[64,256]{1,0:T(8,128)(2,1)S(1)} %collective-permute-done.8.two), custom_call_target="tpu_custom_call" | custom-call | flops 2415919104 | bytes 1048576 | tf_op jit(solution)/shard_map/edge_halo/pallas_call | solution.py:258
  74.4 1.6 %collective-permute-start.9 = (bf16[256,256]{1,0:T(8,128)(2,1)S(1)}, bf16[256,256]{1,0:T(8,128)(2,1)S(1)}, u32[]{:S(2)}, u32[]{:S(2)}) collective-permute-start(bf16[256,256]{1,0:T(8,128)(2,1)S(1)} %edge_halo.3.mine), channel_id=1, source_target_pairs={{0,1},{1,0},{2,3},{3,2},{4,5},{5,4},{6,7},{7,6},{8,9},{9,8},{10,11... | collective-permute-start | bytes 393224 | tf_op jit(solution)/shard_map/ppermute | solution.py:135
  76.0 1.0 %collective-permute-done.9.other = bf16[256,256]{1,0:T(8,128)(2,1)S(1)} collective-permute-done((bf16[256,256]{1,0:T(8,128)(2,1)S(1)}, bf16[256,256]{1,0:T(8,128)(2,1)S(1)}, u32[]{:S(2)}, u32[]{:S(2)}) %collective-permute-start.9) | collective-permute-done | bytes 131104 | tf_op jit(solution)/shard_map/ppermute | solution.py:135
  77.0 1.4 %node_last.1 = bf16[256,256]{1,0:T(8,128)(2,1)} custom-call(s32[1]{0:T(128)} %bitcast.core, bf16[256,512]{1,0:T(8,128)(2,1)S(1)} %get-tuple-element.84.state, bf16[256,256]{1,0:T(8,128)(2,1)S(1)} %edge_halo.3.mine, bf16[256,256]{1,0:T(8,128)(2,1)S(1)} %collective-permute-done.9.other, bf16[1024,256]{1,0:T(8,128)(2,1)S(1)} %get-tuple-element.89.in_mine, ...), custom_call_target="tpu_custom_call" | custom-call | flops 402653184 | bytes 1048576 | tf_op jit(solution)/shard_map/node_last/pallas_call | solution.py:241
  (45 shorter events, 0.1 us)
Async XLA Ops:
  5.3 12.5 %copy-start.31 = (s32[1,2,64]{2,1,0:T(2,128)S(1)}, s32[1,2,64]{2,1,0:T(2,128)}, u32[]{:S(2)}) copy-start(s32[1,2,64]{2,1,0:T(2,128)} %param.25) | copy-start | bytes 1540
  5.3 12.5 %copy-start.27 = (s32[1,12288]{1,0:T(1,128)S(1)}, s32[1,12288]{1,0:T(1,128)}, u32[]{:S(2)}) copy-start(s32[1,12288]{1,0:T(1,128)} %param.23) | copy-start | bytes 147460
  5.4 15.0 %copy-start.24 = (bf16[2,512,256]{2,1,0:T(8,128)(2,1)S(1)}, bf16[2,512,256]{2,1,0:T(8,128)(2,1)}, u32[]{:S(2)}) copy-start(bf16[2,512,256]{2,1,0:T(8,128)(2,1)} %param.27) | copy-start | bytes 1572868
  5.4 15.0 %copy-start.25 = (bf16[2,512,256]{2,1,0:T(8,128)(2,1)S(1)}, bf16[2,512,256]{2,1,0:T(8,128)(2,1)}, u32[]{:S(2)}) copy-start(bf16[2,512,256]{2,1,0:T(8,128)(2,1)} %param.26) | copy-start | bytes 1572868
  5.4 37.8 %all-to-all-start = ((bf16[64,64,256]{2,1,0:T(8,128)(2,1)}), bf16[64,64,256]{2,1,0:T(8,128)(2,1)S(1)}, u32[]{:S(2)}, u32[]{:S(2)}) async-start(bf16[64,64,256]{2,1,0:T(8,128)(2,1)} %embed.1), calls=%async_computation | async-start | bytes 4194304 | tf_op jit(solution)/shard_map/all_to_all | solution.py:174
  16.0 5.4 %copy-start.30 = (bf16[2,256]{1,0:T(2,128)(2,1)S(1)}, bf16[2,256]{1,0:T(2,128)(2,1)}, u32[]{:S(2)}) copy-start(bf16[2,256]{1,0:T(2,128)(2,1)} %param.28) | copy-start | bytes 3076
  16.0 10.1 %collective-permute-start.1 = (bf16[3,256]{1,0:T(4,128)(2,1)}, bf16[3,256]{1,0:T(4,128)(2,1)}, u32[]{:S(2)}, u32[]{:S(2)}) collective-permute-start(bf16[3,256]{1,0:T(4,128)(2,1)} %param.30), channel_id=1, source_target_pairs={{0,1},{1,0},{2,3},{3,2},{4,5},{5,4},{6,7},{7,6},{8,9},{9,8},{10,11... | collective-permute-start | bytes 4616 | tf_op jit(solution)/shard_map/ppermute | solution.py:135
  17.4 10.1 %collective-permute-start.2 = (bf16[3,256,512]{2,1,0:T(8,128)(2,1)}, bf16[3,256,512]{2,1,0:T(8,128)(2,1)}, u32[]{:S(2)}, u32[]{:S(2)}) collective-permute-start(bf16[3,256,512]{2,1,0:T(8,128)(2,1)} %param.31), channel_id=1, source_target_pairs={{0,1},{1,0},{2,3},{3,2},{4,5},{5,4},{6,7},{7,6},{8,9},{9,8},{10,11... | collective-permute-start | bytes 2359304 | tf_op jit(solution)/shard_map/ppermute | solution.py:135
  17.5 12.1 %collective-permute-start = (bf16[3,1024,256]{2,1,0:T(8,128)(2,1)}, bf16[3,1024,256]{2,1,0:T(8,128)(2,1)}, u32[]{:S(2)}, u32[]{:S(2)}) collective-permute-start(bf16[3,1024,256]{2,1,0:T(8,128)(2,1)} %param.29), channel_id=1, source_target_pairs={{0,1},{1,0},{2,3},{3,2},{4,5},{5,4},{6,7},{7,6},{8,9},{9,8},{10,11... | collective-permute-start | bytes 4718600 | tf_op jit(solution)/shard_map/ppermute | solution.py:135
  17.9 4.9 %copy-start.23 = (bf16[3,1024,256]{2,1,0:T(8,128)(2,1)S(1)}, bf16[3,1024,256]{2,1,0:T(8,128)(2,1)}, u32[]{:S(2)}) copy-start(bf16[3,1024,256]{2,1,0:T(8,128)(2,1)} %param.29) | copy-start | bytes 4718596
  21.4 2.5 %copy-start.26 = (bf16[256,256]{1,0:T(8,128)(2,1)S(1)}, bf16[256,256]{1,0:T(8,128)(2,1)}, u32[]{:S(2)}) copy-start(bf16[256,256]{1,0:T(8,128)(2,1)} %param.17) | copy-start | bytes 393220
  21.4 4.5 %copy-start.28 = (s32[1,64,64]{2,1,0:T(8,128)S(1)}, s32[1,64,64]{2,1,0:T(8,128)}, u32[]{:S(2)}) copy-start(s32[1,64,64]{2,1,0:T(8,128)} %param.21) | copy-start | bytes 49156
  21.4 4.6 %copy-start.29 = (bf16[1,64,64]{2,1,0:T(8,128)(2,1)S(1)}, bf16[1,64,64]{2,1,0:T(8,128)(2,1)}, u32[]{:S(2)}) copy-start(bf16[1,64,64]{2,1,0:T(8,128)(2,1)} %param.22) | copy-start | bytes 24580
  43.2 4.6 %copy-start.2 = (bf16[1024,256]{1,0:T(8,128)(2,1)S(1)}, bf16[1024,256]{1,0:T(8,128)(2,1)}, u32[]{:S(2)}) copy-start(bf16[1024,256]{1,0:T(8,128)(2,1)} %get-tuple-element.59.in_mine) | copy-start | bytes 1572868
  43.2 4.6 %copy-start.3 = (bf16[1024,256]{1,0:T(8,128)(2,1)S(1)}, bf16[1024,256]{1,0:T(8,128)(2,1)}, u32[]{:S(2)}) copy-start(bf16[1024,256]{1,0:T(8,128)(2,1)} %get-tuple-element.60.in_other) | copy-start | bytes 1572868
  43.2 4.6 %copy-start.6 = (bf16[256,512]{1,0:T(8,128)(2,1)S(1)}, bf16[256,512]{1,0:T(8,128)(2,1)}, u32[]{:S(2)}) copy-start(bf16[256,512]{1,0:T(8,128)(2,1)} %get-tuple-element.63.out_mine) | copy-start | bytes 786436
  43.2 4.6 %copy-start.7 = (bf16[256,512]{1,0:T(8,128)(2,1)S(1)}, bf16[256,512]{1,0:T(8,128)(2,1)}, u32[]{:S(2)}) copy-start(bf16[256,512]{1,0:T(8,128)(2,1)} %get-tuple-element.64.out_other) | copy-start | bytes 786436
  43.2 4.6 %copy-start.10 = (bf16[512,256]{1,0:T(8,128)(2,1)S(1)}, bf16[512,256]{1,0:T(8,128)(2,1)}, u32[]{:S(2)}) copy-start(bf16[512,256]{1,0:T(8,128)(2,1)} %get-tuple-element.66.recv_w) | copy-start | bytes 786436
  43.2 4.6 %copy-start.11 = (bf16[512,256]{1,0:T(8,128)(2,1)S(1)}, bf16[512,256]{1,0:T(8,128)(2,1)}, u32[]{:S(2)}) copy-start(bf16[512,256]{1,0:T(8,128)(2,1)} %get-tuple-element.65.send_w) | copy-start | bytes 786436
  43.2 4.6 %copy-start.18 = (f32[1,256]{1,0:T(1,128)S(1)}, f32[1,256]{1,0:T(1,128)}, u32[]{:S(2)}) copy-start(f32[1,256]{1,0:T(1,128)} %get-tuple-element.67.edge_bias) | copy-start | bytes 3076
  43.3 4.6 %copy-start.19 = (f32[1,256]{1,0:T(1,128)S(1)}, f32[1,256]{1,0:T(1,128)}, u32[]{:S(2)}) copy-start(f32[1,256]{1,0:T(1,128)} %get-tuple-element.61.bias_mine) | copy-start | bytes 3076
  43.3 4.6 %copy-start.22 = (f32[1,256]{1,0:T(1,128)S(1)}, f32[1,256]{1,0:T(1,128)}, u32[]{:S(2)}) copy-start(f32[1,256]{1,0:T(1,128)} %get-tuple-element.62.bias_other) | copy-start | bytes 3076
  43.3 7.4 %copy-start.14 = (s32[1,12288]{1,0:T(1,128)S(1)}, s32[1,12288]{1,0:T(1,128)}, u32[]{:S(2)}) copy-start(s32[1,12288]{1,0:T(1,128)} %node.11) | copy-start | bytes 147460
  44.0 3.8 %collective-permute-start.3 = (bf16[256,256]{1,0:T(8,128)(2,1)S(1)}, bf16[256,256]{1,0:T(8,128)(2,1)S(1)}, u32[]{:S(2)}, u32[]{:S(2)}) collective-permute-start(bf16[256,256]{1,0:T(8,128)(2,1)S(1)} %slots.1.mine), channel_id=1, source_target_pairs={{0,1},{1,0},{2,3},{3,2},{4,5},{5,4},{6,7},{7,6},{8,9},{9,8},{10,11... | collective-permute-start | bytes 393224 | tf_op jit(solution)/shard_map/ppermute | solution.py:135
  48.9 7.1 %collective-permute-start.4 = (bf16[64,256]{1,0:T(8,128)(2,1)S(1)}, bf16[64,256]{1,0:T(8,128)(2,1)S(1)}, u32[]{:S(2)}, u32[]{:S(2)}) collective-permute-start(bf16[64,256]{1,0:T(8,128)(2,1)S(1)} %get-tuple-element.73), channel_id=1, source_target_pairs={{0,1},{1,0},{2,4},{3,5},{4,2},{5,3},{6,8},{7,9},{8,6},{9,7},{10,12... | collective-permute-start | bytes 98312 | tf_op jit(solution)/shard_map/ppermute | solution.py:249
  50.7 5.3 %collective-permute-start.5 = (bf16[64,256]{1,0:T(8,128)(2,1)S(1)}, bf16[64,256]{1,0:T(8,128)(2,1)S(1)}, u32[]{:S(2)}, u32[]{:S(2)}) collective-permute-start(bf16[64,256]{1,0:T(8,128)(2,1)S(1)} %get-tuple-element.74), channel_id=1, source_target_pairs={{0,2},{2,0},{4,6},{6,4},{8,10},{10,8},{12,14},{14,12},{16,18},{18,... | collective-permute-start | bytes 98312 | tf_op jit(solution)/shard_map/ppermute | solution.py:250
  54.1 8.3 %copy-start = (bf16[1024,256]{1,0:T(8,128)(2,1)S(1)}, bf16[1024,256]{1,0:T(8,128)(2,1)}, u32[]{:S(2)}) copy-start(bf16[1024,256]{1,0:T(8,128)(2,1)} %get-tuple-element.75.in_mine) | copy-start | bytes 1572868
  54.2 8.2 %copy-start.1 = (bf16[1024,256]{1,0:T(8,128)(2,1)S(1)}, bf16[1024,256]{1,0:T(8,128)(2,1)}, u32[]{:S(2)}) copy-start(bf16[1024,256]{1,0:T(8,128)(2,1)} %get-tuple-element.76.in_other) | copy-start | bytes 1572868
  54.2 8.2 %copy-start.4 = (bf16[256,512]{1,0:T(8,128)(2,1)S(1)}, bf16[256,512]{1,0:T(8,128)(2,1)}, u32[]{:S(2)}) copy-start(bf16[256,512]{1,0:T(8,128)(2,1)} %get-tuple-element.79.out_mine) | copy-start | bytes 786436
  54.2 8.2 %copy-start.5 = (bf16[256,512]{1,0:T(8,128)(2,1)S(1)}, bf16[256,512]{1,0:T(8,128)(2,1)}, u32[]{:S(2)}) copy-start(bf16[256,512]{1,0:T(8,128)(2,1)} %get-tuple-element.80.out_other) | copy-start | bytes 786436
  54.2 8.2 %copy-start.8 = (bf16[512,256]{1,0:T(8,128)(2,1)S(1)}, bf16[512,256]{1,0:T(8,128)(2,1)}, u32[]{:S(2)}) copy-start(bf16[512,256]{1,0:T(8,128)(2,1)} %get-tuple-element.82.recv_w) | copy-start | bytes 786436
  54.2 8.2 %copy-start.9 = (bf16[512,256]{1,0:T(8,128)(2,1)S(1)}, bf16[512,256]{1,0:T(8,128)(2,1)}, u32[]{:S(2)}) copy-start(bf16[512,256]{1,0:T(8,128)(2,1)} %get-tuple-element.81.send_w) | copy-start | bytes 786436
  54.2 8.2 %copy-start.16 = (f32[1,256]{1,0:T(1,128)S(1)}, f32[1,256]{1,0:T(1,128)}, u32[]{:S(2)}) copy-start(f32[1,256]{1,0:T(1,128)} %get-tuple-element.83.edge_bias) | copy-start | bytes 3076
  54.2 8.2 %copy-start.17 = (f32[1,256]{1,0:T(1,128)S(1)}, f32[1,256]{1,0:T(1,128)}, u32[]{:S(2)}) copy-start(f32[1,256]{1,0:T(1,128)} %get-tuple-element.77.bias_mine) | copy-start | bytes 3076
  54.2 8.2 %copy-start.21 = (f32[1,256]{1,0:T(1,128)S(1)}, f32[1,256]{1,0:T(1,128)}, u32[]{:S(2)}) copy-start(f32[1,256]{1,0:T(1,128)} %get-tuple-element.78.bias_other) | copy-start | bytes 3076
  59.8 2.6 %collective-permute-start.6 = (bf16[256,256]{1,0:T(8,128)(2,1)S(1)}, bf16[256,256]{1,0:T(8,128)(2,1)S(1)}, u32[]{:S(2)}, u32[]{:S(2)}) collective-permute-start(bf16[256,256]{1,0:T(8,128)(2,1)S(1)} %edge_halo.2.mine), channel_id=1, source_target_pairs={{0,1},{1,0},{2,3},{3,2},{4,5},{5,4},{6,7},{7,6},{8,9},{9,8},{10,11... | collective-permute-start | bytes 393224 | tf_op jit(solution)/shard_map/ppermute | solution.py:135
  63.5 7.1 %collective-permute-start.7 = (bf16[64,256]{1,0:T(8,128)(2,1)S(1)}, bf16[64,256]{1,0:T(8,128)(2,1)S(1)}, u32[]{:S(2)}, u32[]{:S(2)}) collective-permute-start(bf16[64,256]{1,0:T(8,128)(2,1)S(1)} %get-tuple-element.87), channel_id=1, source_target_pairs={{0,1},{1,0},{2,4},{3,5},{4,2},{5,3},{6,8},{7,9},{8,6},{9,7},{10,12... | collective-permute-start | bytes 98312 | tf_op jit(solution)/shard_map/ppermute | solution.py:249
  65.3 5.2 %collective-permute-start.8 = (bf16[64,256]{1,0:T(8,128)(2,1)S(1)}, bf16[64,256]{1,0:T(8,128)(2,1)S(1)}, u32[]{:S(2)}, u32[]{:S(2)}) collective-permute-start(bf16[64,256]{1,0:T(8,128)(2,1)S(1)} %get-tuple-element.88), channel_id=1, source_target_pairs={{0,2},{2,0},{4,6},{6,4},{8,10},{10,8},{12,14},{14,12},{16,18},{18,... | collective-permute-start | bytes 98312 | tf_op jit(solution)/shard_map/ppermute | solution.py:250
  68.8 8.2 %copy-start.12 = (bf16[256,512]{1,0:T(8,128)(2,1)S(1)}, bf16[256,512]{1,0:T(8,128)(2,1)}, u32[]{:S(2)}) copy-start(bf16[256,512]{1,0:T(8,128)(2,1)} %get-tuple-element.93.out_mine) | copy-start | bytes 786436
  68.8 8.2 %copy-start.13 = (bf16[256,512]{1,0:T(8,128)(2,1)S(1)}, bf16[256,512]{1,0:T(8,128)(2,1)}, u32[]{:S(2)}) copy-start(bf16[256,512]{1,0:T(8,128)(2,1)} %get-tuple-element.94.out_other) | copy-start | bytes 786436
  68.8 8.2 %copy-start.15 = (f32[1,256]{1,0:T(1,128)S(1)}, f32[1,256]{1,0:T(1,128)}, u32[]{:S(2)}) copy-start(f32[1,256]{1,0:T(1,128)} %get-tuple-element.91.bias_mine) | copy-start | bytes 3076
  68.8 8.2 %copy-start.20 = (f32[1,256]{1,0:T(1,128)S(1)}, f32[1,256]{1,0:T(1,128)}, u32[]{:S(2)}) copy-start(f32[1,256]{1,0:T(1,128)} %get-tuple-element.92.bias_other) | copy-start | bytes 3076
  74.4 2.6 %collective-permute-start.9 = (bf16[256,256]{1,0:T(8,128)(2,1)S(1)}, bf16[256,256]{1,0:T(8,128)(2,1)S(1)}, u32[]{:S(2)}, u32[]{:S(2)}) collective-permute-start(bf16[256,256]{1,0:T(8,128)(2,1)S(1)} %edge_halo.3.mine), channel_id=1, source_target_pairs={{0,1},{1,0},{2,3},{3,2},{4,5},{5,4},{6,7},{7,6},{8,9},{9,8},{10,11... | collective-permute-start | bytes 393224 | tf_op jit(solution)/shard_map/ppermute | solution.py:135
